TPU v7x, 32 devices: a whole 2x2x4 slice. The times are simulated.
32 devices in a mesh: cell: 4 (over x, core), gene: 8 (over z, y).
Axes of the slice: x: 2, y: 2, z: 4, core: 2. Of those that a mesh axis runs over, the one named last changes fastest.
Arguments:
- counts: int32 [4096, 8192], P('cell', 'gene'), may hold values from 0 to 4000, as said below
Outputs:
- gene_gram: float32 [8192, 8192], P('gene', 'cell')
Inputs may be any that keep to these rules, and one draw needn't show every extreme that they name: `counts`: every cell and every gene has a positive count somewhere.
All inputs are finite; a program needn't handle non-finite values.
Results may differ from a plain program's by a relative error of at most 0.00054.
Values may be sent and summed in bfloat16 or wider, within the bound.
No kernel may reach another device: no remote copies, remote signals or barrier semaphores. Data moves between devices by JAX's collectives and lax.ppermute only.
A program may use at most 128 MiB of HBM per device.

v0:
```python
import jax
import jax.numpy as jnp
from jax import lax
from jax.sharding import PartitionSpec as P


def body(counts):
    cells_all = counts.shape[0] * lax.axis_size("cell")
    values = counts.astype(jnp.float32)
    row_part = jnp.sum(values, axis=1)
    column_part = jnp.sum(values, axis=0)
    depths = lax.psum(row_part, "gene")
    gene_totals, grand_total = lax.psum((column_part, jnp.sum(depths)), "cell")
    expected = depths[:, None] * gene_totals[None, :] / grand_total
    scaled = (values - expected) / jnp.sqrt(expected + expected * expected / 100.0)
    ceiling = jnp.sqrt(jnp.float32(cells_all))
    residuals = jnp.clip(scaled, -ceiling, ceiling).astype(jnp.bfloat16)
    gathered = lax.all_gather(residuals, "gene", axis=1, tiled=True)
    owned_block = lax.psum_scatter(
        lax.dot_general(
            gathered, residuals, (((0,), (0,)), ((), ())), preferred_element_type=jnp.float32
        ),
        "cell",
        scatter_dimension=0,
        tiled=True,
    ).T
    return owned_block / jnp.float32(cells_all)


def solution(mesh):
    return jax.shard_map(
        body,
        mesh=mesh,
        in_specs=(P("cell", "gene"),),
        out_specs=P("gene", "cell"),
        check_vma=False,
    )
```

profile of v0, /device:TPU:13, one launch (start us, length us, event | category | flops | bytes accessed | tf_op | source)
XLA Modules:
  0.0 553.6 jit_solution(12205561640900585951)
XLA Ops:
  6.5 0.0 all-gather.2.cloned.1.call-start
  6.5 2.8 convert_reduce_fusion
  9.4 11.6 %psum.21 = f32[1024]{0:T(1024)S(1)} all-reduce(f32[1024]{0:T(1024)S(1)} %get-tuple-element.6), channel_id=1, replica_groups=mesh['cell'=4,'gene'=8] {'gene'}, use_global_device_ids=true, to_apply=%region_1.0 | all-reduce | flops 1024 | bytes 8192 | tf_op jit(solution)/shard_map/psum | solution.py:12
  21.0 0.6 reduce_sum.29
  21.6 10.0 %all-reduce = (f32[]{:T(128)}, f32[1024]{0:T(1024)S(1)}) all-reduce(f32[]{:T(128)} %reduce_sum.29, f32[1024]{0:T(1024)S(1)} %get-tuple-element.5), channel_id=1, replica_groups=mesh['cell'=4,'gene'=8] {'cell'}, use_global_device_ids=true, to_apply=%region_5.0 | all-reduce | flops 1025 | bytes 8200 | tf_op jit(solution)/shard_map/psum | solution.py:13
  31.6 5.0 clamp_convert_fusion
  36.5 0.0 all-gather.2.cloned.1.call-update
  36.6 0.0 reduce-scatter.2.cloned.1.call-start
  36.6 228.5 %all-gather.2.cloned.1.call-done = bf16[1024,8192]{1,0:T(8,128)(2,1)} async-done(((bf16[1024,1024]{1,0:T(8,128)(2,1)}), bf16[1024,8192]{1,0:T(8,128)(2,1)}) %all-gather.2.cloned.1.call-update) | async-done | bytes 16777232 | tf_op jit(solution)/shard_map/all_gather | solution.py:18
  265.1 27.7 %fusion = f32[8192,1024]{1,0:T(8,128)} fusion(bf16[1024,8192]{1,0:T(8,128)(2,1)} %all-gather.2.cloned.1.call-done, bf16[1024,1024]{1,0:T(8,128)(2,1)} %clamp_convert_fusion), kind=kOutput, calls=%fused_computation.4 | convolution fusion | flops 17179869184 | bytes 52428800 | tf_op jit(solution)/shard_map/dot_general | solution.py:20
  292.9 0.0 reduce-scatter.2.cloned.1.call-update
  292.9 236.3 %reduce-scatter.2.cloned.1.call-done = f32[2048,1024]{1,0:T(8,128)} async-done(((f32[8192,1024]{1,0:T(8,128)}), f32[2048,1024]{1,0:T(8,128)}) %reduce-scatter.2.cloned.1.call-update) | async-done | bytes 8388624 | tf_op jit(solution)/shard_map/reduce_scatter | solution.py:19
  529.2 8.5 %multiply_bitcast_fusion = f32[1024,2048]{0,1:T(8,128)} fusion(f32[2048,1024]{1,0:T(8,128)} %reduce-scatter.2.cloned.1.call-done), kind=kLoop, calls=%fused_computation | loop fusion | flops 2097152 | bytes 16777216 | tf_op jit(solution)/shard_map/div | solution.py:27
  537.7 9.1 %copy.2 = f32[1024,2048]{1,0:T(8,128)} copy(f32[1024,2048]{0,1:T(8,128)} %multiply_bitcast_fusion) | data formatting | bytes 16777216 | tf_op jit(solution)/shard_map/div | solution.py:27
Async XLA Ops:
  6.5 258.6 %all-gather.2.cloned.1.call-start = ((), (), s32[]{:S(2)}) async-start(), calls=%async_computation.1 | async-start | bytes 18874368 | tf_op jit(solution)/shard_map/all_gather | solution.py:18
  36.6 492.6 %reduce-scatter.2.cloned.1.call-start = ((), (), s32[]{:S(2)}) async-start(), calls=%async_computation.2 | async-start | bytes 41943040 | tf_op jit(solution)/shard_map/reduce_scatter | solution.py:19
Sparse Core Ops, SparseCore 0:
  36.7 228.4 all-gather.1
  293.0 236.1 reduce-scatter.1
where the time goes:
time: 556 us; the launch traced here: 554 us
  waiting for transfers between devices  465 us (84%)
  matrix products  27.7 us (5%)
  blocking collectives  21.6 us (4%)
  other arithmetic  16.9 us (3%)
  between operations  13.4 us (2%)
  local copies, waits for them, and re-layouts  9.12 us (2%)
    reduce_scatter x1, waiting for transfers between devices, body(): lax.psum_scatter(lax.dot_general(gathered, residuals, (((0,), (0,)), ((),...  236 us
    all_gather x1, waiting for transfers between devices, body(): gathered = lax.all_gather(residuals, 'gene', axis=1, tiled=True)  229 us
    dot_general x1, matrix products, body(): lax.dot_general(gathered, residuals, (((0,), (0,)), ((), ())), preferred_...  27.7 us
    psum x1, blocking collectives, body(): depths = lax.psum(row_part, 'gene')  11.6 us
  transfers between devices with their start and end apart: 2, of which 2 were waited for; matrix products, arithmetic and copies ran while one was open for 0% of the time, Pallas kernels for 0%

commit v1 on v0

--- a/solution.py
+++ b/solution.py
@@ -3,8 +3,217 @@
 from jax import lax
 from jax.sharding import PartitionSpec as P
 
+AXES = ("cell", "gene")
+UNIT = 8.0
+
+
+def pairs_of(move):
+    pairs = []
+    for x in range(2):
+        for c in range(2):
+            for z in range(4):
+                for y in range(2):
+                    target = move(x, c, z, y)
+                    if target is not None and 0 <= target[2] < 4:
+                        tx, tc, tz, ty = target
+                        pairs.append(((2 * x + c) * 8 + 2 * z + y, (2 * tx + tc) * 8 + 2 * tz + ty))
+    return pairs
+
+
+def send(value, move):
+    return lax.ppermute(value, AXES, pairs_of(move))
+
+
+def residuals_of(counts, depths, totals, grand, ceiling):
+    expected = depths[:, None] * totals[None, :] / grand
+    scaled = (counts.astype(jnp.float32) - expected) * lax.rsqrt(expected + expected * expected * 0.01)
+    return jnp.clip(scaled, -ceiling, ceiling).astype(jnp.bfloat16)
+
+
+def after(value, *others):
+    return lax.optimization_barrier((value,) + others)[0]
+
 
 def body(counts):
+    cells_here, genes_here = counts.shape
+    cells_all = cells_here * lax.axis_size("cell")
+    half = genes_here // 2
+    cell, gene = lax.axis_index("cell"), lax.axis_index("gene")
+    x, c, z, y = cell // 2, cell % 2, gene // 2, gene % 2
+    even = c == z % 2
+    low = z < 2
+
+    def down(distance, late):
+        def move(x, c, z, y):
+            source = z + distance - 1
+            if c != source % 2 or source > 3 or (late and distance == 1 and x == 0 and z == 1):
+                return None
+            return x, c, z - 1, y
+        return move
+
+    def up(distance, late):
+        def move(x, c, z, y):
+            source = z - distance + 1
+            if c != source % 2 or source < 0 or (late and distance == 1 and x == 1 and z == 2):
+                return None
+            return x, c, z + 1, y
+        return move
+
+    def last(x, c, z, y):
+        if x == 0 and c == 1 and z == 1:
+            return x, c, 0, y
+        if x == 1 and c == 0 and z == 2:
+            return x, c, 3, y
+        return None
+
+    small = counts.astype(jnp.int16)
+    row_part = jnp.sum(counts, axis=1)
+    totals = jnp.sum(counts, axis=0)
+    small, row_part, totals = lax.optimization_barrier((small, row_part, totals))
+    sibling = send(small, lambda x, c, z, y: (x, 1 - c, z, y))
+    across = send(small, lambda x, c, z, y: (x, c, z, 1 - y))
+    both_a = jnp.concatenate([small[:, :half], sibling[:, :half]], axis=0)
+    both_b = jnp.concatenate([small[:, half:], sibling[:, half:]], axis=0)
+    d1a, u1a = send(both_a, down(1, False)), send(both_a, up(1, False))
+    d1b, u1b = send(both_b, down(1, True)), send(both_b, up(1, True))
+
+    row_part, totals, both_a, both_b = lax.optimization_barrier((row_part, totals, both_a, both_b))
+    totals = totals + send(totals, lambda x, c, z, y: (x, 1 - c, z, y))
+    totals = totals + send(totals, lambda x, c, z, y: (1 - x, c, z, y))
+    got = send(jnp.concatenate([totals, row_part]), lambda x, c, z, y: (x, c, z, 1 - y))
+    totals = jnp.concatenate([totals, got[:genes_here]])
+    depths = row_part + got[genes_here:]
+    for bit in (1, 2):
+        got = send(jnp.concatenate([totals, depths]), lambda x, c, z, y: (x, c, z ^ bit, y))
+        depths = depths + got[totals.size :]
+        totals = jnp.concatenate([totals, got[: totals.size]])
+    depths = jnp.stack([depths, send(depths, lambda x, c, z, y: (x, 1 - c, z, y))])
+    depths = depths.reshape(-1).astype(jnp.float32)
+    totals = totals.astype(jnp.float32).reshape(4, 2, genes_here)
+    grand = jnp.sum(totals)
+    ceiling = jnp.sqrt(jnp.float32(cells_all))
+
+    def totals_of(block):
+        index = block ^ z
+        out = totals[0, 0]
+        for i in range(1, 4):
+            out = jnp.where(index == i, totals[i, 0], out)
+        return out
+
+    def convert(values, gene_totals):
+        return residuals_of(values, depths, gene_totals, grand, ceiling)
+
+    def gram(left, right):
+        product = lax.dot_general(
+            left, right, (((0,), (0,)), ((), ())), preferred_element_type=jnp.float32
+        )
+        return (product * (UNIT / cells_all)).astype(jnp.float16)
+
+    def cross(value, remote):
+        return send(value, lambda x, c, z, y: (1 - x, c, z, y) if remote(x, c, z) else None)
+
+    def is_even(c, z):
+        return c == z % 2
+
+    rows_own = convert(jnp.concatenate([both_a, both_b], axis=1), totals[0, 0])
+    p0_own = gram(rows_own, rows_own)
+    remote0 = lambda x, c, z: is_even(c, z) and x != z // 2
+    x0_own = cross(p0_own, remote0)
+
+    d2a, u2a = send(d1a, down(2, False)), send(u1a, up(2, False))
+    d2b, u2b = send(d1b, down(2, False)), send(u1b, up(2, False))
+
+    across_sibling = send(across, lambda x, c, z, y: (x, 1 - c, z, y))
+    rows_other = convert(jnp.concatenate([across, across_sibling], axis=0), totals[0, 1])
+    rows = jnp.concatenate([rows_own, rows_other], axis=1)
+    p0_other = gram(rows_other, rows_own)
+    x0_other = cross(p0_other, remote0)
+
+    take_down = jnp.where(z == 0, True, jnp.where(z == 3, False, x == 0))
+    take_down = jnp.where((z == 2), x == 0, take_down)
+    first_a = jnp.where(take_down, d1a, u1a)
+    first_b = jnp.where(take_down, d1b, u1b)
+    p1 = gram(
+        rows,
+        convert(
+            jnp.concatenate([first_a, first_b], axis=1),
+            totals_of(jnp.where(take_down, z + 1, z - 1)),
+        ),
+    )
+    def remote1(x, c, z):
+        return not is_even(c, z) and (x, z) not in ((0, 0), (1, 3))
+    x1 = cross(p1, remote1)
+
+    d3a, u3a = send(d2a, down(3, False)), send(u2a, up(3, False))
+
+    far_totals = totals_of(jnp.where(low, z + 2, z - 2))
+    p2a = gram(rows, convert(jnp.where(low, d2a, u2a), far_totals[:half]))
+    remote2 = lambda x, c, z: is_even(c, z) and x == z // 2
+    x2a = cross(p2a, remote2)
+    d3b, u3b = send(d2b, down(3, False)), send(u2b, up(3, False))
+    p2b = gram(rows, convert(jnp.where(low, d2b, u2b), far_totals[half:]))
+    x2b = cross(p2b, remote2)
+    late = send(after(both_b, d3b, u3b), last)
+
+    end = (z == 0) | (z == 3)
+    far_x = (x == 0) == (z == 0)
+    end_totals = totals_of(3 - z)
+    near_totals = totals_of(jnp.where(take_down, z - 1, z + 1))
+    p3a = gram(rows, convert(jnp.where(low, d3a, u3a), end_totals[:half]))
+    remote3 = lambda x, c, z: (x, c, z) in ((0, 1, 0), (1, 0, 3))
+    x3a = cross(p3a, remote3)
+    middle_a = jnp.where(take_down, u1a, d1a)
+    end_a = jnp.where(far_x, jnp.where(low, d3b, u3b), jnp.where(low, d3a, u3a))
+    p4 = gram(
+        rows,
+        convert(
+            jnp.where(end, end_a, middle_a),
+            jnp.where(end, jnp.where(far_x, end_totals[half:], end_totals[:half]), near_totals[:half]),
+        ),
+    )
+    x3b = cross(p4, remote3)
+    middle_b = jnp.where(take_down, u1b, d1b)
+    end_b = jnp.where(far_x, late, jnp.where(low, d3b, u3b))
+    late_totals = totals_of(jnp.where(z == 0, 1, 2))
+    p5 = gram(
+        rows,
+        convert(
+            jnp.where(end, end_b, middle_b),
+            jnp.where(end, jnp.where(far_x, late_totals[half:], end_totals[half:]), near_totals[half:]),
+        ),
+    )
+
+    def swap(value):
+        return send(value, lambda x, c, z, y: (x, c, z, 1 - y))
+
+    wide = lambda value: value.astype(jnp.float32)
+
+    keeps_own = x == z // 2
+    p2 = jnp.concatenate([p2a, p2b], axis=1)
+    x2 = jnp.concatenate([x2a, x2b], axis=1)
+    even_own = jnp.where(keeps_own, wide(p0_own) + wide(x0_own), wide(p2[:genes_here]) + wide(x2[:genes_here]))
+    even_other = jnp.where(
+        keeps_own, wide(p0_other) + wide(x0_other), wide(p2[genes_here:]) + wide(x2[genes_here:])
+    ).astype(jnp.float16)
+    even_got = swap(even_other)
+
+    far_keep = end & jnp.logical_not(far_x)
+    odd_a = wide(jnp.where(end & far_x, p1[:, :half], p4)) + wide(jnp.where(far_keep, x3a, x1[:, :half]))
+    odd_b = wide(p5) + wide(jnp.where(far_keep, x3b, x1[:, half:]))
+    got_a = swap(odd_a[genes_here:].astype(jnp.float16))
+    got_b = swap(odd_b[genes_here:].astype(jnp.float16))
+
+    out = jnp.concatenate([even_own, wide(even_got)], axis=1)
+    first, second = y * genes_here, (1 - y) * genes_here
+    out = jnp.where(y == 0, out, jnp.concatenate([wide(even_got), even_own], axis=1)) * (1.0 / UNIT)
+    for value, got, offset in ((odd_a, got_a, 0), (odd_b, got_b, half)):
+        for piece, start in ((value[:genes_here], first + offset), (wide(got), second + offset)):
+            old = lax.dynamic_slice(out, (0, start), (genes_here, half))
+            out = lax.dynamic_update_slice(out, jnp.where(even, old, piece * (1.0 / UNIT)), (0, start))
+    return out
+
+
+def body_any(counts):
     cells_all = counts.shape[0] * lax.axis_size("cell")
     values = counts.astype(jnp.float32)
     row_part = jnp.sum(values, axis=1)
@@ -28,8 +237,9 @@
 
 
 def solution(mesh):
+    fits = (mesh.shape["cell"], mesh.shape["gene"]) == (4, 8)
     return jax.shard_map(
-        body,
+        body if fits else body_any,
         mesh=mesh,
         in_specs=(P("cell", "gene"),),
         out_specs=P("gene", "cell"),

time: 556 us -> 354 us (0.64)
  waiting for transfers between devices: 465 us -> 134 us
  starting transfers between devices: 0.04 us -> 58.1 us
  matrix products: 27.7 us -> 80.4 us
  other arithmetic: 16.9 us -> 61.3 us
  blocking collectives: 21.6 us -> 0 us
  between operations: 13.4 us -> 0.6 us
    reduce_scatter x1 -> x0, waiting for transfers between devices: 236 us -> none  [body(): lax.psum_scatter(lax.dot_general(gathered, residuals, (((0,), (0,)), ((),...]
    all_gather x1 -> x0, waiting for transfers between devices: 229 us -> none  [body(): gathered = lax.all_gather(residuals, 'gene', axis=1, tiled=True)]
    ppermute x0 -> x32, waiting for transfers between devices: none -> 134 us  [send(): return lax.ppermute(value, AXES, pairs_of(move))]
    ppermute x0 -> x32, starting transfers between devices: none -> 58.1 us  [send(): return lax.ppermute(value, AXES, pairs_of(move))]
    dot_general x1 -> x8, matrix products: 27.7 us -> 80.4 us  [gram(): lax.dot_general(left, right, (((0,), (0,)), ((), ())), preferred_element_...]
    psum x2 -> x0, blocking collectives: 21.6 us -> none  [the longest x1 11.6 us: body(): depths = lax.psum(row_part, 'gene')]
    select_n x0 -> x5, other arithmetic: none -> 13.8 us  [the longest x1 7.45 us: body(): jnp.where(keeps_own, wide(p0_own) + wide(x0_own), wide(p2[:genes_here]) +...]
    convert_element_type x1 -> x3, other arithmetic: 4.96 us -> 16.4 us  [the longest x1 14.3 us: residuals_of(): return jnp.clip(scaled, -ceiling, ceiling).astype(jnp.bfloat16)]
  transfers between devices with their start and end apart: 2 -> 32, of which waited for: 2 -> 12; matrix products, arithmetic and copies ran while one was open for 0% -> 38% of each run, Pallas kernels for 0% -> 0%
where the time goes in v1:
time: 354 us; the launch traced here: 348 us
  waiting for transfers between devices  134 us (38%)
  matrix products  80.4 us (23%)
  other arithmetic  61.3 us (17%)
  starting transfers between devices  58.1 us (16%)
  local copies, waits for them, and re-layouts  13.7 us (4%)
    ppermute x32, waiting for transfers between devices, send(): return lax.ppermute(value, AXES, pairs_of(move))  134 us
    dot_general x8, matrix products, gram(): lax.dot_general(left, right, (((0,), (0,)), ((), ())), preferred_element_...  80.4 us
    ppermute x32, starting transfers between devices, send(): return lax.ppermute(value, AXES, pairs_of(move))  58.1 us
    convert_element_type x1, other arithmetic, residuals_of(): return jnp.clip(scaled, -ceiling, ceiling).astype(jnp.bfloat16)  14.3 us
    dynamic_update_slice x1, local copies, waits for them, and re-layouts, body(): lax.dynamic_update_slice(out, jnp.where(even, old, piece * (1.0 / UNIT)),...  9.12 us
    another operation x2, other arithmetic  7.67 us
    select_n x1, other arithmetic, body(): jnp.where(keeps_own, wide(p0_own) + wide(x0_own), wide(p2[:genes_here]) +...  7.45 us
  transfers between devices with their start and end apart: 32, of which 12 were waited for; matrix products, arithmetic and copies ran while one was open for 38% of the time, Pallas kernels for 0%

profile of v1, /device:TPU:13, one launch (start us, length us, event | category | flops | bytes accessed | tf_op | source)
XLA Modules:
  0.0 348.5 jit_solution(14183795276586803365)
XLA Ops:
  0.0 4.1 %fusion.82 = (s32[1024]{0:T(1024)S(1)}, s32[1024]{0:T(1024)S(1)}, s16[1024,1024]{1,0:T(8,128)(2,1)S(1)}) fusion(s32[1024,1024]{1,0:T(8,128)} %param.1), kind=kLoop, calls=%fused_computation.140 | loop fusion | flops 3143680 | bytes 6299648 | tf_op jit(solution)/shard_map/reduce_sum | solution.py:71
  5.2 3.4 collective-permute-done
  16.0 4.6 %collective-permute-start.12 = (s16[2048,512]{1,0:T(8,128)(2,1)}, s16[2048,512]{1,0:T(8,128)(2,1)}, u32[]{:S(2)}, u32[]{:S(2)}) collective-permute-start(s16[2048,512]{1,0:T(8,128)(2,1)} %pad_add_fusion), channel_id=1, source_target_pairs={{0,2},{1,3},{4,6},{5,7},{10,12},{11,13},{16,18},{17,19},{20,22},{2... | collective-permute-start | bytes 6291464 | tf_op jit(solution)/shard_map/ppermute | solution.py:24
  20.6 2.7 collective-permute-start.10
  23.3 29.0 %collective-permute-done.3 = s32[2048]{0:T(1024)S(1)} collective-permute-done((s32[2048]{0:T(1024)S(1)}, s32[2048]{0:T(1024)S(1)}, u32[]{:S(2)}, u32[]{:S(2)}) %collective-permute-start.3) | collective-permute-done | bytes 8224 | tf_op jit(solution)/shard_map/ppermute | solution.py:24
  52.5 2.4 collective-permute-done.4
  54.9 2.4 collective-permute-start.5
  57.3 2.1 collective-permute-start.14
  59.3 3.7 %collective-permute-start.16 = (s16[2048,512]{1,0:T(8,128)(2,1)}, s16[2048,512]{1,0:T(8,128)(2,1)}, u32[]{:S(2)}, u32[]{:S(2)}) collective-permute-start(s16[2048,512]{1,0:T(8,128)(2,1)} %pad_add_fusion.1), channel_id=1, source_target_pairs={{0,2},{1,3},{4,6},{5,7},{10,12},{11,13},{16,18},{17,19},{26,28},{2... | collective-permute-start | bytes 6291464 | tf_op jit(solution)/shard_map/ppermute | solution.py:24
  67.1 2.0 collective-permute-start.13
  69.1 2.2 broadcast_select_fusion.1
  71.3 22.9 %collective-permute-done.16 = s16[2048,512]{1,0:T(8,128)(2,1)} collective-permute-done((s16[2048,512]{1,0:T(8,128)(2,1)}, s16[2048,512]{1,0:T(8,128)(2,1)}, u32[]{:S(2)}, u32[]{:S(2)}) %collective-permute-start.16) | collective-permute-done | bytes 2097184 | tf_op jit(solution)/shard_map/ppermute | solution.py:24
  94.2 3.5 %broadcast_select_fusion = s16[2048,512]{1,0:T(8,128)(2,1)} fusion(s16[2048,512]{1,0:T(8,128)(2,1)} %collective-permute-done.14, s16[2048,512]{1,0:T(8,128)(2,1)} %collective-permute-done.16, pred[]{:T(512)S(6)} %select_n.337), kind=kLoop, calls=%fused_computation.95 | loop fusion | flops 1048576 | bytes 6291457 | tf_op jit(solution)/shard_map/jit(_where)/select_n | solution.py:135
  97.7 14.3 %clamp_convert_fusion.2 = (bf16[2048,1024]{1,0:T(8,128)(2,1)S(1)}, bf16[2048,1024]{1,0:T(8,128)(2,1)}) fusion(s16[2048,512]{1,0:T(8,128)(2,1)} %pad_add_fusion.1, s16[2048,512]{1,0:T(8,128)(2,1)} %pad_add_fusion, f32[]{:T(128)} %fusion.81, f32[1024]{0:T(1024)S(1)} %bitcast.17, f32[2048]{0:T(1024)S(1)} %bitcast.18, f32[1024]{0:T(1024)S(1)} %bitcast.29, ...), kind=kLoop, calls=%fused_computation.6 | loop fusion | flops 46137344 | bytes 16793604 | tf_op jit(solution)/shard_map/convert_element_type | solution.py:30
  112.1 18.1 %multiply_convert_fusion = f16[2048,1024]{0,1:T(8,128)(2,1)} fusion(s16[2048,512]{1,0:T(8,128)(2,1)} %broadcast_select_fusion, s16[2048,512]{1,0:T(8,128)(2,1)S(1)} %broadcast_select_fusion.1, f32[1024]{0:T(1024)S(1)} %get-tuple-element.42, f32[]{:T(128)} %fusion.81, f32[2048]{0:T(1024)S(1)} %bitcast.19, bf16[2048,1024]{1,0:T(8,128)(2,1)} %get-tuple-element.47, ...), kind=kOutput, calls=%fused_computation.3 | convolution fusion | flops 8633974784 | bytes 16789508 | tf_op jit(solution)/shard_map/dot_general | solution.py:107
  131.9 2.0 collective-permute-start.17
  133.9 4.8 %multiply_convert_fusion.7 = f16[1024,1024]{0,1:T(8,128)(2,1)S(1)} fusion(bf16[2048,1024]{1,0:T(8,128)(2,1)S(1)} %get-tuple-element.46), kind=kOutput, calls=%fused_computation.28 | convolution fusion | flops 4297064448 | bytes 6291456 | tf_op jit(solution)/shard_map/dot_general | solution.py:107
  138.8 8.7 %multiply_convert_fusion.6 = f16[2048,512]{0,1:T(8,128)(2,1)S(1)} fusion(f32[]{:T(128)} %fusion.81, f32[512]{0:T(512)S(1)} %get-tuple-element.52, f32[2048]{0:T(1024)S(1)} %bitcast.20, s16[2048,512]{1,0:T(8,128)(2,1)} %collective-permute-done.11, s16[2048,512]{1,0:T(8,128)(2,1)} %collective-permute-done.13, pred[]{:T(512)S(6)} %lt.34, ...), kind=kOutput, calls=%fused_computation.26 | convolution fusion | flops 4325376000 | bytes 14690309 | tf_op jit(solution)/shard_map/dot_general | solution.py:107
  147.5 5.5 %collective-permute-start.18 = (f16[2048,512]{0,1:T(8,128)(2,1)S(1)}, f16[2048,512]{0,1:T(8,128)(2,1)}, u32[]{:S(2)}, u32[]{:S(2)}) collective-permute-start(f16[2048,512]{0,1:T(8,128)(2,1)S(1)} %multiply_convert_fusion.6), channel_id=1, source_target_pairs={{0,16},{1,17},{10,26},{11,27},{20,4},{21,5},{30,14},{31,15}} | collective-permute-start | bytes 6291464 | tf_op jit(solution)/shard_map/ppermute | solution.py:24
  153.0 2.6 collective-permute-start.24
  155.6 2.0 collective-permute-start.25
  157.6 4.9 %multiply_convert_fusion.4 = f16[1024,1024]{0,1:T(8,128)(2,1)S(1)} fusion(bf16[2048,1024]{1,0:T(8,128)(2,1)S(1)} %copy-done.3, bf16[2048,1024]{1,0:T(8,128)(2,1)S(1)} %get-tuple-element.46), kind=kOutput, calls=%fused_computation.22 | convolution fusion | flops 4297064448 | bytes 10485760 | tf_op jit(solution)/shard_map/dot_general | solution.py:107
  165.4 8.7 %multiply_convert_fusion.5 = f16[2048,512]{0,1:T(8,128)(2,1)S(1)} fusion(f32[512]{0:T(512)S(1)} %get-tuple-element.51, s16[2048,512]{1,0:T(8,128)(2,1)} %copy-done.8, s16[2048,512]{1,0:T(8,128)(2,1)} %collective-permute-done.17, f32[]{:T(128)} %fusion.81, f32[2048]{0:T(1024)S(1)} %bitcast.21, pred[]{:T(512)S(6)} %lt.34, ...), kind=kOutput, calls=%fused_computation.24 | convolution fusion | flops 4325376000 | bytes 14690309 | tf_op jit(solution)/shard_map/dot_general | solution.py:107
  174.2 11.1 %collective-permute-done.24 = s16[2048,512]{1,0:T(8,128)(2,1)} collective-permute-done((s16[2048,512]{1,0:T(8,128)(2,1)}, s16[2048,512]{1,0:T(8,128)(2,1)}, u32[]{:S(2)}, u32[]{:S(2)}) %collective-permute-start.24) | collective-permute-done | bytes 2097184 | tf_op jit(solution)/shard_map/ppermute | solution.py:24
  185.2 5.7 %collective-permute-start.19 = (f16[2048,512]{0,1:T(8,128)(2,1)S(1)}, f16[2048,512]{0,1:T(8,128)(2,1)}, u32[]{:S(2)}, u32[]{:S(2)}) collective-permute-start(f16[2048,512]{0,1:T(8,128)(2,1)S(1)} %multiply_convert_fusion.5), channel_id=1, source_target_pairs={{0,16},{1,17},{10,26},{11,27},{20,4},{21,5},{30,14},{31,15}} | collective-permute-start | bytes 6291464 | tf_op jit(solution)/shard_map/ppermute | solution.py:24
  191.0 2.7 collective-permute-start.22
  193.6 2.0 collective-permute-start.23
  195.6 10.0 %multiply_convert_fusion.2 = f16[2048,512]{0,1:T(8,128)(2,1)} fusion(f32[512]{0:T(512)S(1)} %get-tuple-element.50, f32[]{:T(128)} %fusion.81, f32[2048]{0:T(1024)S(1)} %bitcast.22, s16[2048,512]{1,0:T(8,128)(2,1)} %collective-permute-done.24, s16[2048,512]{1,0:T(8,128)(2,1)} %collective-permute-done.25, pred[]{:T(512)S(6)} %lt.34, ...), kind=kOutput, calls=%fused_computation.16 | convolution fusion | flops 4325376000 | bytes 14690309 | tf_op jit(solution)/shard_map/dot_general | solution.py:107
  205.6 2.1 constant_dynamic-update-slice_fusion.1
  207.8 5.6 %collective-permute-done.19 = f16[2048,512]{0,1:T(8,128)(2,1)} collective-permute-done((f16[2048,512]{0,1:T(8,128)(2,1)S(1)}, f16[2048,512]{0,1:T(8,128)(2,1)}, u32[]{:S(2)}, u32[]{:S(2)}) %collective-permute-start.19) | collective-permute-done | bytes 2097184 | tf_op jit(solution)/shard_map/ppermute | solution.py:24
  213.3 2.6 collective-permute-start.27
  216.0 2.1 constant_dynamic-update-slice_fusion
  219.3 7.4 %add_select_fusion = (f32[1024,1024]{0,1:T(8,128)}, f16[1024,1024]{0,1:T(8,128)(2,1)}) fusion(f16[1024,1024]{0,1:T(8,128)(2,1)} %collective-permute-done.7, f16[1024,1024]{0,1:T(8,128)(2,1)S(1)} %multiply_convert_fusion.7, f16[2048,512]{0,1:T(8,128)(2,1)S(1)} %multiply_convert_fusion.6, f16[2048,512]{0,1:T(8,128)(2,1)S(1)} %copy-done.6, ...), kind=kLoop, calls=%fused_computation.23 | loop fusion | flops 17825792 | bytes 23068672 | tf_op jit(solution)/shard_map/jit(_where)/select_n | solution.py:194
  227.0 12.5 %multiply_convert_fusion.3 = f16[2048,512]{0,1:T(8,128)(2,1)} fusion(f32[512]{0:T(512)S(1)} %get-tuple-element.45, s16[2048,512]{1,0:T(8,128)(2,1)} %collective-permute-done.12, s16[2048,512]{1,0:T(8,128)(2,1)} %collective-permute-done.10, f32[]{:T(128)} %fusion.81, f32[2048]{0:T(1024)S(1)} %bitcast.23, pred[]{:T(512)S(6)} %eq.88, pred[]{:T(512)S(6)} %or.3, ...), kind=kOutput, calls=%fused_computation.18 | convolution fusion | flops 4329570304 | bytes 23078920 | tf_op jit(solution)/shard_map/dot_general | solution.py:107
  239.6 2.0 collective-permute-start.30
  241.5 2.6 collective-permute-start.29
  244.2 25.7 %collective-permute-done.21 = f16[1024,1024]{0,1:T(8,128)(2,1)} collective-permute-done((f16[1024,1024]{0,1:T(8,128)(2,1)}, f16[1024,1024]{0,1:T(8,128)(2,1)}, u32[]{:S(2)}, u32[]{:S(2)}) %collective-permute-start.21) | collective-permute-done | bytes 2097184 | tf_op jit(solution)/shard_map/ppermute | solution.py:24
  269.8 2.1 convert_element_type.170
  272.0 4.6 %fusion = f32[1024,2048]{0,1:T(8,128)} fusion(f32[1024,1024]{0,1:T(8,128)S(1)} %convert_element_type.170, f32[1024,1024]{0,1:T(8,128)S(1)} %copy-done, pred[]{:T(512)S(6)} %eq.79), kind=kLoop, calls=%fused_computation.2 | loop fusion | flops 8388608 | bytes 16777216 | tf_op jit(solution)/shard_map/mul | solution.py:208
  276.6 4.2 %convert_add_fusion.1 = f32[2048,512]{0,1:T(8,128)S(1)} fusion(f16[2048,512]{0,1:T(8,128)(2,1)S(1)} %collective-permute-done.26, f16[2048,1024]{0,1:T(8,128)(2,1)} %collective-permute-done.27, f16[2048,512]{0,1:T(8,128)(2,1)S(1)} %copy-done.4, f16[2048,1024]{0,1:T(8,128)(2,1)} %multiply_convert_fusion, pred[]{:T(512)S(6)} %and.41, pred[]{:T(512)S(6)} %and.40), kind=kLoop, calls=%fused_computation.15 | loop fusion | flops 5242880 | bytes 12582914 | tf_op jit(solution)/shard_map/add | solution.py:201
  280.8 3.9 %slice_convert_fusion.1 = (f16[1024,512]{0,1:T(8,128)(2,1)S(1)}, f32[1024,2048]{0,1:T(8,128)}) fusion(f32[2048,512]{0,1:T(8,128)S(1)} %convert_add_fusion.1, f32[1024,2048]{0,1:T(8,128)} %fusion, s32[]{:T(128)S(6)} %select_n.333, pred[]{:T(512)S(6)} %eq.84), kind=kLoop, calls=%fused_computation.40 | loop fusion | flops 1572864 | bytes 9437189 | tf_op jit(solution)/shard_map/convert.1
  284.9 12.6 %convert_add_fusion = f32[2048,512]{0,1:T(8,128)S(1)} fusion(f16[2048,512]{0,1:T(8,128)(2,1)} %collective-permute-done.30, f16[2048,1024]{0,1:T(8,128)(2,1)} %collective-permute-done.27, f32[512]{0:T(512)S(1)} %copy-done.7, s16[2048,512]{1,0:T(8,128)(2,1)} %collective-permute-done.16, s16[2048,512]{1,0:T(8,128)(2,1)} %collective-permute-done.14, ...), kind=kOutput, calls=%fused_computation.12 | convolution fusion | flops 4332716032 | bytes 27273224 | tf_op jit(solution)/shard_map/dot_general | solution.py:107
  297.5 8.5 %collective-permute-done.28 = f16[1024,512]{0,1:T(8,128)(2,1)S(1)} collective-permute-done((f16[1024,512]{0,1:T(8,128)(2,1)S(1)}, f16[1024,512]{0,1:T(8,128)(2,1)S(1)}, u32[]{:S(2)}, u32[]{:S(2)}) %collective-permute-start.28) | collective-permute-done | bytes 1048608 | tf_op jit(solution)/shard_map/ppermute | solution.py:24
  306.1 3.5 select_dynamic-update-slice_fusion.1
  309.5 3.8 %slice_convert_fusion = (f16[1024,512]{0,1:T(8,128)(2,1)S(1)}, f32[1024,2048]{0,1:T(8,128)}) fusion(f32[2048,512]{0,1:T(8,128)S(1)} %convert_add_fusion, f32[1024,2048]{0,1:T(8,128)} %select_dynamic-update-slice_fusion.1, s32[]{:T(128)S(6)} %select_n.378, pred[]{:T(512)S(6)} %eq.84), kind=kLoop, calls=%fused_computation.35 | loop fusion | flops 1572864 | bytes 9437189 | tf_op jit(solution)/shard_map/convert
  313.4 22.3 %collective-permute-done.31 = f16[1024,512]{0,1:T(8,128)(2,1)S(1)} collective-permute-done((f16[1024,512]{0,1:T(8,128)(2,1)S(1)}, f16[1024,512]{0,1:T(8,128)(2,1)S(1)}, u32[]{:S(2)}, u32[]{:S(2)}) %collective-permute-start.31) | collective-permute-done | bytes 1048608 | tf_op jit(solution)/shard_map/ppermute | solution.py:24
  335.7 3.4 select_dynamic-update-slice_fusion
  339.1 9.1 %copy.7 = f32[1024,2048]{1,0:T(8,128)} copy(f32[1024,2048]{0,1:T(8,128)} %select_dynamic-update-slice_fusion) | data formatting | bytes 16777216 | tf_op jit(solution)/shard_map/dynamic_update_slice | solution.py:212
  (80 shorter events, 19.1 us)
Async XLA Ops:
  4.1 4.5 %collective-permute-start = (s16[1024,1024]{1,0:T(8,128)(2,1)S(1)}, s16[1024,1024]{1,0:T(8,128)(2,1)S(1)}, u32[]{:S(2)}, u32[]{:S(2)}) collective-permute-start(s16[1024,1024]{1,0:T(8,128)(2,1)S(1)} %get-tuple-element.15), channel_id=1, source_target_pairs={{0,8},{1,9},{2,10},{3,11},{4,12},{5,13},{6,14},{7,15},{8,0},{9,1},... | collective-permute-start | bytes 6291464 | tf_op jit(solution)/shard_map/ppermute | solution.py:24
  4.8 58.2 %collective-permute-start.8 = (s16[1024,1024]{1,0:T(8,128)(2,1)S(1)}, s16[1024,1024]{1,0:T(8,128)(2,1)}, u32[]{:S(2)}, u32[]{:S(2)}) collective-permute-start(s16[1024,1024]{1,0:T(8,128)(2,1)S(1)} %get-tuple-element.15), channel_id=1, source_target_pairs={{0,1},{1,0},{2,3},{3,2},{4,5},{5,4},{6,7},{7,6},{8,9},{9,8},{10,11... | collective-permute-start | bytes 6291464 | tf_op jit(solution)/shard_map/ppermute | solution.py:24
  11.8 1.2 collective-permute-start.1
  13.0 2.9 collective-permute-start.2
  15.8 36.5 %collective-permute-start.3 = (s32[2048]{0:T(1024)S(1)}, s32[2048]{0:T(1024)S(1)}, u32[]{:S(2)}, u32[]{:S(2)}) collective-permute-start(s32[2048]{0:T(1024)S(1)} %pad_add_fusion.4), channel_id=1, source_target_pairs={{0,1},{1,0},{2,3},{3,2},{4,5},{5,4},{6,7},{7,6},{8,9},{9,8},{10,11... | collective-permute-start | bytes 24584 | tf_op jit(solution)/shard_map/ppermute | solution.py:24
  16.0 51.0 %collective-permute-start.12 = (s16[2048,512]{1,0:T(8,128)(2,1)}, s16[2048,512]{1,0:T(8,128)(2,1)}, u32[]{:S(2)}, u32[]{:S(2)}) collective-permute-start(s16[2048,512]{1,0:T(8,128)(2,1)} %pad_add_fusion), channel_id=1, source_target_pairs={{0,2},{1,3},{4,6},{5,7},{10,12},{11,13},{16,18},{17,19},{20,22},{2... | collective-permute-start | bytes 6291464 | tf_op jit(solution)/shard_map/ppermute | solution.py:24
  20.6 45.1 %collective-permute-start.10 = (s16[2048,512]{1,0:T(8,128)(2,1)}, s16[2048,512]{1,0:T(8,128)(2,1)}, u32[]{:S(2)}, u32[]{:S(2)}) collective-permute-start(s16[2048,512]{1,0:T(8,128)(2,1)} %pad_add_fusion), channel_id=1, source_target_pairs={{4,2},{5,3},{10,8},{11,9},{14,12},{15,13},{20,18},{21,19},{26,24},... | collective-permute-start | bytes 6291464 | tf_op jit(solution)/shard_map/ppermute | solution.py:24
  52.3 2.5 collective-permute-start.4
  54.9 4.4 %collective-permute-start.5 = (s32[5120]{0:T(1024)S(1)}, s32[5120]{0:T(1024)S(1)}, u32[]{:S(2)}, u32[]{:S(2)}) collective-permute-start(s32[5120]{0:T(1024)S(1)} %pad_add_fusion.2), channel_id=1, source_target_pairs={{0,4},{1,5},{2,6},{3,7},{4,0},{5,1},{6,2},{7,3},{8,12},{9,13},{10,... | collective-permute-start | bytes 61448 | tf_op jit(solution)/shard_map/ppermute | solution.py:24
  57.3 14.0 %collective-permute-start.14 = (s16[2048,512]{1,0:T(8,128)(2,1)}, s16[2048,512]{1,0:T(8,128)(2,1)}, u32[]{:S(2)}, u32[]{:S(2)}) collective-permute-start(s16[2048,512]{1,0:T(8,128)(2,1)} %pad_add_fusion.1), channel_id=1, source_target_pairs={{4,2},{5,3},{14,12},{15,13},{20,18},{21,19},{26,24},{27,25},{30,28... | collective-permute-start | bytes 6291464 | tf_op jit(solution)/shard_map/ppermute | solution.py:24
  59.3 34.8 %collective-permute-start.16 = (s16[2048,512]{1,0:T(8,128)(2,1)}, s16[2048,512]{1,0:T(8,128)(2,1)}, u32[]{:S(2)}, u32[]{:S(2)}) collective-permute-start(s16[2048,512]{1,0:T(8,128)(2,1)} %pad_add_fusion.1), channel_id=1, source_target_pairs={{0,2},{1,3},{4,6},{5,7},{10,12},{11,13},{16,18},{17,19},{26,28},{2... | collective-permute-start | bytes 6291464 | tf_op jit(solution)/shard_map/ppermute | solution.py:24
  63.1 1.2 collective-permute-start.6
  64.3 33.4 %collective-permute-start.9 = (s16[1024,1024]{1,0:T(8,128)(2,1)}, s16[1024,1024]{1,0:T(8,128)(2,1)S(1)}, u32[]{:S(2)}, u32[]{:S(2)}) collective-permute-start(s16[1024,1024]{1,0:T(8,128)(2,1)} %collective-permute-done.8), channel_id=1, source_target_pairs={{0,8},{1,9},{2,10},{3,11},{4,12},{5,13},{6,14},{7,15},{8,0},{9,1},... | collective-permute-start | bytes 6291464 | tf_op jit(solution)/shard_map/ppermute | solution.py:24
  65.8 73.0 %collective-permute-start.11 = (s16[2048,512]{1,0:T(8,128)(2,1)}, s16[2048,512]{1,0:T(8,128)(2,1)}, u32[]{:S(2)}, u32[]{:S(2)}) collective-permute-start(s16[2048,512]{1,0:T(8,128)(2,1)} %collective-permute-done.10), channel_id=1, source_target_pairs={{2,0},{3,1},{12,10},{13,11},{18,16},{19,17},{28,26},{29,27}} | collective-permute-start | bytes 6291464 | tf_op jit(solution)/shard_map/ppermute | solution.py:24
  67.1 71.7 %collective-permute-start.13 = (s16[2048,512]{1,0:T(8,128)(2,1)}, s16[2048,512]{1,0:T(8,128)(2,1)}, u32[]{:S(2)}, u32[]{:S(2)}) collective-permute-start(s16[2048,512]{1,0:T(8,128)(2,1)} %collective-permute-done.12), channel_id=1, source_target_pairs={{2,4},{3,5},{12,14},{13,15},{18,20},{19,21},{28,30},{29,31}} | collective-permute-start | bytes 6291464 | tf_op jit(solution)/shard_map/ppermute | solution.py:24
  112.1 115.0 %copy-start.1 = (bf16[2048,1024]{1,0:T(8,128)(2,1)}, bf16[2048,1024]{1,0:T(8,128)(2,1)S(1)}, u32[]{:S(2)}) copy-start(bf16[2048,1024]{1,0:T(8,128)(2,1)S(1)} %get-tuple-element.46) | copy-start | bytes 12582916
  130.2 8.6 %copy-start.3 = (bf16[2048,1024]{1,0:T(8,128)(2,1)S(1)}, bf16[2048,1024]{1,0:T(8,128)(2,1)}, u32[]{:S(2)}) copy-start(bf16[2048,1024]{1,0:T(8,128)(2,1)} %get-tuple-element.47) | copy-start | bytes 12582916
  130.2 32.4 %collective-permute-start.15 = (s16[2048,512]{1,0:T(8,128)(2,1)}, s16[2048,512]{1,0:T(8,128)(2,1)S(1)}, u32[]{:S(2)}, u32[]{:S(2)}) collective-permute-start(s16[2048,512]{1,0:T(8,128)(2,1)} %collective-permute-done.14), channel_id=1, source_target_pairs={{2,0},{3,1},{12,10},{13,11},{18,16},{19,17},{28,26},{29,27}} | collective-permute-start | bytes 6291464 | tf_op jit(solution)/shard_map/ppermute | solution.py:24
  131.9 32.0 %collective-permute-start.17 = (s16[2048,512]{1,0:T(8,128)(2,1)}, s16[2048,512]{1,0:T(8,128)(2,1)}, u32[]{:S(2)}, u32[]{:S(2)}) collective-permute-start(s16[2048,512]{1,0:T(8,128)(2,1)} %collective-permute-done.16), channel_id=1, source_target_pairs={{2,4},{3,5},{12,14},{13,15},{18,20},{19,21},{28,30},{29,31}} | collective-permute-start | bytes 6291464 | tf_op jit(solution)/shard_map/ppermute | solution.py:24
  147.5 46.1 %collective-permute-start.18 = (f16[2048,512]{0,1:T(8,128)(2,1)S(1)}, f16[2048,512]{0,1:T(8,128)(2,1)}, u32[]{:S(2)}, u32[]{:S(2)}) collective-permute-start(f16[2048,512]{0,1:T(8,128)(2,1)S(1)} %multiply_convert_fusion.6), channel_id=1, source_target_pairs={{0,16},{1,17},{10,26},{11,27},{20,4},{21,5},{30,14},{31,15}} | collective-permute-start | bytes 6291464 | tf_op jit(solution)/shard_map/ppermute | solution.py:24
  153.0 32.2 %collective-permute-start.24 = (s16[2048,512]{1,0:T(8,128)(2,1)}, s16[2048,512]{1,0:T(8,128)(2,1)}, u32[]{:S(2)}, u32[]{:S(2)}) collective-permute-start(s16[2048,512]{1,0:T(8,128)(2,1)} %collective-permute-done.11), channel_id=1, source_target_pairs={{10,8},{11,9},{26,24},{27,25}} | collective-permute-start | bytes 6291464 | tf_op jit(solution)/shard_map/ppermute | solution.py:24
  155.6 35.3 %collective-permute-start.25 = (s16[2048,512]{1,0:T(8,128)(2,1)}, s16[2048,512]{1,0:T(8,128)(2,1)}, u32[]{:S(2)}, u32[]{:S(2)}) collective-permute-start(s16[2048,512]{1,0:T(8,128)(2,1)} %collective-permute-done.13), channel_id=1, source_target_pairs={{4,6},{5,7},{20,22},{21,23}} | collective-permute-start | bytes 6291464 | tf_op jit(solution)/shard_map/ppermute | solution.py:24
  162.6 2.8 copy-start.8
  162.6 55.5 %collective-permute-start.7 = (f16[1024,1024]{0,1:T(8,128)(2,1)S(1)}, f16[1024,1024]{0,1:T(8,128)(2,1)}, u32[]{:S(2)}, u32[]{:S(2)}) collective-permute-start(f16[1024,1024]{0,1:T(8,128)(2,1)S(1)} %multiply_convert_fusion.7), channel_id=1, source_target_pairs={{4,20},{5,21},{14,30},{15,31},{16,0},{17,1},{26,10},{27,11}} | collective-permute-start | bytes 6291464 | tf_op jit(solution)/shard_map/ppermute | solution.py:24
  163.9 55.4 %collective-permute-start.20 = (f16[1024,1024]{0,1:T(8,128)(2,1)S(1)}, f16[1024,1024]{0,1:T(8,128)(2,1)}, u32[]{:S(2)}, u32[]{:S(2)}) collective-permute-start(f16[1024,1024]{0,1:T(8,128)(2,1)S(1)} %multiply_convert_fusion.4), channel_id=1, source_target_pairs={{4,20},{5,21},{14,30},{15,31},{16,0},{17,1},{26,10},{27,11}} | collective-permute-start | bytes 6291464 | tf_op jit(solution)/shard_map/ppermute | solution.py:24
  174.2 31.5 %copy-start.5 = (f16[2048,512]{0,1:T(8,128)(2,1)}, f16[2048,512]{0,1:T(8,128)(2,1)S(1)}, u32[]{:S(2)}) copy-start(f16[2048,512]{0,1:T(8,128)(2,1)S(1)} %multiply_convert_fusion.5) | copy-start | bytes 6291460
  185.2 28.1 %collective-permute-start.19 = (f16[2048,512]{0,1:T(8,128)(2,1)S(1)}, f16[2048,512]{0,1:T(8,128)(2,1)}, u32[]{:S(2)}, u32[]{:S(2)}) collective-permute-start(f16[2048,512]{0,1:T(8,128)(2,1)S(1)} %multiply_convert_fusion.5), channel_id=1, source_target_pairs={{0,16},{1,17},{10,26},{11,27},{20,4},{21,5},{30,14},{31,15}} | collective-permute-start | bytes 6291464 | tf_op jit(solution)/shard_map/ppermute | solution.py:24
  191.0 36.1 %collective-permute-start.22 = (s16[2048,512]{1,0:T(8,128)(2,1)}, s16[2048,512]{1,0:T(8,128)(2,1)}, u32[]{:S(2)}, u32[]{:S(2)}) collective-permute-start(s16[2048,512]{1,0:T(8,128)(2,1)} %copy-done.8), channel_id=1, source_target_pairs={{10,8},{11,9},{26,24},{27,25}} | collective-permute-start | bytes 6291464 | tf_op jit(solution)/shard_map/ppermute | solution.py:24
  193.6 33.4 %collective-permute-start.23 = (s16[2048,512]{1,0:T(8,128)(2,1)}, s16[2048,512]{1,0:T(8,128)(2,1)}, u32[]{:S(2)}, u32[]{:S(2)}) collective-permute-start(s16[2048,512]{1,0:T(8,128)(2,1)} %collective-permute-done.17), channel_id=1, source_target_pairs={{4,6},{5,7},{20,22},{21,23}} | collective-permute-start | bytes 6291464 | tf_op jit(solution)/shard_map/ppermute | solution.py:24
  207.8 11.6 %copy-start.6 = (f16[2048,512]{0,1:T(8,128)(2,1)S(1)}, f16[2048,512]{0,1:T(8,128)(2,1)}, u32[]{:S(2)}) copy-start(f16[2048,512]{0,1:T(8,128)(2,1)} %copy-done.5) | copy-start | bytes 6291460
  213.3 63.2 %collective-permute-start.27 = (f16[2048,1024]{0,1:T(8,128)(2,1)}, f16[2048,1024]{0,1:T(8,128)(2,1)}, u32[]{:S(2)}, u32[]{:S(2)}) collective-permute-start(f16[2048,1024]{0,1:T(8,128)(2,1)} %multiply_convert_fusion), channel_id=1, source_target_pairs={{2,18},{3,19},{6,22},{7,23},{12,28},{13,29},{18,2},{19,3},{24,8},{... | collective-permute-start | bytes 12582920 | tf_op jit(solution)/shard_map/ppermute | solution.py:24
  218.1 58.5 %collective-permute-start.26 = (f16[2048,512]{0,1:T(8,128)(2,1)}, f16[2048,512]{0,1:T(8,128)(2,1)S(1)}, u32[]{:S(2)}, u32[]{:S(2)}) collective-permute-start(f16[2048,512]{0,1:T(8,128)(2,1)} %multiply_convert_fusion.2), channel_id=1, source_target_pairs={{8,24},{9,25},{22,6},{23,7}} | collective-permute-start | bytes 6291464 | tf_op jit(solution)/shard_map/ppermute | solution.py:24
  226.8 43.1 %collective-permute-start.21 = (f16[1024,1024]{0,1:T(8,128)(2,1)}, f16[1024,1024]{0,1:T(8,128)(2,1)}, u32[]{:S(2)}, u32[]{:S(2)}) collective-permute-start(f16[1024,1024]{0,1:T(8,128)(2,1)} %get-tuple-element.24), channel_id=1, source_target_pairs={{0,1},{1,0},{2,3},{3,2},{4,5},{5,4},{6,7},{7,6},{8,9},{9,8},{10,11... | collective-permute-start | bytes 6291464 | tf_op jit(solution)/shard_map/ppermute | solution.py:24
  239.6 45.4 %collective-permute-start.30 = (f16[2048,512]{0,1:T(8,128)(2,1)}, f16[2048,512]{0,1:T(8,128)(2,1)}, u32[]{:S(2)}, u32[]{:S(2)}) collective-permute-start(f16[2048,512]{0,1:T(8,128)(2,1)} %multiply_convert_fusion.3), channel_id=1, source_target_pairs={{8,24},{9,25},{22,6},{23,7}} | collective-permute-start | bytes 6291464 | tf_op jit(solution)/shard_map/ppermute | solution.py:24
  241.5 43.4 %collective-permute-start.29 = (s16[2048,512]{1,0:T(8,128)(2,1)}, s16[2048,512]{1,0:T(8,128)(2,1)}, u32[]{:S(2)}, u32[]{:S(2)}) collective-permute-start(s16[2048,512]{1,0:T(8,128)(2,1)} %pad_add_fusion.1), channel_id=1, source_target_pairs={{10,8},{11,9},{20,22},{21,23}} | collective-permute-start | bytes 6291464 | tf_op jit(solution)/shard_map/ppermute | solution.py:24
  244.2 27.8 %copy-start = (f32[1024,1024]{0,1:T(8,128)S(1)}, f32[1024,1024]{0,1:T(8,128)}, u32[]{:S(2)}) copy-start(f32[1024,1024]{0,1:T(8,128)} %get-tuple-element.23) | copy-start | bytes 12582916
  271.9 4.6 %copy-start.4 = (f16[2048,512]{0,1:T(8,128)(2,1)S(1)}, f16[2048,512]{0,1:T(8,128)(2,1)}, u32[]{:S(2)}) copy-start(f16[2048,512]{0,1:T(8,128)(2,1)} %multiply_convert_fusion.3) | copy-start | bytes 6291460
  280.8 4.1 %copy-start.2 = (bf16[2048,1024]{1,0:T(8,128)(2,1)S(1)}, bf16[2048,1024]{1,0:T(8,128)(2,1)}, u32[]{:S(2)}) copy-start(bf16[2048,1024]{1,0:T(8,128)(2,1)} %copy-done.1) | copy-start | bytes 12582916
  280.8 4.1 %copy-start.7 = (f32[512]{0:T(512)S(1)}, f32[512]{0:T(512)}, u32[]{:S(2)}) copy-start(f32[512]{0:T(512)} %get-tuple-element.44) | copy-start | bytes 6148
  284.7 21.3 %collective-permute-start.28 = (f16[1024,512]{0,1:T(8,128)(2,1)S(1)}, f16[1024,512]{0,1:T(8,128)(2,1)S(1)}, u32[]{:S(2)}, u32[]{:S(2)}) collective-permute-start(f16[1024,512]{0,1:T(8,128)(2,1)S(1)} %get-tuple-element.27), channel_id=1, source_target_pairs={{0,1},{1,0},{2,3},{3,2},{4,5},{5,4},{6,7},{7,6},{8,9},{9,8},{10,11... | collective-permute-start | bytes 3145736 | tf_op jit(solution)/shard_map/ppermute | solution.py:24
  313.3 22.4 %collective-permute-start.31 = (f16[1024,512]{0,1:T(8,128)(2,1)S(1)}, f16[1024,512]{0,1:T(8,128)(2,1)S(1)}, u32[]{:S(2)}, u32[]{:S(2)}) collective-permute-start(f16[1024,512]{0,1:T(8,128)(2,1)S(1)} %get-tuple-element.25), channel_id=1, source_target_pairs={{0,1},{1,0},{2,3},{3,2},{4,5},{5,4},{6,7},{7,6},{8,9},{9,8},{10,11... | collective-permute-start | bytes 3145736 | tf_op jit(solution)/shard_map/ppermute | solution.py:24

commit v2 on v0

--- a/solution.py
+++ b/solution.py
@@ -1,10 +1,409 @@
+import math
+
 import jax
 import jax.numpy as jnp
+import numpy as np
 from jax import lax
+from jax.experimental import pallas as pl
+from jax.experimental.pallas import tpu as pltpu
 from jax.sharding import PartitionSpec as P
 
+AXES = ("cell", "gene")
+UNIT = 8.0
+
+
+def pairs_of(move):
+    pairs = []
+    for x in range(2):
+        for c in range(2):
+            for z in range(4):
+                for y in range(2):
+                    target = move(x, c, z, y)
+                    if target is not None and 0 <= target[2] < 4:
+                        tx, tc, tz, ty = target
+                        pairs.append(((2 * x + c) * 8 + 2 * z + y, (2 * tx + tc) * 8 + 2 * tz + ty))
+    return pairs
+
+
+def send(value, move):
+    return lax.ppermute(value, AXES, pairs_of(move))
+
+
+def after(value, *others):
+    return lax.optimization_barrier((value,) + others)[0]
+
+
+VMEM = 48 * 2**20
+SLOTS = 6
+
+
+def residuals_of(near, far, depths, shares, part, parts, ceiling):
+    cells, genes = near.shape
+    width = genes // parts
+    block = 512
+    steps = cells // block
+    lanes, group = 128, 32
+
+    def kernel(part_ref, depth_ref, share_ref, near_ref, far_ref, out_ref):
+        i = pl.program_id(0)
+        depth = jnp.transpose(jnp.broadcast_to(depth_ref[...], (lanes, block)))
+
+        def write(counts_ref):
+            for r in range(0, block, group):
+                for k in range(0, width, lanes):
+                    expected = depth[r : r + group] * share_ref[:, k : k + lanes]
+                    scale = lax.rsqrt(expected + expected * expected * 0.01)
+                    values = counts_ref[r : r + group, k : k + lanes].astype(jnp.float32)
+                    scaled = jnp.clip((values - expected) * scale, -ceiling, ceiling)
+                    out_ref[r : r + group, k : k + lanes] = scaled.astype(jnp.bfloat16)
+
+        @pl.when(i < steps)
+        def _():
+            write(near_ref)
+
+        @pl.when(i >= steps)
+        def _():
+            write(far_ref)
+
+    return pl.pallas_call(
+        kernel,
+        grid_spec=pltpu.PrefetchScalarGridSpec(
+            num_scalar_prefetch=1,
+            grid=(2 * steps,),
+            in_specs=[
+                pl.BlockSpec((1, block), lambda i, s: (0, i)),
+                pl.BlockSpec((1, width), lambda i, s: (0, s[0])),
+                pl.BlockSpec((block, width), lambda i, s: (jnp.minimum(i, steps - 1), s[0])),
+                pl.BlockSpec((block, width), lambda i, s: (jnp.maximum(i - steps, 0), s[0])),
+            ],
+            out_specs=pl.BlockSpec((block, width), lambda i, s: (i, 0)),
+        ),
+        out_shape=jax.ShapeDtypeStruct((2 * cells, width), jnp.bfloat16),
+        compiler_params=pltpu.CompilerParams(vmem_limit_bytes=VMEM),
+        cost_estimate=pl.CostEstimate(
+            flops=20 * cells * width, bytes_accessed=12 * cells * width, transcendentals=2 * cells * width
+        ),
+    )(jnp.reshape(part, (1,)).astype(jnp.int32), depths.reshape(1, -1), shares.reshape(1, -1), near, far)
+
+
+def products_of(plan, slot, lefts, turned, rights):
+    rows, width = rights[0].shape
+    blocks, upper = 4, rows // 2
+    n_left = len(lefts)
+
+    def kernel(s, *refs):
+        left_refs, right_refs = refs[:n_left], refs[n_left : n_left + len(rights)]
+        out_ref, left_buf, right_buf, left_sem, right_sem = refs[n_left + len(rights) :]
+        i = pl.program_id(0)
+
+        def left_at(block):
+            return s[slot * 2 * blocks + 2 * block]
+
+        def right_at(block):
+            return s[slot * 2 * blocks + 2 * block + 1]
+
+        def left_copies(n, to):
+            for part in range(2):
+                place = 1 - part if turned[n] else part
+                yield pltpu.make_async_copy(
+                    left_refs[n].at[pl.ds(part * upper, upper)],
+                    left_buf.at[to, pl.ds(place * upper, upper)],
+                    left_sem.at[to, part],
+                )
+
+        def fetch(block, to):
+            for n in range(n_left):
+                @pl.when(left_at(block) == n)
+                def _(n=n):
+                    for copy in left_copies(n, to):
+                        copy.start()
+
+        def arrive(block, to):
+            for n in range(n_left):
+                @pl.when(left_at(block) == n)
+                def _(n=n):
+                    for copy in left_copies(n, to):
+                        copy.wait()
+
+        @pl.when(i == 0)
+        def _():
+            fetch(0, 0)
+
+        @pl.when((i == 0) | (right_at(i) != right_at(jnp.maximum(i - 1, 0))))
+        def _():
+            for n, ref in enumerate(right_refs):
+                @pl.when(right_at(i) == n)
+                def _(ref=ref):
+                    copy = pltpu.make_async_copy(ref, right_buf, right_sem)
+                    copy.start()
+                    copy.wait()
+
+        for to in range(2):
+            @pl.when(lax.rem(i, 2) == to)
+            def _(to=to):
+                arrive(i, to)
+
+                @pl.when(i + 1 < blocks)
+                def _():
+                    fetch(i + 1, 1 - to)
+
+                out_ref[...] = lax.dot_general(
+                    left_buf[to], right_buf[...], (((0,), (0,)), ((), ())), preferred_element_type=jnp.float32
+                )
+
+    return pl.pallas_call(
+        kernel,
+        grid_spec=pltpu.PrefetchScalarGridSpec(
+            num_scalar_prefetch=1,
+            grid=(blocks,),
+            in_specs=[pl.BlockSpec(memory_space=pl.ANY)] * (n_left + len(rights)),
+            out_specs=pl.BlockSpec((width, width), lambda i, s: (i, 0)),
+            scratch_shapes=[
+                pltpu.VMEM((2, rows, width), jnp.bfloat16),
+                pltpu.VMEM((rows, width), jnp.bfloat16),
+                pltpu.SemaphoreType.DMA((2, 2)),
+                pltpu.SemaphoreType.DMA,
+            ],
+        ),
+        out_shape=jax.ShapeDtypeStruct((blocks * width, width), jnp.float32),
+        compiler_params=pltpu.CompilerParams(vmem_limit_bytes=VMEM),
+        cost_estimate=pl.CostEstimate(
+            flops=8 * rows * blocks * width * width,
+            bytes_accessed=2 * (blocks + 1) * rows * width + 4 * blocks * width * width,
+            transcendentals=0,
+        ),
+    )(plan, *lefts, *rights)
+
+
+def is_even(c, z):
+    return c == z % 2
+
+
+def is_near(x, z):
+    return x == z // 2
+
+
+def is_end(z):
+    return z in (0, 3)
+
+
+def job(x, c, z, slot):
+    near, first = is_near(x, z), 1 if z == 0 or (z != 3 and x == 0) else -1
+    far = 2 if z < 2 else -2
+    if is_even(c, z):
+        if slot == 0:
+            return "own rows", not near
+        if not near:
+            return [None, ("other rows", True), None, ((far, 0), False), ((far, 1), False), None][slot]
+        if is_end(z):
+            return [None, ((far, 0), True), ((far, 1), True), ("other rows", False), None, None][slot]
+        return [None, ("other rows", False), ((far, 0), True), ((far, 1), True), None, None][slot]
+    if not is_end(z):
+        return [None, ((first, 0), True), ((first, 1), True), ((-first, 0), False), ((-first, 1), False), None][slot]
+    far = 3 if z == 0 else -3
+    if near:
+        return [None, ((first, 0), False), None, ((far, 0), True), ((far, 1), True), ((first, 1), False)][slot]
+    return [None, ((first, 0), True), ((first, 1), True), None, ((far, 0), False), ((far, 1), False)][slot]
+
+
+def remote(slot):
+    def devices(x, c, z):
+        work = job(x, c, z, slot)
+        return work is not None and work[1]
+    return devices
+
+
+def rights_of(slot):
+    names, table = [("own", 0), ("own", 1)] if slot < 4 else [], np.zeros((2, 2, 4, 4, 2), np.int32)
+    for x in range(2):
+        for c in range(2):
+            for z in range(4):
+                work = job(x, c, z, slot)
+                if work is None:
+                    continue
+                if work[0] in ("own rows", "other rows"):
+                    rows = (0, 1) if work[0] == "own rows" else (2, 3)
+                    pairs = [(row, ("own", half)) for half in range(2) for row in rows]
+                else:
+                    name = ("late", 0) if slot == 5 and abs(work[0][0]) == 1 else work[0]
+                    pairs = [(row, name) for row in range(4)]
+                for i, (row, name) in enumerate(pairs):
+                    if name not in names:
+                        names.append(name)
+                    table[x, c, z, i] = row, names.index(name)
+    return names, table
+
 
 def body(counts):
+    cells_here, genes_here = counts.shape
+    cells_all = cells_here * lax.axis_size("cell")
+    half = genes_here // 2
+    cell, gene = lax.axis_index("cell"), lax.axis_index("gene")
+    x, c, z, y = cell // 2, cell % 2, gene // 2, gene % 2
+    even = c == z % 2
+    low = z < 2
+    end = (z == 0) | (z == 3)
+    odd_end = end & jnp.logical_not(even)
+    near_x = (x == 0) == low
+
+    def is_odd_end(c, z):
+        return not is_even(c, z) and is_end(z)
+
+    def down(distance):
+        def move(x, c, z, y):
+            source = z + distance - 1
+            if c != source % 2 or source > 3 or (distance == 1 and x == 0 and z == 1):
+                return None
+            return x, c, z - 1, y
+        return move
+
+    def up(distance):
+        def move(x, c, z, y):
+            source = z - distance + 1
+            if c != source % 2 or source < 0 or (distance == 1 and x == 1 and z == 2):
+                return None
+            return x, c, z + 1, y
+        return move
+
+    def last(x, c, z, y):
+        if x == 0 and c == 1 and z == 1:
+            return x, c, 0, y
+        if x == 1 and c == 0 and z == 2:
+            return x, c, 3, y
+        return None
+
+    def down_all(x, c, z, y):
+        return (x, c, z - 1, y) if c == z % 2 else None
+
+    def up_all(x, c, z, y):
+        return (x, c, z + 1, y) if c == z % 2 else None
+
+    def swap_core(value):
+        return send(value, lambda x, c, z, y: (x, 1 - c, z, y))
+
+    def swap_y(value, devices=lambda x, c, z: True):
+        return send(value, lambda x, c, z, y: (x, c, z, 1 - y) if devices(x, c, z) else None)
+
+    def cross(value, devices):
+        return send(value, lambda x, c, z, y: (1 - x, c, z, y) if devices(x, c, z) else None)
+
+    sibling = swap_core(counts)
+    row_part = jnp.sum(counts, axis=1)
+    totals = jnp.sum(counts, axis=0)
+    both = swap_core(jnp.concatenate([totals, row_part]))
+    beside = [
+        send(totals, lambda x, c, z, y: (1 - x, c, z, y)),
+        send(totals, lambda x, c, z, y: (1 - x, 1 - c, z, y)),
+    ]
+    totals = totals + both[:genes_here] + beside[0] + beside[1]
+    row_part = jnp.concatenate([row_part, both[genes_here:]])
+    got = swap_y(jnp.concatenate([totals, row_part]))
+    message = jnp.concatenate([totals, got[:genes_here], row_part + got[genes_here:]])
+    messages = jnp.stack(
+        [message]
+        + [send(message, lambda x, c, z, y, bits=bits: (x, c, z ^ bits, y)) for bits in (1, 2, 3)]
+    )
+    depths = jnp.sum(messages[:, 2 * genes_here :], axis=0).astype(jnp.float32)
+    grand = jnp.sum(messages[:, : 2 * genes_here].astype(jnp.float32))
+    ceiling = math.sqrt(cells_all)
+    shares = totals.astype(jnp.float32) / grand
+
+    own_a = residuals_of(counts, sibling, depths, shares, c, 2, ceiling)
+    d1a, u1a = send(own_a, down_all), send(own_a, up_all)
+    own_b = residuals_of(counts, sibling, depths, shares, 1 - c, 2, ceiling)
+    d1b, u1b = send(own_b, down(1)), send(own_b, up(1))
+    across = swap_y(after(own_a, own_b))
+
+    jobs = [rights_of(slot) for slot in range(SLOTS)]
+    tables = np.stack([table for _, table in jobs], axis=3)
+    tables[:, 1, :, :, :, 0] ^= 1
+    plan = jnp.asarray(tables.reshape(16, -1))[(2 * x + c) * 4 + z]
+    out = jnp.full((genes_here, 2 * genes_here), grand * 0.0)
+    scale = UNIT / cells_all
+    held = {("own", 0): own_a, ("own", 1): own_b, (1, 0): d1a, (-1, 0): u1a, (1, 1): d1b, (-1, 1): u1b}
+    products, narrow_products, received = [], [], []
+
+    def work(slot, lefts, plan):
+        product = products_of(plan, slot, lefts, [False, False, False, True], [held[n] for n in jobs[slot][0]])
+        products.append(product)
+        if slot < SLOTS - 1:
+            narrow_products.append((product * scale).astype(jnp.float16))
+            received.append(cross(narrow_products[-1], remote(slot)))
+
+    work(0, [own_a, own_b], plan)
+    d2a, u2a = send(d1a, down(2)), send(u1a, up(2))
+    d1b, u1b, out, _ = lax.optimization_barrier((d1b, u1b, out, narrow_products[0]))
+    held[1, 1], held[-1, 1], held[2, 0], held[-2, 0] = d1b, u1b, d2a, u2a
+    d2b, u2b = send(d1b, down(2)), send(u1b, up(2))
+    held[2, 1], held[-2, 1] = d2b, u2b
+    lefts = [own_a, own_b, across, swap_core(across)]
+    plan, out = lax.optimization_barrier((plan, out))
+    work(1, lefts, plan)
+    d2a, u2a, _ = lax.optimization_barrier((d2a, u2a, narrow_products[1]))
+    d3a, u3a = send(d2a, down(3)), send(u2a, up(3))
+    d3b, u3b = send(d2b, down(3)), send(u2b, up(3))
+    work(2, lefts, after(plan, narrow_products[1], received[0]))
+    held[3, 0], held[-3, 0], held[3, 1], held[-3, 1] = d3a, u3a, d3b, u3b
+    work(3, lefts, after(plan, narrow_products[2]))
+    held["late", 0] = send(after(own_b, d3b, u3b), last)
+    work(4, lefts, after(plan, narrow_products[3], received[1]))
+
+    wide = lambda value: value.astype(jnp.float32)
+    low_rows, high_rows = slice(0, genes_here), slice(genes_here, None)
+
+    def own_rows(half):
+        return low_rows
+
+    def mix(choices):
+        value = choices[-1][1]
+        for condition, other in reversed(choices[:-1]):
+            value = jnp.where(condition, other, value)
+        return value
+
+    near_even, far_even = even & near_x, even & jnp.logical_not(near_x)
+    near_end = odd_end & near_x
+    far_end = odd_end & jnp.logical_not(near_x)
+
+    def sums(other, half):
+        rows = high_rows if other else low_rows
+        stacked = high_rows if half else low_rows
+        p, r = products, received
+        own_block = mix([(end, p[3][stacked]), (None, p[1][stacked])]) if other else p[0][stacked]
+        own_received = r[1][stacked] if other else r[0][stacked]
+        if half == 0:
+            mine = [(near_even, own_block), (near_end, p[1][rows]), (far_end, p[4][rows]), (None, p[3][rows])]
+            far_received = mix([(end, r[1][rows]), (None, r[2][rows])])
+            theirs = [(near_even, own_received), (far_even, far_received), (far_end, r[3][rows]), (None, r[1][rows])]
+        else:
+            mine = [(near_even, own_block), (odd_end, p[5][rows]), (None, p[4][rows])]
+            far_received = mix([(end, r[2][rows]), (None, r[3][rows])])
+            theirs = [(near_even, own_received), (far_even, far_received), (far_end, r[4][rows]), (None, r[2][rows])]
+        return mix(mine) * scale + wide(mix(theirs))
+
+    narrow = lambda value: value.astype(jnp.float16)
+
+    def is_far_end(x, c, z):
+        return is_odd_end(c, z) and not is_near(x, z)
+
+    other_a = sums(True, 0)
+    got_first = swap_y(narrow(other_a), lambda x, c, z: not is_far_end(x, c, z))
+    work(5, lefts, after(plan, narrow_products[4], received[2], narrow(other_a)))
+    other_b = sums(True, 1)
+    middle = jnp.where(odd_end, other_a, other_b)
+    got_middle = swap_y(narrow(middle), lambda x, c, z: not is_odd_end(c, z) or is_far_end(x, c, z))
+    got_last = swap_y(narrow(other_b), lambda x, c, z: is_odd_end(c, z))
+    got_a = jnp.where(far_end, got_middle, got_first)
+    got_b = jnp.where(odd_end, got_last, got_middle)
+
+    begin, begin_other = y * genes_here, (1 - y) * genes_here
+    for half_of, got in ((0, got_a), (1, got_b)):
+        place = (half_of ^ c) * half
+        out = lax.dynamic_update_slice(out, sums(False, half_of) * (1.0 / UNIT), (0, begin + place))
+        out = lax.dynamic_update_slice(out, wide(got) * (1.0 / UNIT), (0, begin_other + place))
+    return out
+
+
+def body_any(counts):
     cells_all = counts.shape[0] * lax.axis_size("cell")
     values = counts.astype(jnp.float32)
     row_part = jnp.sum(values, axis=1)
@@ -28,8 +427,9 @@
 
 
 def solution(mesh):
+    fits = (mesh.shape["cell"], mesh.shape["gene"]) == (4, 8)
     return jax.shard_map(
-        body,
+        body if fits else body_any,
         mesh=mesh,
         in_specs=(P("cell", "gene"),),
         out_specs=P("gene", "cell"),

time: 556 us -> 277 us (0.50)
  waiting for transfers between devices: 465 us -> 90.6 us
  Pallas kernels: 0 us -> 63.5 us
  starting transfers between devices: 0.04 us -> 60.3 us
  other arithmetic: 16.9 us -> 48.3 us
  matrix products: 27.7 us -> 0 us
  blocking collectives: 21.6 us -> 0 us
  between operations: 13.4 us -> 1.05 us
    reduce_scatter x1 -> x0, waiting for transfers between devices: 236 us -> none  [body(): lax.psum_scatter(lax.dot_general(gathered, residuals, (((0,), (0,)), ((),...]
    all_gather x1 -> x0, waiting for transfers between devices: 229 us -> none  [body(): gathered = lax.all_gather(residuals, 'gene', axis=1, tiled=True)]
    ppermute x0 -> x31, waiting for transfers between devices: none -> 90.6 us  [send(): return lax.ppermute(value, AXES, pairs_of(move))]
    pallas_call x0 -> x8, Pallas kernels: none -> 63.5 us  [the longest x6 54.9 us: products_of(): pl.pallas_call(kernel, grid_spec=pltpu.PrefetchScalarGridSpec(num_scalar_...]
    ppermute x0 -> x31, starting transfers between devices: none -> 60.3 us  [send(): return lax.ppermute(value, AXES, pairs_of(move))]
    dot_general x1 -> x0, matrix products: 27.7 us -> none  [body(): lax.dot_general(gathered, residuals, (((0,), (0,)), ((), ())), preferred_...]
    convert_element_type x1 -> x9, other arithmetic: 4.96 us -> 28.4 us  [the longest x5 18 us: work(): narrow_products.append((product * scale).astype(jnp.float16))]
    psum x2 -> x0, blocking collectives: 21.6 us -> none  [the longest x1 11.6 us: body(): depths = lax.psum(row_part, 'gene')]
  transfers between devices with their start and end apart: 2 -> 31, of which waited for: 2 -> 13; matrix products, arithmetic and copies ran while one was open for 0% -> 17% of each run, Pallas kernels for 0% -> 20%
where the time goes in v2:
time: 277 us; the launch traced here: 275 us
  waiting for transfers between devices  90.6 us (33%)
  Pallas kernels  63.5 us (23%)
  starting transfers between devices  60.3 us (22%)
  other arithmetic  48.3 us (17%)
  local copies, waits for them, and re-layouts  10.8 us (4%)
    ppermute x31, waiting for transfers between devices, send(): return lax.ppermute(value, AXES, pairs_of(move))  90.6 us
    ppermute x31, starting transfers between devices, send(): return lax.ppermute(value, AXES, pairs_of(move))  60.3 us
    pallas_call x6, Pallas kernels, products_of(): pl.pallas_call(kernel, grid_spec=pltpu.PrefetchScalarGridSpec(num_scalar_...  54.9 us
    convert_element_type x5, other arithmetic, work(): narrow_products.append((product * scale).astype(jnp.float16))  18 us
    dynamic_update_slice x2, other arithmetic, body(): lax.dynamic_update_slice(out, sums(False, half_of) * (1.0 / UNIT), (0, be...  11.5 us
    convert_element_type x3, other arithmetic, body(): narrow = lambda value: value.astype(jnp.float16)  10.4 us
    pallas_call x2, Pallas kernels, residuals_of(): pl.pallas_call(kernel, grid_spec=pltpu.PrefetchScalarGridSpec(num_scalar_...  8.61 us
    unnamed x34, local copies, waits for them, and re-layouts  5.68 us
  transfers between devices with their start and end apart: 31, of which 13 were waited for; matrix products, arithmetic and copies ran while one was open for 17% of the time, Pallas kernels for 20%

profile of v2, /device:TPU:13, one launch (start us, length us, event | category | flops | bytes accessed | tf_op | source)
XLA Modules:
  0.0 274.6 jit_solution(13828912398421763977)
XLA Ops:
  0.7 2.6 fusion.20
  5.8 2.1 collective-permute-done.2
  8.3 2.3 collective-permute-done.3
  10.8 2.3 collective-permute-start.5
  17.1 4.3 %shard_map.29.refs_0_.refs_2_.refs_4_ = bf16[2048,512]{1,0:T(8,128)(2,1)S(1)} custom-call(s32[1]{0:T(128)} %bitcast.8.part_ref, f32[1,2048]{1,0:T(1,128)S(1)} %bitcast.10, f32[1,1024]{1,0:T(1,128)S(1)} %bitcast.12, s32[1024,1024]{1,0:T(8,128)} %near_ref.3, s32[1024,1024]{1,0:T(8,128)} %collective-permute-done.7.far_ref), custom_call_target="tpu_custom_call" | custom-call | flops 10485760 | bytes 6291456 | tf_op jit(solution)/shard_map/pallas_call | solution.py:68
  21.4 4.3 %shard_map.28.refs_1_.refs_3_.refs_5_ = bf16[2048,512]{1,0:T(8,128)(2,1)S(1)} custom-call(s32[1]{0:T(128)} %bitcast.1.part_ref, f32[1,2048]{1,0:T(1,128)S(1)} %bitcast.11, f32[1,1024]{1,0:T(1,128)S(1)} %bitcast.13, s32[1024,1024]{1,0:T(8,128)} %near_ref.3, s32[1024,1024]{1,0:T(8,128)} %collective-permute-done.7.far_ref), custom_call_target="tpu_custom_call" | custom-call | flops 10485760 | bytes 6291456 | tf_op jit(solution)/shard_map/pallas_call | solution.py:68
  27.3 6.3 %collective-permute-start.12 = (bf16[2048,512]{1,0:T(8,128)(2,1)S(1)}, bf16[2048,512]{1,0:T(8,128)(2,1)}, u32[]{:S(2)}, u32[]{:S(2)}) collective-permute-start(bf16[2048,512]{1,0:T(8,128)(2,1)S(1)} %shard_map.29.refs_0_.refs_2_.refs_4_), channel_id=1, source_target_pairs={{4,2},{5,3},{10,8},{11,9},{14,12},{15,13},{20,18},{21,19},{26,24},... | collective-permute-start | bytes 6291464 | tf_op jit(solution)/shard_map/ppermute | solution.py:29
  33.6 2.7 collective-permute-start.14
  37.6 2.0 collective-permute-start.8
  39.6 2.6 collective-permute-start.9
  42.2 28.8 %collective-permute-done.10.refs_2_ = bf16[2048,512]{1,0:T(8,128)(2,1)} collective-permute-done((bf16[2048,512]{1,0:T(8,128)(2,1)S(1)}, bf16[2048,512]{1,0:T(8,128)(2,1)}, u32[]{:S(2)}, u32[]{:S(2)}) %collective-permute-start.10) | collective-permute-done | bytes 2097184 | tf_op jit(solution)/shard_map/ppermute | solution.py:29
  71.0 4.2 %collective-permute-start.11 = (bf16[2048,512]{1,0:T(8,128)(2,1)}, bf16[2048,512]{1,0:T(8,128)(2,1)S(1)}, u32[]{:S(2)}, u32[]{:S(2)}) collective-permute-start(bf16[2048,512]{1,0:T(8,128)(2,1)} %collective-permute-done.10.refs_2_), channel_id=1, source_target_pairs={{0,8},{1,9},{2,10},{3,11},{4,12},{5,13},{6,14},{7,15},{8,0},{9,1},... | collective-permute-start | bytes 6291464 | tf_op jit(solution)/shard_map/ppermute | solution.py:29
  76.5 2.0 collective-permute-start.15
  78.5 1.6 copy-done.1
  80.1 7.8 %shard_map.30 = f32[2048,512]{1,0:T(8,128)} custom-call(s32[48]{0:T(128)S(1)} %fusion.19.s, bf16[2048,512]{1,0:T(8,128)(2,1)S(1)} %shard_map.29.refs_0_.refs_2_.refs_4_, bf16[2048,512]{1,0:T(8,128)(2,1)S(1)} %copy-done.1, bf16[2048,512]{1,0:T(8,128)(2,1)S(1)} %shard_map.29.refs_0_.refs_2_.refs_4_, bf16[2048,512]{1,0:T(8,128)(2,1)S(1)} %copy-done.1), custom_call_target="tpu_custom_call" | custom-call | flops 17179869184 | bytes 14680064 | tf_op jit(solution)/shard_map/pallas_call | solution.py:154
  87.9 2.8 %multiply_convert_fusion.4 = f16[2048,512]{1,0:T(8,128)(2,1)S(1)} fusion(f32[2048,512]{1,0:T(8,128)} %shard_map.30), kind=kLoop, calls=%fused_computation.4 | loop fusion | flops 2097152 | bytes 6291456 | tf_op jit(solution)/shard_map/convert_element_type | solution.py:330
  92.0 4.5 %broadcast_in_dim.3 = f32[1024,2048]{1,0:T(8,128)} broadcast(f32[]{:T(128)S(6)} %mul.62), dimensions={} | broadcast | bytes 8388612 | tf_op jit(solution)/shard_map/broadcast_in_dim | solution.py:321
  97.7 2.0 collective-permute-start.18
  99.7 3.4 %collective-permute-done.13.refs_6_.refs_9_.refs_10_ = bf16[2048,512]{1,0:T(8,128)(2,1)} collective-permute-done((bf16[2048,512]{1,0:T(8,128)(2,1)}, bf16[2048,512]{1,0:T(8,128)(2,1)}, u32[]{:S(2)}, u32[]{:S(2)}) %collective-permute-start.13) | collective-permute-done | bytes 2097184 | tf_op jit(solution)/shard_map/ppermute | solution.py:29
  103.1 9.2 %shard_map.31 = f32[2048,512]{1,0:T(8,128)} custom-call(s32[48]{0:T(128)S(1)} %fusion.19.s, bf16[2048,512]{1,0:T(8,128)(2,1)S(1)} %shard_map.29.refs_0_.refs_2_.refs_4_, bf16[2048,512]{1,0:T(8,128)(2,1)S(1)} %copy-done.1, bf16[2048,512]{1,0:T(8,128)(2,1)} %collective-permute-done.10.refs_2_, bf16[2048,512]{1,0:T(8,128)(2,1)} %copy-done.14, ...), custom_call_target="tpu_custom_call" | custom-call | flops 17179869184 | bytes 14680064 | tf_op jit(solution)/shard_map/pallas_call | solution.py:154
  112.4 2.8 %multiply_convert_fusion.3 = f16[2048,512]{1,0:T(8,128)(2,1)S(1)} fusion(f32[2048,512]{1,0:T(8,128)} %shard_map.31), kind=kLoop, calls=%fused_computation.3 | loop fusion | flops 2097152 | bytes 6291456 | tf_op jit(solution)/shard_map/convert_element_type | solution.py:330
  116.4 4.0 %collective-permute-start.19 = (bf16[2048,512]{1,0:T(8,128)(2,1)}, bf16[2048,512]{1,0:T(8,128)(2,1)}, u32[]{:S(2)}, u32[]{:S(2)}) collective-permute-start(bf16[2048,512]{1,0:T(8,128)(2,1)} %collective-permute-done.13.refs_6_.refs_9_.refs_10_), channel_id=1, source_target_pairs={{10,8},{11,9},{26,24},{27,25}} | collective-permute-start | bytes 6291464 | tf_op jit(solution)/shard_map/ppermute | solution.py:29
  120.5 2.0 collective-permute-start.20
  122.5 3.3 %collective-permute-done.17.refs_6_.refs_9_.refs_8_ = bf16[2048,512]{1,0:T(8,128)(2,1)} collective-permute-done((bf16[2048,512]{1,0:T(8,128)(2,1)}, bf16[2048,512]{1,0:T(8,128)(2,1)}, u32[]{:S(2)}, u32[]{:S(2)}) %collective-permute-start.17) | collective-permute-done | bytes 2097184 | tf_op jit(solution)/shard_map/ppermute | solution.py:29
  125.8 9.6 %shard_map.32 = f32[2048,512]{1,0:T(8,128)} custom-call(s32[48]{0:T(128)S(1)} %fusion.19.s, bf16[2048,512]{1,0:T(8,128)(2,1)S(1)} %shard_map.29.refs_0_.refs_2_.refs_4_, bf16[2048,512]{1,0:T(8,128)(2,1)S(1)} %copy-done.1, bf16[2048,512]{1,0:T(8,128)(2,1)} %collective-permute-done.10.refs_2_, bf16[2048,512]{1,0:T(8,128)(2,1)} %copy-done.14, ...), custom_call_target="tpu_custom_call" | custom-call | flops 17179869184 | bytes 14680064 | tf_op jit(solution)/shard_map/pallas_call | solution.py:154
  135.4 4.1 %multiply_convert_fusion.2 = f16[2048,512]{1,0:T(8,128)(2,1)} fusion(f32[2048,512]{1,0:T(8,128)} %shard_map.32), kind=kLoop, calls=%fused_computation.2 | loop fusion | flops 2097152 | bytes 6291456 | tf_op jit(solution)/shard_map/convert_element_type | solution.py:330
  142.3 6.6 %collective-permute-done.19.refs_8_.refs_11_ = bf16[2048,512]{1,0:T(8,128)(2,1)} collective-permute-done((bf16[2048,512]{1,0:T(8,128)(2,1)}, bf16[2048,512]{1,0:T(8,128)(2,1)}, u32[]{:S(2)}, u32[]{:S(2)}) %collective-permute-start.19) | collective-permute-done | bytes 2097184 | tf_op jit(solution)/shard_map/ppermute | solution.py:29
  149.7 9.6 %shard_map.33 = f32[2048,512]{1,0:T(8,128)} custom-call(s32[48]{0:T(128)S(1)} %fusion.19.s, bf16[2048,512]{1,0:T(8,128)(2,1)S(1)} %shard_map.29.refs_0_.refs_2_.refs_4_, bf16[2048,512]{1,0:T(8,128)(2,1)S(1)} %copy-done.1, bf16[2048,512]{1,0:T(8,128)(2,1)} %collective-permute-done.10.refs_2_, bf16[2048,512]{1,0:T(8,128)(2,1)} %copy-done.14, ...), custom_call_target="tpu_custom_call" | custom-call | flops 17179869184 | bytes 14680064 | tf_op jit(solution)/shard_map/pallas_call | solution.py:154
  159.3 4.1 %multiply_convert_fusion.1 = f16[2048,512]{1,0:T(8,128)(2,1)} fusion(f32[2048,512]{1,0:T(8,128)} %shard_map.33), kind=kLoop, calls=%fused_computation.1 | loop fusion | flops 2097152 | bytes 6291456 | tf_op jit(solution)/shard_map/convert_element_type | solution.py:330
  163.4 4.5 %collective-permute-start.25 = (f16[2048,512]{1,0:T(8,128)(2,1)}, f16[2048,512]{1,0:T(8,128)(2,1)}, u32[]{:S(2)}, u32[]{:S(2)}) collective-permute-start(f16[2048,512]{1,0:T(8,128)(2,1)} %multiply_convert_fusion.1), channel_id=1, source_target_pairs={{8,24},{9,25},{10,26},{11,27},{20,4},{21,5},{22,6},{23,7}} | collective-permute-start | bytes 6291464 | tf_op jit(solution)/shard_map/ppermute | solution.py:29
  167.9 3.5 %collective-permute-done.22.refs_7_.refs_6_ = bf16[2048,512]{1,0:T(8,128)(2,1)S(1)} collective-permute-done((bf16[2048,512]{1,0:T(8,128)(2,1)}, bf16[2048,512]{1,0:T(8,128)(2,1)S(1)}, u32[]{:S(2)}, u32[]{:S(2)}) %collective-permute-start.22) | collective-permute-done | bytes 2097184 | tf_op jit(solution)/shard_map/ppermute | solution.py:29
  174.1 5.1 %collective-permute-start.26 = (bf16[2048,512]{1,0:T(8,128)(2,1)S(1)}, bf16[2048,512]{1,0:T(8,128)(2,1)}, u32[]{:S(2)}, u32[]{:S(2)}) collective-permute-start(bf16[2048,512]{1,0:T(8,128)(2,1)S(1)} %copy-done.1), channel_id=1, source_target_pairs={{10,8},{11,9},{20,22},{21,23}} | collective-permute-start | bytes 6291464 | tf_op jit(solution)/shard_map/ppermute | solution.py:29
  179.2 9.6 %shard_map.34 = f32[2048,512]{1,0:T(8,128)} custom-call(s32[48]{0:T(128)S(1)} %fusion.19.s, bf16[2048,512]{1,0:T(8,128)(2,1)S(1)} %shard_map.29.refs_0_.refs_2_.refs_4_, bf16[2048,512]{1,0:T(8,128)(2,1)S(1)} %copy-done.1, bf16[2048,512]{1,0:T(8,128)(2,1)} %collective-permute-done.10.refs_2_, bf16[2048,512]{1,0:T(8,128)(2,1)} %copy-done.14, ...), custom_call_target="tpu_custom_call" | custom-call | flops 17179869184 | bytes 14680064 | tf_op jit(solution)/shard_map/pallas_call | solution.py:154
  188.8 4.3 %multiply_convert_fusion = f16[2048,512]{1,0:T(8,128)(2,1)} fusion(f32[2048,512]{1,0:T(8,128)} %shard_map.34), kind=kLoop, calls=%fused_computation | loop fusion | flops 2097152 | bytes 6291456 | tf_op jit(solution)/shard_map/convert_element_type | solution.py:330
  193.1 2.0 collective-permute-start.27
  195.1 18.3 %collective-permute-done.25 = f16[2048,512]{1,0:T(8,128)(2,1)} collective-permute-done((f16[2048,512]{1,0:T(8,128)(2,1)}, f16[2048,512]{1,0:T(8,128)(2,1)}, u32[]{:S(2)}, u32[]{:S(2)}) %collective-permute-start.25) | collective-permute-done | bytes 2097184 | tf_op jit(solution)/shard_map/ppermute | solution.py:29
  213.4 4.2 %fusion.23 = (f16[1024,512]{1,0:T(8,128)(2,1)}, f32[1024,512]{1,0:T(8,128)}) fusion(f16[2048,512]{1,0:T(8,128)(2,1)} %collective-permute-done.25, f16[2048,512]{1,0:T(8,128)(2,1)S(1)} %collective-permute-done.24, f16[2048,512]{1,0:T(8,128)(2,1)S(1)} %copy-done.10, pred[]{:T(512)S(6)} %and.47, f32[2048,512]{1,0:T(8,128)S(1)} %copy-done.3, ...), kind=kLoop, calls=%fused_computation.47 | loop fusion | flops 6291456 | bytes 17825796 | tf_op jit(solution)/shard_map/convert_element_type | solution.py:383
  217.6 9.1 %shard_map.35 = f32[2048,512]{1,0:T(8,128)} custom-call(s32[48]{0:T(128)S(1)} %fusion.19.s, bf16[2048,512]{1,0:T(8,128)(2,1)S(1)} %shard_map.29.refs_0_.refs_2_.refs_4_, bf16[2048,512]{1,0:T(8,128)(2,1)S(1)} %copy-done.1, bf16[2048,512]{1,0:T(8,128)(2,1)} %collective-permute-done.10.refs_2_, bf16[2048,512]{1,0:T(8,128)(2,1)} %copy-done.14, ...), custom_call_target="tpu_custom_call" | custom-call | flops 17179869184 | bytes 14680064 | tf_op jit(solution)/shard_map/pallas_call | solution.py:154
  226.8 4.7 %fusion.21 = (f16[1024,512]{1,0:T(8,128)(2,1)}, f32[1024,512]{1,0:T(8,128)S(1)}) fusion(f16[2048,512]{1,0:T(8,128)(2,1)} %collective-permute-done.27, pred[]{:T(512)S(6)} %and.46, f16[2048,512]{1,0:T(8,128)(2,1)} %collective-permute-done.25, f16[2048,512]{1,0:T(8,128)(2,1)S(1)} %collective-permute-done.24, pred[]{:T(512)S(6)} %and.47, ...), kind=kLoop, calls=%fused_computation.46 | loop fusion | flops 5767168 | bytes 15728645 | tf_op jit(solution)/shard_map/convert_element_type | solution.py:383
  231.5 1.5 select_convert_fusion
  233.0 2.1 collective-permute-start.28
  235.2 3.1 %collective-permute-start.29 = (f16[1024,512]{1,0:T(8,128)(2,1)}, f16[1024,512]{1,0:T(8,128)(2,1)}, u32[]{:S(2)}, u32[]{:S(2)}) collective-permute-start(f16[1024,512]{1,0:T(8,128)(2,1)} %get-tuple-element.35), channel_id=1, source_target_pairs={{0,1},{1,0},{2,3},{3,2},{4,5},{5,4},{8,9},{9,8},{10,11},{11,10},{1... | collective-permute-start | bytes 3145736 | tf_op jit(solution)/shard_map/ppermute | solution.py:29
  239.1 7.5 %fusion.11 = f32[1024,2048]{1,0:T(8,128)} fusion(f32[1024,2048]{1,0:T(8,128)} %broadcast_in_dim.3, s32[]{:T(128)S(6)} %select_n.195, f32[2048,512]{1,0:T(8,128)} %shard_map.30, f32[2048,512]{1,0:T(8,128)} %shard_map.33, f32[2048,512]{1,0:T(8,128)} %shard_map.34, f32[2048,512]{1,0:T(8,128)} %shard_map.31, f16[2048,512]{1,0:T(8,128)(2,1)} %copy-done.12, ...), kind=kLoop, calls=%fused_computation.19 | loop fusion | flops 5767168 | bytes 14680073 | tf_op jit(solution)/shard_map/dynamic_update_slice | solution.py:401
  246.6 8.2 %collective-permute-done.28 = f16[1024,512]{1,0:T(8,128)(2,1)S(1)} collective-permute-done((f16[1024,512]{1,0:T(8,128)(2,1)}, f16[1024,512]{1,0:T(8,128)(2,1)S(1)}, u32[]{:S(2)}, u32[]{:S(2)}) %collective-permute-start.28) | collective-permute-done | bytes 1048608 | tf_op jit(solution)/shard_map/ppermute | solution.py:29
  254.7 11.3 %collective-permute-done.29 = f16[1024,512]{1,0:T(8,128)(2,1)} collective-permute-done((f16[1024,512]{1,0:T(8,128)(2,1)}, f16[1024,512]{1,0:T(8,128)(2,1)}, u32[]{:S(2)}, u32[]{:S(2)}) %collective-permute-start.29) | collective-permute-done | bytes 1048608 | tf_op jit(solution)/shard_map/ppermute | solution.py:29
  266.1 2.9 %multiply_dynamic-update-slice_fusion.1 = f32[1024,2048]{1,0:T(8,128)} fusion(f32[1024,2048]{1,0:T(8,128)} %fusion.11, s32[]{:T(128)S(6)} %select_n.214, f16[1024,512]{1,0:T(8,128)(2,1)S(1)} %collective-permute-done.28, f16[1024,512]{1,0:T(8,128)(2,1)} %collective-permute-done.29, pred[]{:T(512)S(6)} %and.46), kind=kLoop, calls=%fused_computation.21 | loop fusion | flops 1572864 | bytes 4194309 | tf_op jit(solution)/shard_map/dynamic_update_slice | solution.py:402
  269.0 4.0 %fusion.4 = f32[1024,2048]{1,0:T(8,128)} fusion(f32[1024,2048]{1,0:T(8,128)} %multiply_dynamic-update-slice_fusion.1, s32[]{:T(128)S(6)} %select_n.221, f32[2048,512]{1,0:T(8,128)S(1)} %copy-done.11, f32[2048,512]{1,0:T(8,128)S(1)} %copy-done.5, f32[2048,512]{1,0:T(8,128)S(1)} %copy-done.4, f16[2048,512]{1,0:T(8,128)(2,1)} %collective-permute-done.27, ...), kind=kLoop, calls=%fused_computation.10 | loop fusion | flops 5242880 | bytes 12582921 | tf_op jit(solution)/shard_map/dynamic_update_slice | solution.py:401
  273.0 1.6 multiply_dynamic-update-slice_fusion
  (82 shorter events, 22.3 us)
Async XLA Ops:
  0.0 17.1 %collective-permute-start.7 = (s32[1024,1024]{1,0:T(8,128)}, s32[1024,1024]{1,0:T(8,128)}, u32[]{:S(2)}, u32[]{:S(2)}) collective-permute-start(s32[1024,1024]{1,0:T(8,128)} %near_ref.3), channel_id=1, source_target_pairs={{0,8},{1,9},{2,10},{3,11},{4,12},{5,13},{6,14},{7,15},{8,0},{9,1},... | collective-permute-start | bytes 12582920 | tf_op jit(solution)/shard_map/ppermute | solution.py:29
  3.2 4.7 %collective-permute-start = (s32[2048]{0:T(1024)S(1)}, s32[2048]{0:T(1024)S(1)}, u32[]{:S(2)}, u32[]{:S(2)}) collective-permute-start(s32[2048]{0:T(1024)S(1)} %pad_add_fusion.3), channel_id=1, source_target_pairs={{0,8},{1,9},{2,10},{3,11},{4,12},{5,13},{6,14},{7,15},{8,0},{9,1},... | collective-permute-start | bytes 24584 | tf_op jit(solution)/shard_map/ppermute | solution.py:29
  3.3 2.5 collective-permute-start.1
  4.6 3.3 %collective-permute-start.2 = (s32[1024]{0:T(1024)S(1)}, s32[1024]{0:T(1024)S(1)}, u32[]{:S(2)}, u32[]{:S(2)}) collective-permute-start(s32[1024]{0:T(1024)S(1)} %get-tuple-element.31), channel_id=1, source_target_pairs={{0,24},{1,25},{2,26},{3,27},{4,28},{5,29},{6,30},{7,31},{8,16},{9,... | collective-permute-start | bytes 12296 | tf_op jit(solution)/shard_map/ppermute | solution.py:29
  8.0 2.6 collective-permute-start.3
  10.6 2.7 collective-permute-start.4
  10.8 3.7 %collective-permute-start.5 = (s32[4096]{0:T(1024)S(1)}, s32[4096]{0:T(1024)S(1)}, u32[]{:S(2)}, u32[]{:S(2)}) collective-permute-start(s32[4096]{0:T(1024)S(1)} %pad_add_fusion.1), channel_id=1, source_target_pairs={{0,4},{1,5},{2,6},{3,7},{4,0},{5,1},{6,2},{7,3},{8,12},{9,13},{10,... | collective-permute-start | bytes 49160 | tf_op jit(solution)/shard_map/ppermute | solution.py:29
  13.1 2.6 collective-permute-start.6
  25.7 1.3 copy-start
  27.1 43.9 %collective-permute-start.10 = (bf16[2048,512]{1,0:T(8,128)(2,1)S(1)}, bf16[2048,512]{1,0:T(8,128)(2,1)}, u32[]{:S(2)}, u32[]{:S(2)}) collective-permute-start(bf16[2048,512]{1,0:T(8,128)(2,1)S(1)} %shard_map.29.refs_0_.refs_2_.refs_4_), channel_id=1, source_target_pairs={{0,1},{1,0},{2,3},{3,2},{4,5},{5,4},{6,7},{7,6},{8,9},{9,8},{10,11... | collective-permute-start | bytes 6291464 | tf_op jit(solution)/shard_map/ppermute | solution.py:29
  27.3 47.9 %collective-permute-start.12 = (bf16[2048,512]{1,0:T(8,128)(2,1)S(1)}, bf16[2048,512]{1,0:T(8,128)(2,1)}, u32[]{:S(2)}, u32[]{:S(2)}) collective-permute-start(bf16[2048,512]{1,0:T(8,128)(2,1)S(1)} %shard_map.29.refs_0_.refs_2_.refs_4_), channel_id=1, source_target_pairs={{4,2},{5,3},{10,8},{11,9},{14,12},{15,13},{20,18},{21,19},{26,24},... | collective-permute-start | bytes 6291464 | tf_op jit(solution)/shard_map/ppermute | solution.py:29
  33.6 42.9 %collective-permute-start.14 = (bf16[2048,512]{1,0:T(8,128)(2,1)S(1)}, bf16[2048,512]{1,0:T(8,128)(2,1)}, u32[]{:S(2)}, u32[]{:S(2)}) collective-permute-start(bf16[2048,512]{1,0:T(8,128)(2,1)S(1)} %shard_map.29.refs_0_.refs_2_.refs_4_), channel_id=1, source_target_pairs={{0,2},{1,3},{4,6},{5,7},{10,12},{11,13},{16,18},{17,19},{20,22},{2... | collective-permute-start | bytes 6291464 | tf_op jit(solution)/shard_map/ppermute | solution.py:29
  37.6 53.1 %collective-permute-start.8 = (bf16[2048,512]{1,0:T(8,128)(2,1)}, bf16[2048,512]{1,0:T(8,128)(2,1)}, u32[]{:S(2)}, u32[]{:S(2)}) collective-permute-start(bf16[2048,512]{1,0:T(8,128)(2,1)} %copy-done), channel_id=1, source_target_pairs={{4,2},{5,3},{14,12},{15,13},{20,18},{21,19},{26,24},{27,25},{30,28... | collective-permute-start | bytes 6291464 | tf_op jit(solution)/shard_map/ppermute | solution.py:29
  39.6 52.4 %collective-permute-start.9 = (bf16[2048,512]{1,0:T(8,128)(2,1)}, bf16[2048,512]{1,0:T(8,128)(2,1)}, u32[]{:S(2)}, u32[]{:S(2)}) collective-permute-start(bf16[2048,512]{1,0:T(8,128)(2,1)} %copy-done), channel_id=1, source_target_pairs={{0,2},{1,3},{4,6},{5,7},{10,12},{11,13},{16,18},{17,19},{26,28},{2... | collective-permute-start | bytes 6291464 | tf_op jit(solution)/shard_map/ppermute | solution.py:29
  71.0 26.7 %collective-permute-start.11 = (bf16[2048,512]{1,0:T(8,128)(2,1)}, bf16[2048,512]{1,0:T(8,128)(2,1)S(1)}, u32[]{:S(2)}, u32[]{:S(2)}) collective-permute-start(bf16[2048,512]{1,0:T(8,128)(2,1)} %collective-permute-done.10.refs_2_), channel_id=1, source_target_pairs={{0,8},{1,9},{2,10},{3,11},{4,12},{5,13},{6,14},{7,15},{8,0},{9,1},... | collective-permute-start | bytes 6291464 | tf_op jit(solution)/shard_map/ppermute | solution.py:29
  75.2 27.9 %collective-permute-start.13 = (bf16[2048,512]{1,0:T(8,128)(2,1)}, bf16[2048,512]{1,0:T(8,128)(2,1)}, u32[]{:S(2)}, u32[]{:S(2)}) collective-permute-start(bf16[2048,512]{1,0:T(8,128)(2,1)} %collective-permute-done.12.refs_7_.refs_11_), channel_id=1, source_target_pairs={{2,0},{3,1},{12,10},{13,11},{18,16},{19,17},{28,26},{29,27}} | collective-permute-start | bytes 6291464 | tf_op jit(solution)/shard_map/ppermute | solution.py:29
  76.5 26.6 %collective-permute-start.15 = (bf16[2048,512]{1,0:T(8,128)(2,1)}, bf16[2048,512]{1,0:T(8,128)(2,1)}, u32[]{:S(2)}, u32[]{:S(2)}) collective-permute-start(bf16[2048,512]{1,0:T(8,128)(2,1)} %collective-permute-done.14.refs_8_.refs_6_), channel_id=1, source_target_pairs={{2,4},{3,5},{12,14},{13,15},{18,20},{19,21},{28,30},{29,31}} | collective-permute-start | bytes 6291464 | tf_op jit(solution)/shard_map/ppermute | solution.py:29
  78.5 1.6 copy-start.1
  90.7 29.8 %collective-permute-start.16 = (f16[2048,512]{1,0:T(8,128)(2,1)S(1)}, f16[2048,512]{1,0:T(8,128)(2,1)S(1)}, u32[]{:S(2)}, u32[]{:S(2)}) collective-permute-start(f16[2048,512]{1,0:T(8,128)(2,1)S(1)} %multiply_convert_fusion.4), channel_id=1, source_target_pairs={{4,20},{5,21},{14,30},{15,31},{16,0},{17,1},{26,10},{27,11}} | collective-permute-start | bytes 6291464 | tf_op jit(solution)/shard_map/ppermute | solution.py:29
  96.4 29.4 %collective-permute-start.17 = (bf16[2048,512]{1,0:T(8,128)(2,1)}, bf16[2048,512]{1,0:T(8,128)(2,1)}, u32[]{:S(2)}, u32[]{:S(2)}) collective-permute-start(bf16[2048,512]{1,0:T(8,128)(2,1)} %collective-permute-done.8.refs_7_.refs_9_), channel_id=1, source_target_pairs={{2,0},{3,1},{12,10},{13,11},{18,16},{19,17},{28,26},{29,27}} | collective-permute-start | bytes 6291464 | tf_op jit(solution)/shard_map/ppermute | solution.py:29
  97.7 5.4 %copy-start.14 = (bf16[2048,512]{1,0:T(8,128)(2,1)}, bf16[2048,512]{1,0:T(8,128)(2,1)S(1)}, u32[]{:S(2)}) copy-start(bf16[2048,512]{1,0:T(8,128)(2,1)S(1)} %collective-permute-done.11.refs_3_) | copy-start | bytes 6291460
  97.7 28.0 %collective-permute-start.18 = (bf16[2048,512]{1,0:T(8,128)(2,1)}, bf16[2048,512]{1,0:T(8,128)(2,1)}, u32[]{:S(2)}, u32[]{:S(2)}) collective-permute-start(bf16[2048,512]{1,0:T(8,128)(2,1)} %collective-permute-done.9.refs_8_.refs_4_), channel_id=1, source_target_pairs={{2,4},{3,5},{12,14},{13,15},{18,20},{19,21},{28,30},{29,31}} | collective-permute-start | bytes 6291464 | tf_op jit(solution)/shard_map/ppermute | solution.py:29
  115.1 52.8 %collective-permute-start.21 = (f16[2048,512]{1,0:T(8,128)(2,1)S(1)}, f16[2048,512]{1,0:T(8,128)(2,1)S(1)}, u32[]{:S(2)}, u32[]{:S(2)}) collective-permute-start(f16[2048,512]{1,0:T(8,128)(2,1)S(1)} %multiply_convert_fusion.3), channel_id=1, source_target_pairs={{0,16},{1,17},{2,18},{3,19},{4,20},{5,21},{6,22},{7,23},{12,28},{1... | collective-permute-start | bytes 6291464 | tf_op jit(solution)/shard_map/ppermute | solution.py:29
  116.4 32.5 %collective-permute-start.19 = (bf16[2048,512]{1,0:T(8,128)(2,1)}, bf16[2048,512]{1,0:T(8,128)(2,1)}, u32[]{:S(2)}, u32[]{:S(2)}) collective-permute-start(bf16[2048,512]{1,0:T(8,128)(2,1)} %collective-permute-done.13.refs_6_.refs_9_.refs_10_), channel_id=1, source_target_pairs={{10,8},{11,9},{26,24},{27,25}} | collective-permute-start | bytes 6291464 | tf_op jit(solution)/shard_map/ppermute | solution.py:29
  120.5 14.9 %copy-start.12 = (f16[2048,512]{1,0:T(8,128)(2,1)}, f16[2048,512]{1,0:T(8,128)(2,1)S(1)}, u32[]{:S(2)}) copy-start(f16[2048,512]{1,0:T(8,128)(2,1)S(1)} %collective-permute-done.16) | copy-start | bytes 6291460
  120.5 29.2 %collective-permute-start.20 = (bf16[2048,512]{1,0:T(8,128)(2,1)}, bf16[2048,512]{1,0:T(8,128)(2,1)}, u32[]{:S(2)}, u32[]{:S(2)}) collective-permute-start(bf16[2048,512]{1,0:T(8,128)(2,1)} %collective-permute-done.15.refs_9_.refs_10_.refs_7_), channel_id=1, source_target_pairs={{4,6},{5,7},{20,22},{21,23}} | collective-permute-start | bytes 6291464 | tf_op jit(solution)/shard_map/ppermute | solution.py:29
  139.5 55.6 %collective-permute-start.24 = (f16[2048,512]{1,0:T(8,128)(2,1)}, f16[2048,512]{1,0:T(8,128)(2,1)S(1)}, u32[]{:S(2)}, u32[]{:S(2)}) collective-permute-start(f16[2048,512]{1,0:T(8,128)(2,1)} %multiply_convert_fusion.2), channel_id=1, source_target_pairs={{0,16},{1,17},{2,18},{3,19},{6,22},{7,23},{10,26},{11,27},{12,28},... | collective-permute-start | bytes 6291464 | tf_op jit(solution)/shard_map/ppermute | solution.py:29
  140.9 30.5 %collective-permute-start.22 = (bf16[2048,512]{1,0:T(8,128)(2,1)}, bf16[2048,512]{1,0:T(8,128)(2,1)S(1)}, u32[]{:S(2)}, u32[]{:S(2)}) collective-permute-start(bf16[2048,512]{1,0:T(8,128)(2,1)} %collective-permute-done.17.refs_6_.refs_9_.refs_8_), channel_id=1, source_target_pairs={{10,8},{11,9},{26,24},{27,25}} | collective-permute-start | bytes 6291464 | tf_op jit(solution)/shard_map/ppermute | solution.py:29
  148.9 22.5 %collective-permute-start.23 = (bf16[2048,512]{1,0:T(8,128)(2,1)}, bf16[2048,512]{1,0:T(8,128)(2,1)S(1)}, u32[]{:S(2)}, u32[]{:S(2)}) collective-permute-start(bf16[2048,512]{1,0:T(8,128)(2,1)} %collective-permute-done.18.refs_11_.refs_12_.refs_5_), channel_id=1, source_target_pairs={{4,6},{5,7},{20,22},{21,23}} | collective-permute-start | bytes 6291464 | tf_op jit(solution)/shard_map/ppermute | solution.py:29
  163.4 50.0 %collective-permute-start.25 = (f16[2048,512]{1,0:T(8,128)(2,1)}, f16[2048,512]{1,0:T(8,128)(2,1)}, u32[]{:S(2)}, u32[]{:S(2)}) collective-permute-start(f16[2048,512]{1,0:T(8,128)(2,1)} %multiply_convert_fusion.1), channel_id=1, source_target_pairs={{8,24},{9,25},{10,26},{11,27},{20,4},{21,5},{22,6},{23,7}} | collective-permute-start | bytes 6291464 | tf_op jit(solution)/shard_map/ppermute | solution.py:29
  167.9 11.3 %copy-start.9 = (f16[2048,512]{1,0:T(8,128)(2,1)}, f16[2048,512]{1,0:T(8,128)(2,1)S(1)}, u32[]{:S(2)}) copy-start(f16[2048,512]{1,0:T(8,128)(2,1)S(1)} %collective-permute-done.21) | copy-start | bytes 6291460
  171.4 1.4 copy-start.15
  172.8 1.4 copy-start.16
  174.1 43.5 %collective-permute-start.26 = (bf16[2048,512]{1,0:T(8,128)(2,1)S(1)}, bf16[2048,512]{1,0:T(8,128)(2,1)}, u32[]{:S(2)}, u32[]{:S(2)}) collective-permute-start(bf16[2048,512]{1,0:T(8,128)(2,1)S(1)} %copy-done.1), channel_id=1, source_target_pairs={{10,8},{11,9},{20,22},{21,23}} | collective-permute-start | bytes 6291464 | tf_op jit(solution)/shard_map/ppermute | solution.py:29
  179.2 34.2 %copy-start.3 = (f32[2048,512]{1,0:T(8,128)S(1)}, f32[2048,512]{1,0:T(8,128)}, u32[]{:S(2)}) copy-start(f32[2048,512]{1,0:T(8,128)} %shard_map.33) | copy-start | bytes 12582916
  188.8 24.6 %copy-start.2 = (f32[2048,512]{1,0:T(8,128)S(1)}, f32[2048,512]{1,0:T(8,128)}, u32[]{:S(2)}) copy-start(f32[2048,512]{1,0:T(8,128)} %shard_map.31) | copy-start | bytes 12582916
  188.8 24.6 %copy-start.10 = (f16[2048,512]{1,0:T(8,128)(2,1)S(1)}, f16[2048,512]{1,0:T(8,128)(2,1)}, u32[]{:S(2)}) copy-start(f16[2048,512]{1,0:T(8,128)(2,1)} %copy-done.9) | copy-start | bytes 6291460
  193.1 33.7 %collective-permute-start.27 = (f16[2048,512]{1,0:T(8,128)(2,1)}, f16[2048,512]{1,0:T(8,128)(2,1)}, u32[]{:S(2)}, u32[]{:S(2)}) collective-permute-start(f16[2048,512]{1,0:T(8,128)(2,1)} %multiply_convert_fusion), channel_id=1, source_target_pairs={{8,24},{9,25},{22,6},{23,7}} | collective-permute-start | bytes 6291464 | tf_op jit(solution)/shard_map/ppermute | solution.py:29
  195.1 31.7 %copy-start.6 = (f16[2048,512]{1,0:T(8,128)(2,1)}, f16[2048,512]{1,0:T(8,128)(2,1)S(1)}, u32[]{:S(2)}) copy-start(f16[2048,512]{1,0:T(8,128)(2,1)S(1)} %collective-permute-done.24) | copy-start | bytes 6291460
  226.7 4.7 %copy-start.8 = (f32[1024,512]{1,0:T(8,128)S(1)}, f32[1024,512]{1,0:T(8,128)}, u32[]{:S(2)}) copy-start(f32[1024,512]{1,0:T(8,128)} %get-tuple-element.36) | copy-start | bytes 6291460
  233.0 21.7 %collective-permute-start.28 = (f16[1024,512]{1,0:T(8,128)(2,1)}, f16[1024,512]{1,0:T(8,128)(2,1)S(1)}, u32[]{:S(2)}, u32[]{:S(2)}) collective-permute-start(f16[1024,512]{1,0:T(8,128)(2,1)} %select_convert_fusion), channel_id=1, source_target_pairs={{0,1},{1,0},{2,3},{3,2},{4,5},{5,4},{6,7},{7,6},{10,11},{11,10},{1... | collective-permute-start | bytes 3145736 | tf_op jit(solution)/shard_map/ppermute | solution.py:29
  235.2 30.9 %collective-permute-start.29 = (f16[1024,512]{1,0:T(8,128)(2,1)}, f16[1024,512]{1,0:T(8,128)(2,1)}, u32[]{:S(2)}, u32[]{:S(2)}) collective-permute-start(f16[1024,512]{1,0:T(8,128)(2,1)} %get-tuple-element.35), channel_id=1, source_target_pairs={{0,1},{1,0},{2,3},{3,2},{4,5},{5,4},{8,9},{9,8},{10,11},{11,10},{1... | collective-permute-start | bytes 3145736 | tf_op jit(solution)/shard_map/ppermute | solution.py:29
  238.3 34.7 %collective-permute-start.30 = (f16[1024,512]{1,0:T(8,128)(2,1)}, f16[1024,512]{1,0:T(8,128)(2,1)S(1)}, u32[]{:S(2)}, u32[]{:S(2)}) collective-permute-start(f16[1024,512]{1,0:T(8,128)(2,1)} %get-tuple-element.33), channel_id=1, source_target_pairs={{6,7},{7,6},{8,9},{9,8},{22,23},{23,22},{24,25},{25,24}} | collective-permute-start | bytes 3145736 | tf_op jit(solution)/shard_map/ppermute | solution.py:29
  239.1 29.9 %copy-start.5 = (f32[2048,512]{1,0:T(8,128)S(1)}, f32[2048,512]{1,0:T(8,128)}, u32[]{:S(2)}) copy-start(f32[2048,512]{1,0:T(8,128)} %shard_map.30) | copy-start | bytes 12582916
  239.1 29.9 %copy-start.7 = (f16[2048,512]{1,0:T(8,128)(2,1)S(1)}, f16[2048,512]{1,0:T(8,128)(2,1)}, u32[]{:S(2)}) copy-start(f16[2048,512]{1,0:T(8,128)(2,1)} %copy-done.6) | copy-start | bytes 6291460
  239.1 29.9 %copy-start.11 = (f32[2048,512]{1,0:T(8,128)S(1)}, f32[2048,512]{1,0:T(8,128)}, u32[]{:S(2)}) copy-start(f32[2048,512]{1,0:T(8,128)} %shard_map.35) | copy-start | bytes 12582916
  239.1 29.9 %copy-start.13 = (f16[2048,512]{1,0:T(8,128)(2,1)S(1)}, f16[2048,512]{1,0:T(8,128)(2,1)}, u32[]{:S(2)}) copy-start(f16[2048,512]{1,0:T(8,128)(2,1)} %copy-done.12) | copy-start | bytes 6291460
  246.6 22.4 %copy-start.4 = (f32[2048,512]{1,0:T(8,128)S(1)}, f32[2048,512]{1,0:T(8,128)}, u32[]{:S(2)}) copy-start(f32[2048,512]{1,0:T(8,128)} %shard_map.34) | copy-start | bytes 12582916

commit v3 on v2

--- a/solution.py
+++ b/solution.py
@@ -35,6 +35,7 @@
 
 VMEM = 48 * 2**20
 SLOTS = 6
+LIGHT = pl.CostEstimate(flops=0, bytes_accessed=0, transcendentals=0)
 
 
 def residuals_of(near, far, depths, shares, part, parts, ceiling):
@@ -86,9 +87,10 @@
     )(jnp.reshape(part, (1,)).astype(jnp.int32), depths.reshape(1, -1), shares.reshape(1, -1), near, far)
 
 
-def products_of(plan, slot, lefts, turned, rights):
+def products_of(plan, slot, lefts, turned, rights, first=0, blocks=4):
     rows, width = rights[0].shape
-    blocks, upper = 4, rows // 2
+    upper = rows // 2
+    base = (slot * 4 + first) * 2
     n_left = len(lefts)
 
     def kernel(s, *refs):
@@ -97,10 +99,10 @@
         i = pl.program_id(0)
 
         def left_at(block):
-            return s[slot * 2 * blocks + 2 * block]
+            return s[base + 2 * block]
 
         def right_at(block):
-            return s[slot * 2 * blocks + 2 * block + 1]
+            return s[base + 2 * block + 1]
 
         def left_copies(n, to):
             for part in range(2):
@@ -195,8 +197,6 @@
             return "own rows", not near
         if not near:
             return [None, ("other rows", True), None, ((far, 0), False), ((far, 1), False), None][slot]
-        if is_end(z):
-            return [None, ((far, 0), True), ((far, 1), True), ("other rows", False), None, None][slot]
         return [None, ("other rows", False), ((far, 0), True), ((far, 1), True), None, None][slot]
     if not is_end(z):
         return [None, ((first, 0), True), ((first, 1), True), ((-first, 0), False), ((-first, 1), False), None][slot]
@@ -214,7 +214,7 @@
 
 
 def rights_of(slot):
-    names, table = [("own", 0), ("own", 1)] if slot < 4 else [], np.zeros((2, 2, 4, 4, 2), np.int32)
+    names, table = [("own", 0), ("own", 1)] if slot < 2 else [], np.zeros((2, 2, 4, 4, 2), np.int32)
     for x in range(2):
         for c in range(2):
             for z in range(4):
@@ -330,76 +330,103 @@
             narrow_products.append((product * scale).astype(jnp.float16))
             received.append(cross(narrow_products[-1], remote(slot)))
 
+    plan, out = lax.optimization_barrier((plan, out))
     work(0, [own_a, own_b], plan)
     d2a, u2a = send(d1a, down(2)), send(u1a, up(2))
-    d1b, u1b, out, _ = lax.optimization_barrier((d1b, u1b, out, narrow_products[0]))
+    d1b, u1b, _ = lax.optimization_barrier((d1b, u1b, narrow_products[0]))
+    across, d1b, u1b, _ = lax.optimization_barrier((across, d1b, u1b, narrow_products[0]))
     held[1, 1], held[-1, 1], held[2, 0], held[-2, 0] = d1b, u1b, d2a, u2a
     d2b, u2b = send(d1b, down(2)), send(u1b, up(2))
     held[2, 1], held[-2, 1] = d2b, u2b
     lefts = [own_a, own_b, across, swap_core(across)]
-    plan, out = lax.optimization_barrier((plan, out))
-    work(1, lefts, plan)
-    d2a, u2a, _ = lax.optimization_barrier((d2a, u2a, narrow_products[1]))
     d3a, u3a = send(d2a, down(3)), send(u2a, up(3))
+    work(1, lefts, after(plan, received[0], d2a, u2a))
+    d2b, u2b, _ = lax.optimization_barrier((d2b, u2b, narrow_products[1]))
     d3b, u3b = send(d2b, down(3)), send(u2b, up(3))
-    work(2, lefts, after(plan, narrow_products[1], received[0]))
+    work(2, lefts, after(plan, narrow_products[1]))
     held[3, 0], held[-3, 0], held[3, 1], held[-3, 1] = d3a, u3a, d3b, u3b
     work(3, lefts, after(plan, narrow_products[2]))
     held["late", 0] = send(after(own_b, d3b, u3b), last)
-    work(4, lefts, after(plan, narrow_products[3], received[1]))
 
     wide = lambda value: value.astype(jnp.float32)
-    low_rows, high_rows = slice(0, genes_here), slice(genes_here, None)
-
-    def own_rows(half):
-        return low_rows
-
-    def mix(choices):
-        value = choices[-1][1]
+    own_rows, other_rows = slice(0, genes_here), slice(genes_here, None)
+    near_even, far_even = even & near_x, even & jnp.logical_not(near_x)
+    near_end, far_end = odd_end & near_x, odd_end & jnp.logical_not(near_x)
+
+    def total(mine, theirs, rows):
+        return products[mine][rows] * scale + wide(received[theirs][rows])
+
+    def mix(*choices):
+        value = choices[-1]
         for condition, other in reversed(choices[:-1]):
             value = jnp.where(condition, other, value)
         return value
 
-    near_even, far_even = even & near_x, even & jnp.logical_not(near_x)
-    near_end = odd_end & near_x
-    far_end = odd_end & jnp.logical_not(near_x)
-
-    def sums(other, half):
-        rows = high_rows if other else low_rows
-        stacked = high_rows if half else low_rows
-        p, r = products, received
-        own_block = mix([(end, p[3][stacked]), (None, p[1][stacked])]) if other else p[0][stacked]
-        own_received = r[1][stacked] if other else r[0][stacked]
-        if half == 0:
-            mine = [(near_even, own_block), (near_end, p[1][rows]), (far_end, p[4][rows]), (None, p[3][rows])]
-            far_received = mix([(end, r[1][rows]), (None, r[2][rows])])
-            theirs = [(near_even, own_received), (far_even, far_received), (far_end, r[3][rows]), (None, r[1][rows])]
-        else:
-            mine = [(near_even, own_block), (odd_end, p[5][rows]), (None, p[4][rows])]
-            far_received = mix([(end, r[2][rows]), (None, r[3][rows])])
-            theirs = [(near_even, own_received), (far_even, far_received), (far_end, r[4][rows]), (None, r[2][rows])]
-        return mix(mine) * scale + wide(mix(theirs))
-
-    narrow = lambda value: value.astype(jnp.float16)
+    def swap_some(value, devices):
+        value = value.astype(jnp.float16)
+        return value, swap_y(value, devices)
 
     def is_far_end(x, c, z):
         return is_odd_end(c, z) and not is_near(x, z)
 
-    other_a = sums(True, 0)
-    got_first = swap_y(narrow(other_a), lambda x, c, z: not is_far_end(x, c, z))
-    work(5, lefts, after(plan, narrow_products[4], received[2], narrow(other_a)))
-    other_b = sums(True, 1)
-    middle = jnp.where(odd_end, other_a, other_b)
-    got_middle = swap_y(narrow(middle), lambda x, c, z: not is_odd_end(c, z) or is_far_end(x, c, z))
-    got_last = swap_y(narrow(other_b), lambda x, c, z: is_odd_end(c, z))
-    got_a = jnp.where(far_end, got_middle, got_first)
-    got_b = jnp.where(odd_end, got_last, got_middle)
-
+    def is_far_even(x, c, z):
+        return is_even(c, z) and not is_near(x, z)
+
+    sent_a, got_a = swap_some(
+        mix(
+            (near_even, total(1, 1, own_rows)),
+            (near_end, total(1, 1, other_rows)),
+            total(3, 1, other_rows),
+        ),
+        lambda x, c, z: not is_far_end(x, c, z) and not is_far_even(x, c, z),
+    )
+    work(4, lefts, after(plan, narrow_products[3], sent_a))
+    sent_b, got_b = swap_some(
+        mix(
+            (near_even, total(1, 1, other_rows)),
+            (far_even, total(3, 2, other_rows)),
+            total(4, 2, other_rows),
+        ),
+        lambda x, c, z: not is_odd_end(c, z),
+    )
+    plan = after(plan, narrow_products[4], sent_b)
+    rights = [held[name] for name in jobs[5][0]]
+    turned = [False, False, False, True]
+    last_other = products_of(plan, 5, lefts, turned, rights, 2, 2)
+    last_own = products_of(after(plan, last_other), 5, lefts, turned, rights, 0, 2)
+    received[3] = after(received[3], last_own)
+    _, got_c = swap_some(
+        total(4, 3, other_rows), lambda x, c, z: is_far_end(x, c, z) or is_far_even(x, c, z)
+    )
+
+    def last_total(product, rows):
+        return product * scale + wide(jnp.where(near_x, received[2][rows], received[4][rows]))
+
+    _, got_d = swap_some(last_total(last_other, other_rows), lambda x, c, z: is_odd_end(c, z))
+
+    own_first = mix(
+        (near_even, total(0, 0, own_rows)),
+        (far_even, total(3, 2, own_rows)),
+        (near_end, total(1, 1, own_rows)),
+        (far_end, total(4, 3, own_rows)),
+        total(3, 1, own_rows),
+    )
+    own_second = mix(
+        (near_even, total(0, 0, other_rows)),
+        (far_even, total(4, 3, own_rows)),
+        (odd_end, last_total(last_own, own_rows)),
+        total(4, 2, own_rows),
+    )
+    got_first = wide(mix((far_even, got_b), (far_end, got_c), got_a))
+    got_second = wide(mix((far_even, got_c), (odd_end, got_d), got_b))
     begin, begin_other = y * genes_here, (1 - y) * genes_here
-    for half_of, got in ((0, got_a), (1, got_b)):
-        place = (half_of ^ c) * half
-        out = lax.dynamic_update_slice(out, sums(False, half_of) * (1.0 / UNIT), (0, begin + place))
-        out = lax.dynamic_update_slice(out, wide(got) * (1.0 / UNIT), (0, begin_other + place))
+    for value, place in (
+        (own_first, begin + c * half),
+        (got_first, begin_other + c * half),
+        (own_second, begin + (1 - c) * half),
+        (got_second, begin_other + (1 - c) * half),
+    ):
+        out = lax.dynamic_update_slice(out, value * (1.0 / UNIT), (0, place))
     return out
 
 

time: 277 us -> 274 us (0.989)
  the two profiles are of different devices: /device:TPU:13 before, /device:TPU:7 now
where the time goes in v3:
time: 274 us; the launch traced here: 273 us
  waiting for transfers between devices  105 us (38%)
  Pallas kernels  65.7 us (24%)
  other arithmetic  47.7 us (17%)
  starting transfers between devices  44.6 us (16%)
  local copies, waits for them, and re-layouts  9.37 us (3%)
    ppermute x32, waiting for transfers between devices, send(): return lax.ppermute(value, AXES, pairs_of(move))  105 us
    pallas_call x7, Pallas kernels, products_of(): pl.pallas_call(kernel, grid_spec=pltpu.PrefetchScalarGridSpec(num_scalar_...  57.1 us
    ppermute x32, starting transfers between devices, send(): return lax.ppermute(value, AXES, pairs_of(move))  44.6 us
    convert_element_type x4, other arithmetic, swap_some(): value = value.astype(jnp.float16)  19.5 us
    convert_element_type x5, other arithmetic, work(): narrow_products.append((product * scale).astype(jnp.float16))  19.4 us
    pallas_call x2, Pallas kernels, residuals_of(): pl.pallas_call(kernel, grid_spec=pltpu.PrefetchScalarGridSpec(num_scalar_...  8.59 us
  transfers between devices with their start and end apart: 32, of which 11 were waited for; matrix products, arithmetic and copies ran while one was open for 16% of the time, Pallas kernels for 22%

profile of v3, /device:TPU:7, one launch (start us, length us, event | category | flops | bytes accessed | tf_op | source)
XLA Modules:
  0.0 273.1 jit_solution(10268888246720911402)
XLA Ops:
  0.7 2.6 fusion.23
  7.7 2.3 collective-permute-done.3
  10.1 3.4 %collective-permute-start.6 = (s32[4096]{0:T(1024)S(1)}, s32[4096]{0:T(1024)S(1)}, u32[]{:S(2)}, u32[]{:S(2)}) collective-permute-start(s32[4096]{0:T(1024)S(1)} %pad_add_fusion.1), channel_id=1, source_target_pairs={{0,6},{1,7},{2,4},{3,5},{4,2},{5,3},{6,0},{7,1},{8,14},{9,15},{10,... | collective-permute-start | bytes 49160 | tf_op jit(solution)/shard_map/ppermute | solution.py:29
  14.6 2.4 collective-permute-done.5
  18.3 4.5 %broadcast_in_dim.3 = f32[1024,2048]{1,0:T(8,128)} broadcast(f32[]{:T(128)S(6)} %mul.89), dimensions={} | broadcast | bytes 8388612 | tf_op jit(solution)/shard_map/broadcast_in_dim | solution.py:321
  23.5 4.3 %shard_map.28.refs_0_.refs_2_.refs_4_ = bf16[2048,512]{1,0:T(8,128)(2,1)S(1)} custom-call(s32[1]{0:T(128)} %bitcast.5.part_ref, f32[1,2048]{1,0:T(1,128)S(1)} %bitcast.10, f32[1,1024]{1,0:T(1,128)S(1)} %bitcast.12, s32[1024,1024]{1,0:T(8,128)} %near_ref.3, s32[1024,1024]{1,0:T(8,128)} %collective-permute-done.7.far_ref), custom_call_target="tpu_custom_call" | custom-call | flops 10485760 | bytes 6291456 | tf_op jit(solution)/shard_map/pallas_call | solution.py:69
  27.8 1.3 collective-permute-start.9
  29.1 2.1 collective-permute-start.11
  31.1 4.3 %shard_map.29.refs_1_.refs_3_.refs_5_ = bf16[2048,512]{1,0:T(8,128)(2,1)S(1)} custom-call(s32[1]{0:T(128)} %bitcast.8.part_ref, f32[1,2048]{1,0:T(1,128)S(1)} %bitcast.11, f32[1,1024]{1,0:T(1,128)S(1)} %bitcast.13, s32[1024,1024]{1,0:T(8,128)} %near_ref.3, s32[1024,1024]{1,0:T(8,128)} %collective-permute-done.7.far_ref), custom_call_target="tpu_custom_call" | custom-call | flops 10485760 | bytes 6291456 | tf_op jit(solution)/shard_map/pallas_call | solution.py:69
  35.5 1.3 collective-permute-start.14
  37.8 7.6 %shard_map.30 = f32[2048,512]{1,0:T(8,128)} custom-call(s32[48]{0:T(128)S(1)} %fusion.22.s, bf16[2048,512]{1,0:T(8,128)(2,1)S(1)} %shard_map.28.refs_0_.refs_2_.refs_4_, bf16[2048,512]{1,0:T(8,128)(2,1)S(1)} %shard_map.29.refs_1_.refs_3_.refs_5_, bf16[2048,512]{1,0:T(8,128)(2,1)S(1)} %shard_map.28.refs_0_.refs_2_.refs_4_, ...), custom_call_target="tpu_custom_call" | custom-call | flops 17179869184 | bytes 14680064 | tf_op jit(solution)/shard_map/pallas_call | solution.py:156
  45.5 4.1 %multiply_convert_fusion.4 = f16[2048,512]{1,0:T(8,128)(2,1)} fusion(f32[2048,512]{1,0:T(8,128)} %shard_map.30), kind=kLoop, calls=%fused_computation.4 | loop fusion | flops 2097152 | bytes 6291456 | tf_op jit(solution)/shard_map/convert_element_type | solution.py:330
  49.5 27.9 %collective-permute-done.14.refs_5_.refs_9_ = bf16[2048,512]{1,0:T(8,128)(2,1)S(1)} collective-permute-done((bf16[2048,512]{1,0:T(8,128)(2,1)S(1)}, bf16[2048,512]{1,0:T(8,128)(2,1)S(1)}, u32[]{:S(2)}, u32[]{:S(2)}) %collective-permute-start.14) | collective-permute-done | bytes 2097184 | tf_op jit(solution)/shard_map/ppermute | solution.py:29
  77.4 2.0 collective-permute-start.8
  79.4 2.0 collective-permute-start.10
  81.4 2.0 collective-permute-start.12
  83.5 2.3 collective-permute-start.16
  86.6 2.0 collective-permute-start.19
  88.6 1.4 collective-permute-done.16.refs_3_
  89.9 1.6 copy-done.1
  91.5 9.6 %shard_map.31 = f32[2048,512]{1,0:T(8,128)} custom-call(s32[48]{0:T(128)S(1)} %fusion.22.s, bf16[2048,512]{1,0:T(8,128)(2,1)S(1)} %shard_map.28.refs_0_.refs_2_.refs_4_, bf16[2048,512]{1,0:T(8,128)(2,1)S(1)} %copy-done.1, bf16[2048,512]{1,0:T(8,128)(2,1)} %collective-permute-done.13.refs_2_, bf16[2048,512]{1,0:T(8,128)(2,1)} %collective-permute-done.16.refs_3_, ...), custom_call_target="tpu_custom_call" | custom-call | flops 17179869184 | bytes 14680064 | tf_op jit(solution)/shard_map/pallas_call | solution.py:156
  101.1 2.8 %multiply_convert_fusion.3 = f16[2048,512]{1,0:T(8,128)(2,1)S(1)} fusion(f32[2048,512]{1,0:T(8,128)} %shard_map.31), kind=kLoop, calls=%fused_computation.3 | loop fusion | flops 2097152 | bytes 6291456 | tf_op jit(solution)/shard_map/convert_element_type | solution.py:330
  103.9 2.1 collective-permute-start.22
  108.3 9.5 %shard_map.32 = f32[2048,512]{1,0:T(8,128)} custom-call(s32[48]{0:T(128)S(1)} %fusion.22.s, bf16[2048,512]{1,0:T(8,128)(2,1)S(1)} %shard_map.28.refs_0_.refs_2_.refs_4_, bf16[2048,512]{1,0:T(8,128)(2,1)S(1)} %copy-done.1, bf16[2048,512]{1,0:T(8,128)(2,1)} %collective-permute-done.13.refs_2_, bf16[2048,512]{1,0:T(8,128)(2,1)} %collective-permute-done.16.refs_3_, ...), custom_call_target="tpu_custom_call" | custom-call | flops 17179869184 | bytes 14680064 | tf_op jit(solution)/shard_map/pallas_call | solution.py:156
  117.8 4.1 %multiply_convert_fusion.2 = f16[2048,512]{1,0:T(8,128)(2,1)} fusion(f32[2048,512]{1,0:T(8,128)} %shard_map.32), kind=kLoop, calls=%fused_computation.2 | loop fusion | flops 2097152 | bytes 6291456 | tf_op jit(solution)/shard_map/convert_element_type | solution.py:330
  121.9 2.6 collective-permute-start.21
  125.8 27.5 %collective-permute-done.18.refs_7_.refs_11_ = bf16[2048,512]{1,0:T(8,128)(2,1)S(1)} collective-permute-done((bf16[2048,512]{1,0:T(8,128)(2,1)}, bf16[2048,512]{1,0:T(8,128)(2,1)S(1)}, u32[]{:S(2)}, u32[]{:S(2)}) %collective-permute-start.18) | collective-permute-done | bytes 2097184 | tf_op jit(solution)/shard_map/ppermute | solution.py:29
  153.3 2.0 collective-permute-start.24
  155.2 1.4 copy-done.13
  156.6 9.3 %shard_map.33 = f32[2048,512]{1,0:T(8,128)} custom-call(s32[48]{0:T(128)S(1)} %fusion.22.s, bf16[2048,512]{1,0:T(8,128)(2,1)S(1)} %shard_map.28.refs_0_.refs_2_.refs_4_, bf16[2048,512]{1,0:T(8,128)(2,1)S(1)} %copy-done.1, bf16[2048,512]{1,0:T(8,128)(2,1)} %collective-permute-done.13.refs_2_, bf16[2048,512]{1,0:T(8,128)(2,1)} %collective-permute-done.16.refs_3_, ...), custom_call_target="tpu_custom_call" | custom-call | flops 17179869184 | bytes 14680064 | tf_op jit(solution)/shard_map/pallas_call | solution.py:156
  165.9 4.3 %multiply_convert_fusion.1 = f16[2048,512]{1,0:T(8,128)(2,1)} fusion(f32[2048,512]{1,0:T(8,128)} %shard_map.33), kind=kLoop, calls=%fused_computation.1 | loop fusion | flops 2097152 | bytes 6291456 | tf_op jit(solution)/shard_map/convert_element_type | solution.py:330
  171.5 4.3 %fusion.13 = f16[1024,512]{1,0:T(8,128)(2,1)} fusion(f32[2048,512]{1,0:T(8,128)} %shard_map.33, f32[2048,512]{1,0:T(8,128)S(1)} %copy-done.6, pred[]{:T(512)S(6)} %and.46, pred[]{:T(512)S(6)} %and.43, f16[2048,512]{1,0:T(8,128)(2,1)S(1)} %collective-permute-done.22), kind=kLoop, calls=%fused_computation.26 | loop fusion | flops 5767168 | bytes 9437186 | tf_op jit(solution)/shard_map/convert_element_type | solution.py:366
  175.8 2.0 collective-permute-start.26
  177.8 9.6 %shard_map.34 = f32[2048,512]{1,0:T(8,128)} custom-call(s32[48]{0:T(128)S(1)} %fusion.22.s, bf16[2048,512]{1,0:T(8,128)(2,1)S(1)} %shard_map.28.refs_0_.refs_2_.refs_4_, bf16[2048,512]{1,0:T(8,128)(2,1)S(1)} %copy-done.1, bf16[2048,512]{1,0:T(8,128)(2,1)} %collective-permute-done.13.refs_2_, bf16[2048,512]{1,0:T(8,128)(2,1)} %collective-permute-done.16.refs_3_, ...), custom_call_target="tpu_custom_call" | custom-call | flops 17179869184 | bytes 14680064 | tf_op jit(solution)/shard_map/pallas_call | solution.py:156
  187.4 4.3 %multiply_convert_fusion = f16[2048,512]{1,0:T(8,128)(2,1)} fusion(f32[2048,512]{1,0:T(8,128)} %shard_map.34), kind=kLoop, calls=%fused_computation | loop fusion | flops 2097152 | bytes 6291456 | tf_op jit(solution)/shard_map/convert_element_type | solution.py:330
  193.0 3.8 %fusion.16 = f16[1024,512]{1,0:T(8,128)(2,1)} fusion(f32[2048,512]{1,0:T(8,128)} %shard_map.33, f32[2048,512]{1,0:T(8,128)S(1)} %copy-done.7, f32[2048,512]{1,0:T(8,128)S(1)} %copy-done.6, pred[]{:T(512)S(6)} %and.44, pred[]{:T(512)S(6)} %and.43, f16[2048,512]{1,0:T(8,128)(2,1)} %collective-permute-done.21, f16[2048,512]{1,0:T(8,128)(2,1)S(1)} %collective-permute-done.22), kind=kLoop, calls=%fused_computation.29 | loop fusion | flops 5767168 | bytes 9437186 | tf_op jit(solution)/shard_map/convert_element_type | solution.py:366
  197.5 1.7 collective-permute-start.29
  199.2 5.7 %shard_map.35 = f32[1024,512]{1,0:T(8,128)S(1)} custom-call(s32[48]{0:T(128)S(1)} %fusion.22.s, bf16[2048,512]{1,0:T(8,128)(2,1)S(1)} %shard_map.28.refs_0_.refs_2_.refs_4_, bf16[2048,512]{1,0:T(8,128)(2,1)} %copy-done, bf16[2048,512]{1,0:T(8,128)(2,1)} %collective-permute-done.13.refs_2_, bf16[2048,512]{1,0:T(8,128)(2,1)} %collective-permute-done.16.refs_3_, ...), custom_call_target="tpu_custom_call" | custom-call | flops 8589934592 | bytes 8388608 | tf_op jit(solution)/shard_map/pallas_call | solution.py:156
  204.9 5.8 %shard_map.36 = f32[1024,512]{1,0:T(8,128)S(1)} custom-call(s32[48]{0:T(128)S(1)} %fusion.22.s, bf16[2048,512]{1,0:T(8,128)(2,1)S(1)} %shard_map.28.refs_0_.refs_2_.refs_4_, bf16[2048,512]{1,0:T(8,128)(2,1)} %copy-done, bf16[2048,512]{1,0:T(8,128)(2,1)} %collective-permute-done.13.refs_2_, bf16[2048,512]{1,0:T(8,128)(2,1)} %collective-permute-done.16.refs_3_, ...), custom_call_target="tpu_custom_call" | custom-call | flops 8589934592 | bytes 8388608 | tf_op jit(solution)/shard_map/pallas_call | solution.py:156
  210.7 2.7 collective-permute-done.25
  213.4 5.6 %add_convert_fusion.1 = (f16[1024,512]{1,0:T(8,128)(2,1)S(1)}, f32[1024,2048]{1,0:T(8,128)}) fusion(f32[2048,512]{1,0:T(8,128)S(1)} %copy-done.7, f16[2048,512]{1,0:T(8,128)(2,1)} %collective-permute-done.25, f32[1024,2048]{1,0:T(8,128)} %broadcast_in_dim.3, s32[]{:T(128)S(6)} %select_n.139, pred[]{:T(512)S(6)} %and.47, f16[2048,512]{1,0:T(8,128)(2,1)} %copy-done.8, ...), kind=kLoop, calls=%fused_computation.43 | loop fusion | flops 11534336 | bytes 18874376 | tf_op jit(solution)/shard_map/convert_element_type | solution.py:366
  219.0 2.1 collective-permute-start.28
  221.1 24.5 %collective-permute-done.28 = f16[1024,512]{1,0:T(8,128)(2,1)S(1)} collective-permute-done((f16[1024,512]{1,0:T(8,128)(2,1)S(1)}, f16[1024,512]{1,0:T(8,128)(2,1)S(1)}, u32[]{:S(2)}, u32[]{:S(2)}) %collective-permute-start.28) | collective-permute-done | bytes 1048608 | tf_op jit(solution)/shard_map/ppermute | solution.py:29
  245.6 1.7 multiply_dynamic-update-slice_fusion.1
  248.6 5.8 %add_convert_fusion = (f16[1024,512]{1,0:T(8,128)(2,1)S(1)}, f32[1024,2048]{1,0:T(8,128)}) fusion(f32[1024,512]{1,0:T(8,128)S(1)} %copy-done.3, f16[2048,512]{1,0:T(8,128)(2,1)} %collective-permute-done.30, pred[]{:T(512)S(6)} %eq.21, f16[2048,512]{1,0:T(8,128)(2,1)} %collective-permute-done.21, f32[1024,2048]{1,0:T(8,128)} %multiply_dynamic-update-slice_fusion.1, ...), kind=kLoop, calls=%fused_computation.41 | loop fusion | flops 11010048 | bytes 17825800 | tf_op jit(solution)/shard_map/convert_element_type | solution.py:366
  254.5 1.9 collective-permute-start.31
  256.4 13.7 %collective-permute-done.31 = f16[1024,512]{1,0:T(8,128)(2,1)} collective-permute-done((f16[1024,512]{1,0:T(8,128)(2,1)S(1)}, f16[1024,512]{1,0:T(8,128)(2,1)}, u32[]{:S(2)}, u32[]{:S(2)}) %collective-permute-start.31) | collective-permute-done | bytes 1048608 | tf_op jit(solution)/shard_map/ppermute | solution.py:29
  270.1 3.0 %multiply_dynamic-update-slice_fusion = f32[1024,2048]{1,0:T(8,128)} fusion(f32[1024,2048]{1,0:T(8,128)} %get-tuple-element.46, s32[]{:T(128)S(6)} %select_n.153, f16[1024,512]{1,0:T(8,128)(2,1)S(1)} %collective-permute-done.28, f16[1024,512]{1,0:T(8,128)(2,1)} %collective-permute-done.31, f16[1024,512]{1,0:T(8,128)(2,1)S(1)} %collective-permute-done.27, ...), kind=kLoop, calls=%fused_computation.40 | loop fusion | flops 2097152 | bytes 5242886 | tf_op jit(solution)/shard_map/dynamic_update_slice | solution.py:429
  (78 shorter events, 17.7 us)
Async XLA Ops:
  0.0 23.5 %collective-permute-start.7 = (s32[1024,1024]{1,0:T(8,128)}, s32[1024,1024]{1,0:T(8,128)}, u32[]{:S(2)}, u32[]{:S(2)}) collective-permute-start(s32[1024,1024]{1,0:T(8,128)} %near_ref.3), channel_id=1, source_target_pairs={{0,8},{1,9},{2,10},{3,11},{4,12},{5,13},{6,14},{7,15},{8,0},{9,1},... | collective-permute-start | bytes 12582920 | tf_op jit(solution)/shard_map/ppermute | solution.py:29
  3.2 4.2 %collective-permute-start = (s32[2048]{0:T(1024)S(1)}, s32[2048]{0:T(1024)S(1)}, u32[]{:S(2)}, u32[]{:S(2)}) collective-permute-start(s32[2048]{0:T(1024)S(1)} %pad_add_fusion.3), channel_id=1, source_target_pairs={{0,8},{1,9},{2,10},{3,11},{4,12},{5,13},{6,14},{7,15},{8,0},{9,1},... | collective-permute-start | bytes 24584 | tf_op jit(solution)/shard_map/ppermute | solution.py:29
  3.3 3.1 %collective-permute-start.2 = (s32[1024]{0:T(1024)S(1)}, s32[1024]{0:T(1024)S(1)}, u32[]{:S(2)}, u32[]{:S(2)}) collective-permute-start(s32[1024]{0:T(1024)S(1)} %get-tuple-element.41), channel_id=1, source_target_pairs={{0,24},{1,25},{2,26},{3,27},{4,28},{5,29},{6,30},{7,31},{8,16},{9,... | collective-permute-start | bytes 12296 | tf_op jit(solution)/shard_map/ppermute | solution.py:29
  4.0 2.5 collective-permute-start.1
  7.5 2.6 collective-permute-start.3
  10.1 4.5 %collective-permute-start.6 = (s32[4096]{0:T(1024)S(1)}, s32[4096]{0:T(1024)S(1)}, u32[]{:S(2)}, u32[]{:S(2)}) collective-permute-start(s32[4096]{0:T(1024)S(1)} %pad_add_fusion.1), channel_id=1, source_target_pairs={{0,6},{1,7},{2,4},{3,5},{4,2},{5,3},{6,0},{7,1},{8,14},{9,15},{10,... | collective-permute-start | bytes 49160 | tf_op jit(solution)/shard_map/ppermute | solution.py:29
  13.5 3.5 %collective-permute-start.5 = (s32[4096]{0:T(1024)S(1)}, s32[4096]{0:T(1024)S(1)}, u32[]{:S(2)}, u32[]{:S(2)}) collective-permute-start(s32[4096]{0:T(1024)S(1)} %pad_add_fusion.1), channel_id=1, source_target_pairs={{0,4},{1,5},{2,6},{3,7},{4,0},{5,1},{6,2},{7,3},{8,12},{9,13},{10,... | collective-permute-start | bytes 49160 | tf_op jit(solution)/shard_map/ppermute | solution.py:29
  13.5 3.5 %collective-permute-start.4 = (s32[4096]{0:T(1024)S(1)}, s32[4096]{0:T(1024)S(1)}, u32[]{:S(2)}, u32[]{:S(2)}) collective-permute-start(s32[4096]{0:T(1024)S(1)} %pad_add_fusion.1), channel_id=1, source_target_pairs={{0,2},{1,3},{2,0},{3,1},{4,6},{5,7},{6,4},{7,5},{8,10},{9,11},{10,... | collective-permute-start | bytes 49160 | tf_op jit(solution)/shard_map/ppermute | solution.py:29
  27.8 51.6 %collective-permute-start.9 = (bf16[2048,512]{1,0:T(8,128)(2,1)S(1)}, bf16[2048,512]{1,0:T(8,128)(2,1)}, u32[]{:S(2)}, u32[]{:S(2)}) collective-permute-start(bf16[2048,512]{1,0:T(8,128)(2,1)S(1)} %shard_map.28.refs_0_.refs_2_.refs_4_), channel_id=1, source_target_pairs={{4,2},{5,3},{10,8},{11,9},{14,12},{15,13},{20,18},{21,19},{26,24},... | collective-permute-start | bytes 6291464 | tf_op jit(solution)/shard_map/ppermute | solution.py:29
  29.1 52.3 %collective-permute-start.11 = (bf16[2048,512]{1,0:T(8,128)(2,1)S(1)}, bf16[2048,512]{1,0:T(8,128)(2,1)}, u32[]{:S(2)}, u32[]{:S(2)}) collective-permute-start(bf16[2048,512]{1,0:T(8,128)(2,1)S(1)} %shard_map.28.refs_0_.refs_2_.refs_4_), channel_id=1, source_target_pairs={{0,2},{1,3},{4,6},{5,7},{10,12},{11,13},{16,18},{17,19},{20,22},{2... | collective-permute-start | bytes 6291464 | tf_op jit(solution)/shard_map/ppermute | solution.py:29
  35.4 10.0 %copy-start = (bf16[2048,512]{1,0:T(8,128)(2,1)}, bf16[2048,512]{1,0:T(8,128)(2,1)S(1)}, u32[]{:S(2)}) copy-start(bf16[2048,512]{1,0:T(8,128)(2,1)S(1)} %shard_map.29.refs_1_.refs_3_.refs_5_) | copy-start | bytes 6291460
  35.5 42.0 %collective-permute-start.14 = (bf16[2048,512]{1,0:T(8,128)(2,1)S(1)}, bf16[2048,512]{1,0:T(8,128)(2,1)S(1)}, u32[]{:S(2)}, u32[]{:S(2)}) collective-permute-start(bf16[2048,512]{1,0:T(8,128)(2,1)S(1)} %shard_map.29.refs_1_.refs_3_.refs_5_), channel_id=1, source_target_pairs={{4,2},{5,3},{14,12},{15,13},{20,18},{21,19},{26,24},{27,25},{30,28... | collective-permute-start | bytes 6291464 | tf_op jit(solution)/shard_map/ppermute | solution.py:29
  36.8 42.7 %collective-permute-start.15 = (bf16[2048,512]{1,0:T(8,128)(2,1)S(1)}, bf16[2048,512]{1,0:T(8,128)(2,1)S(1)}, u32[]{:S(2)}, u32[]{:S(2)}) collective-permute-start(bf16[2048,512]{1,0:T(8,128)(2,1)S(1)} %shard_map.29.refs_1_.refs_3_.refs_5_), channel_id=1, source_target_pairs={{0,2},{1,3},{4,6},{5,7},{10,12},{11,13},{16,18},{17,19},{26,28},{2... | collective-permute-start | bytes 6291464 | tf_op jit(solution)/shard_map/ppermute | solution.py:29
  37.6 45.9 %collective-permute-start.13 = (bf16[2048,512]{1,0:T(8,128)(2,1)S(1)}, bf16[2048,512]{1,0:T(8,128)(2,1)}, u32[]{:S(2)}, u32[]{:S(2)}) collective-permute-start(bf16[2048,512]{1,0:T(8,128)(2,1)S(1)} %shard_map.28.refs_0_.refs_2_.refs_4_), channel_id=1, source_target_pairs={{0,1},{1,0},{2,3},{3,2},{4,5},{5,4},{6,7},{7,6},{8,9},{9,8},{10,11... | collective-permute-start | bytes 6291464 | tf_op jit(solution)/shard_map/ppermute | solution.py:29
  77.4 6.0 %copy-start.9 = (bf16[2048,512]{1,0:T(8,128)(2,1)}, bf16[2048,512]{1,0:T(8,128)(2,1)S(1)}, u32[]{:S(2)}) copy-start(bf16[2048,512]{1,0:T(8,128)(2,1)S(1)} %collective-permute-done.14.refs_5_.refs_9_) | copy-start | bytes 6291460
  77.4 9.1 %collective-permute-start.8 = (f16[2048,512]{1,0:T(8,128)(2,1)}, f16[2048,512]{1,0:T(8,128)(2,1)}, u32[]{:S(2)}, u32[]{:S(2)}) collective-permute-start(f16[2048,512]{1,0:T(8,128)(2,1)} %multiply_convert_fusion.4), channel_id=1, source_target_pairs={{4,20},{5,21},{14,30},{15,31},{16,0},{17,1},{26,10},{27,11}} | collective-permute-start | bytes 6291464 | tf_op jit(solution)/shard_map/ppermute | solution.py:29
  79.4 4.0 %copy-start.10 = (bf16[2048,512]{1,0:T(8,128)(2,1)}, bf16[2048,512]{1,0:T(8,128)(2,1)S(1)}, u32[]{:S(2)}) copy-start(bf16[2048,512]{1,0:T(8,128)(2,1)S(1)} %collective-permute-done.15.refs_6_.refs_4_) | copy-start | bytes 6291460
  79.4 9.1 %collective-permute-start.10 = (bf16[2048,512]{1,0:T(8,128)(2,1)}, bf16[2048,512]{1,0:T(8,128)(2,1)}, u32[]{:S(2)}, u32[]{:S(2)}) collective-permute-start(bf16[2048,512]{1,0:T(8,128)(2,1)} %collective-permute-done.9.refs_6_.refs_9_), channel_id=1, source_target_pairs={{2,0},{3,1},{12,10},{13,11},{18,16},{19,17},{28,26},{29,27}} | collective-permute-start | bytes 6291464 | tf_op jit(solution)/shard_map/ppermute | solution.py:29
  81.4 7.1 %collective-permute-start.12 = (bf16[2048,512]{1,0:T(8,128)(2,1)}, bf16[2048,512]{1,0:T(8,128)(2,1)}, u32[]{:S(2)}, u32[]{:S(2)}) collective-permute-start(bf16[2048,512]{1,0:T(8,128)(2,1)} %collective-permute-done.11.refs_7_.refs_5_), channel_id=1, source_target_pairs={{2,4},{3,5},{12,14},{13,15},{18,20},{19,21},{28,30},{29,31}} | collective-permute-start | bytes 6291464 | tf_op jit(solution)/shard_map/ppermute | solution.py:29
  83.5 6.5 %collective-permute-start.16 = (bf16[2048,512]{1,0:T(8,128)(2,1)}, bf16[2048,512]{1,0:T(8,128)(2,1)}, u32[]{:S(2)}, u32[]{:S(2)}) collective-permute-start(bf16[2048,512]{1,0:T(8,128)(2,1)} %collective-permute-done.13.refs_2_), channel_id=1, source_target_pairs={{0,8},{1,9},{2,10},{3,11},{4,12},{5,13},{6,14},{7,15},{8,0},{9,1},... | collective-permute-start | bytes 6291464 | tf_op jit(solution)/shard_map/ppermute | solution.py:29
  85.8 36.1 %collective-permute-start.17 = (bf16[2048,512]{1,0:T(8,128)(2,1)}, bf16[2048,512]{1,0:T(8,128)(2,1)S(1)}, u32[]{:S(2)}, u32[]{:S(2)}) collective-permute-start(bf16[2048,512]{1,0:T(8,128)(2,1)} %copy-done.9), channel_id=1, source_target_pairs={{2,0},{3,1},{12,10},{13,11},{18,16},{19,17},{28,26},{29,27}} | collective-permute-start | bytes 6291464 | tf_op jit(solution)/shard_map/ppermute | solution.py:29
  86.6 37.9 %collective-permute-start.19 = (bf16[2048,512]{1,0:T(8,128)(2,1)}, bf16[2048,512]{1,0:T(8,128)(2,1)}, u32[]{:S(2)}, u32[]{:S(2)}) collective-permute-start(bf16[2048,512]{1,0:T(8,128)(2,1)} %copy-done.10), channel_id=1, source_target_pairs={{2,4},{3,5},{12,14},{13,15},{18,20},{19,21},{28,30},{29,31}} | collective-permute-start | bytes 6291464 | tf_op jit(solution)/shard_map/ppermute | solution.py:29
  89.9 1.6 copy-start.1
  103.9 67.6 %collective-permute-start.22 = (f16[2048,512]{1,0:T(8,128)(2,1)S(1)}, f16[2048,512]{1,0:T(8,128)(2,1)S(1)}, u32[]{:S(2)}, u32[]{:S(2)}) collective-permute-start(f16[2048,512]{1,0:T(8,128)(2,1)S(1)} %multiply_convert_fusion.3), channel_id=1, source_target_pairs={{2,18},{3,19},{4,20},{5,21},{6,22},{7,23},{12,28},{13,29},{14,30},... | collective-permute-start | bytes 6291464 | tf_op jit(solution)/shard_map/ppermute | solution.py:29
  106.0 47.2 %collective-permute-start.18 = (bf16[2048,512]{1,0:T(8,128)(2,1)}, bf16[2048,512]{1,0:T(8,128)(2,1)S(1)}, u32[]{:S(2)}, u32[]{:S(2)}) collective-permute-start(bf16[2048,512]{1,0:T(8,128)(2,1)} %collective-permute-done.10.refs_4_.refs_8_), channel_id=1, source_target_pairs={{10,8},{11,9},{26,24},{27,25}} | collective-permute-start | bytes 6291464 | tf_op jit(solution)/shard_map/ppermute | solution.py:29
  107.3 47.9 %collective-permute-start.20 = (bf16[2048,512]{1,0:T(8,128)(2,1)}, bf16[2048,512]{1,0:T(8,128)(2,1)S(1)}, u32[]{:S(2)}, u32[]{:S(2)}) collective-permute-start(bf16[2048,512]{1,0:T(8,128)(2,1)} %collective-permute-done.12.refs_7_.refs_6_), channel_id=1, source_target_pairs={{4,6},{5,7},{20,22},{21,23}} | collective-permute-start | bytes 6291464 | tf_op jit(solution)/shard_map/ppermute | solution.py:29
  121.9 33.3 %copy-start.11 = (bf16[2048,512]{1,0:T(8,128)(2,1)}, bf16[2048,512]{1,0:T(8,128)(2,1)S(1)}, u32[]{:S(2)}) copy-start(bf16[2048,512]{1,0:T(8,128)(2,1)S(1)} %collective-permute-done.17.refs_4_.refs_8_) | copy-start | bytes 6291460
  121.9 71.1 %collective-permute-start.21 = (f16[2048,512]{1,0:T(8,128)(2,1)}, f16[2048,512]{1,0:T(8,128)(2,1)}, u32[]{:S(2)}, u32[]{:S(2)}) collective-permute-start(f16[2048,512]{1,0:T(8,128)(2,1)} %multiply_convert_fusion.2), channel_id=1, source_target_pairs={{0,16},{1,17},{2,18},{3,19},{6,22},{7,23},{10,26},{11,27},{12,28},... | collective-permute-start | bytes 6291464 | tf_op jit(solution)/shard_map/ppermute | solution.py:29
  124.5 51.3 %collective-permute-start.23 = (bf16[2048,512]{1,0:T(8,128)(2,1)S(1)}, bf16[2048,512]{1,0:T(8,128)(2,1)}, u32[]{:S(2)}, u32[]{:S(2)}) collective-permute-start(bf16[2048,512]{1,0:T(8,128)(2,1)S(1)} %collective-permute-done.17.refs_4_.refs_8_), channel_id=1, source_target_pairs={{10,8},{11,9},{26,24},{27,25}} | collective-permute-start | bytes 6291464 | tf_op jit(solution)/shard_map/ppermute | solution.py:29
  153.2 2.0 copy-start.12
  153.3 22.5 %collective-permute-start.24 = (bf16[2048,512]{1,0:T(8,128)(2,1)}, bf16[2048,512]{1,0:T(8,128)(2,1)}, u32[]{:S(2)}, u32[]{:S(2)}) collective-permute-start(bf16[2048,512]{1,0:T(8,128)(2,1)} %collective-permute-done.19.refs_10_.refs_5_), channel_id=1, source_target_pairs={{4,6},{5,7},{20,22},{21,23}} | collective-permute-start | bytes 6291464 | tf_op jit(solution)/shard_map/ppermute | solution.py:29
  155.2 1.4 copy-start.13
  165.9 5.6 %copy-start.6 = (f32[2048,512]{1,0:T(8,128)S(1)}, f32[2048,512]{1,0:T(8,128)}, u32[]{:S(2)}) copy-start(f32[2048,512]{1,0:T(8,128)} %shard_map.31) | copy-start | bytes 12582916
  170.2 43.2 %collective-permute-start.25 = (f16[2048,512]{1,0:T(8,128)(2,1)}, f16[2048,512]{1,0:T(8,128)(2,1)}, u32[]{:S(2)}, u32[]{:S(2)}) collective-permute-start(f16[2048,512]{1,0:T(8,128)(2,1)} %multiply_convert_fusion.1), channel_id=1, source_target_pairs={{0,16},{1,17},{8,24},{9,25},{10,26},{11,27},{20,4},{21,5},{22,6},{... | collective-permute-start | bytes 6291464 | tf_op jit(solution)/shard_map/ppermute | solution.py:29
  171.5 21.5 %copy-start.8 = (f16[2048,512]{1,0:T(8,128)(2,1)}, f16[2048,512]{1,0:T(8,128)(2,1)S(1)}, u32[]{:S(2)}) copy-start(f16[2048,512]{1,0:T(8,128)(2,1)S(1)} %collective-permute-done.22) | copy-start | bytes 6291460
  175.8 23.4 %collective-permute-start.26 = (bf16[2048,512]{1,0:T(8,128)(2,1)S(1)}, bf16[2048,512]{1,0:T(8,128)(2,1)}, u32[]{:S(2)}, u32[]{:S(2)}) collective-permute-start(bf16[2048,512]{1,0:T(8,128)(2,1)S(1)} %copy-done.1), channel_id=1, source_target_pairs={{10,8},{11,9},{20,22},{21,23}} | collective-permute-start | bytes 6291464 | tf_op jit(solution)/shard_map/ppermute | solution.py:29
  187.4 5.6 %copy-start.7 = (f32[2048,512]{1,0:T(8,128)S(1)}, f32[2048,512]{1,0:T(8,128)}, u32[]{:S(2)}) copy-start(f32[2048,512]{1,0:T(8,128)} %shard_map.34) | copy-start | bytes 12582916
  191.7 55.7 %collective-permute-start.30 = (f16[2048,512]{1,0:T(8,128)(2,1)}, f16[2048,512]{1,0:T(8,128)(2,1)}, u32[]{:S(2)}, u32[]{:S(2)}) collective-permute-start(f16[2048,512]{1,0:T(8,128)(2,1)} %multiply_convert_fusion), channel_id=1, source_target_pairs={{8,24},{9,25},{22,6},{23,7}} | collective-permute-start | bytes 6291464 | tf_op jit(solution)/shard_map/ppermute | solution.py:29
  196.8 24.3 %collective-permute-start.27 = (f16[1024,512]{1,0:T(8,128)(2,1)}, f16[1024,512]{1,0:T(8,128)(2,1)S(1)}, u32[]{:S(2)}, u32[]{:S(2)}) collective-permute-start(f16[1024,512]{1,0:T(8,128)(2,1)} %fusion.16), channel_id=1, source_target_pairs={{0,1},{1,0},{2,3},{3,2},{4,5},{5,4},{10,11},{11,10},{12,13},{13,12... | collective-permute-start | bytes 3145736 | tf_op jit(solution)/shard_map/ppermute | solution.py:29
  197.5 23.6 %collective-permute-start.29 = (f16[1024,512]{1,0:T(8,128)(2,1)}, f16[1024,512]{1,0:T(8,128)(2,1)}, u32[]{:S(2)}, u32[]{:S(2)}) collective-permute-start(f16[1024,512]{1,0:T(8,128)(2,1)} %fusion.13), channel_id=1, source_target_pairs={{0,1},{1,0},{2,3},{3,2},{8,9},{9,8},{10,11},{11,10},{12,13},{13,12... | collective-permute-start | bytes 3145736 | tf_op jit(solution)/shard_map/ppermute | solution.py:29
  204.9 5.8 %copy-start.2 = (f32[1024,512]{1,0:T(8,128)}, f32[1024,512]{1,0:T(8,128)S(1)}, u32[]{:S(2)}) copy-start(f32[1024,512]{1,0:T(8,128)S(1)} %shard_map.35) | copy-start | bytes 6291460
  210.7 8.3 %copy-start.4 = (f32[1024,512]{1,0:T(8,128)}, f32[1024,512]{1,0:T(8,128)S(1)}, u32[]{:S(2)}) copy-start(f32[1024,512]{1,0:T(8,128)S(1)} %shard_map.36) | copy-start | bytes 6291460
  219.0 26.7 %collective-permute-start.28 = (f16[1024,512]{1,0:T(8,128)(2,1)S(1)}, f16[1024,512]{1,0:T(8,128)(2,1)S(1)}, u32[]{:S(2)}, u32[]{:S(2)}) collective-permute-start(f16[1024,512]{1,0:T(8,128)(2,1)S(1)} %get-tuple-element.43), channel_id=1, source_target_pairs={{4,5},{5,4},{6,7},{7,6},{14,15},{15,14},{16,17},{17,16},{24,25},{2... | collective-permute-start | bytes 3145736 | tf_op jit(solution)/shard_map/ppermute | solution.py:29
  245.6 2.1 copy-start.3
  245.6 3.0 %copy-start.5 = (f32[1024,512]{1,0:T(8,128)S(1)}, f32[1024,512]{1,0:T(8,128)}, u32[]{:S(2)}) copy-start(f32[1024,512]{1,0:T(8,128)} %copy-done.4) | copy-start | bytes 6291460
  254.5 15.6 %collective-permute-start.31 = (f16[1024,512]{1,0:T(8,128)(2,1)S(1)}, f16[1024,512]{1,0:T(8,128)(2,1)}, u32[]{:S(2)}, u32[]{:S(2)}) collective-permute-start(f16[1024,512]{1,0:T(8,128)(2,1)S(1)} %get-tuple-element.45), channel_id=1, source_target_pairs={{6,7},{7,6},{8,9},{9,8},{22,23},{23,22},{24,25},{25,24}} | collective-permute-start | bytes 3145736 | tf_op jit(solution)/shard_map/ppermute | solution.py:29

commit v4 on v3

--- a/solution.py
+++ b/solution.py
@@ -130,6 +130,7 @@
         @pl.when(i == 0)
         def _():
             fetch(0, 0)
+            fetch(1, 1)
 
         @pl.when((i == 0) | (right_at(i) != right_at(jnp.maximum(i - 1, 0))))
         def _():
@@ -145,7 +146,7 @@
             def _(to=to):
                 arrive(i, to)
 
-                @pl.when(i + 1 < blocks)
+                @pl.when((i > 0) & (i + 1 < blocks))
                 def _():
                     fetch(i + 1, 1 - to)
 

time: 274 us -> 275 us (level)
  the two profiles are of different devices: /device:TPU:7 before, /device:TPU:24 now
where the time goes in v4:
time: 275 us; the launch traced here: 274 us
  waiting for transfers between devices  102 us (37%)
  Pallas kernels  66 us (24%)
  other arithmetic  48.4 us (18%)
  starting transfers between devices  47.3 us (17%)
  local copies, waits for them, and re-layouts  9.38 us (3%)
    ppermute x32, waiting for transfers between devices, send(): return lax.ppermute(value, AXES, pairs_of(move))  102 us
    pallas_call x7, Pallas kernels, products_of(): pl.pallas_call(kernel, grid_spec=pltpu.PrefetchScalarGridSpec(num_scalar_...  57.4 us
    ppermute x32, starting transfers between devices, send(): return lax.ppermute(value, AXES, pairs_of(move))  47.3 us
    convert_element_type x4, other arithmetic, swap_some(): value = value.astype(jnp.float16)  20.3 us
    convert_element_type x5, other arithmetic, work(): narrow_products.append((product * scale).astype(jnp.float16))  19.4 us
    pallas_call x2, Pallas kernels, residuals_of(): pl.pallas_call(kernel, grid_spec=pltpu.PrefetchScalarGridSpec(num_scalar_...  8.61 us
  transfers between devices with their start and end apart: 32, of which 12 were waited for; matrix products, arithmetic and copies ran while one was open for 16% of the time, Pallas kernels for 23%

profile of v4, /device:TPU:24, one launch (start us, length us, event | category | flops | bytes accessed | tf_op | source)
XLA Modules:
  0.0 273.9 jit_solution(7136880509165542081)
XLA Ops:
  0.0 2.6 fusion.23
  6.2 1.7 collective-permute-done.1
  8.0 1.6 collective-permute-start.3
  9.5 2.2 collective-permute-done.3
  12.0 1.7 collective-permute-start.5
  13.7 2.5 collective-permute-start.4
  19.3 4.5 %broadcast_in_dim.3 = f32[1024,2048]{1,0:T(8,128)} broadcast(f32[]{:T(128)S(6)} %mul.89), dimensions={} | broadcast | bytes 8388612 | tf_op jit(solution)/shard_map/broadcast_in_dim | solution.py:322
  24.4 4.3 %shard_map.28.refs_0_.refs_2_.refs_4_ = bf16[2048,512]{1,0:T(8,128)(2,1)S(1)} custom-call(s32[1]{0:T(128)} %bitcast.5.part_ref, f32[1,2048]{1,0:T(1,128)S(1)} %bitcast.10, f32[1,1024]{1,0:T(1,128)S(1)} %bitcast.12, s32[1024,1024]{1,0:T(8,128)} %near_ref.3, s32[1024,1024]{1,0:T(8,128)} %collective-permute-done.7.far_ref), custom_call_target="tpu_custom_call" | custom-call | flops 10485760 | bytes 6291456 | tf_op jit(solution)/shard_map/pallas_call | solution.py:69
  28.7 2.0 collective-permute-start.9
  32.0 4.3 %shard_map.29.refs_1_.refs_3_.refs_5_ = bf16[2048,512]{1,0:T(8,128)(2,1)S(1)} custom-call(s32[1]{0:T(128)} %bitcast.8.part_ref, f32[1,2048]{1,0:T(1,128)S(1)} %bitcast.11, f32[1,1024]{1,0:T(1,128)S(1)} %bitcast.13, s32[1024,1024]{1,0:T(8,128)} %near_ref.3, s32[1024,1024]{1,0:T(8,128)} %collective-permute-done.7.far_ref), custom_call_target="tpu_custom_call" | custom-call | flops 10485760 | bytes 6291456 | tf_op jit(solution)/shard_map/pallas_call | solution.py:69
  38.5 1.6 collective-permute-start.13
  40.0 7.6 %shard_map.30 = f32[2048,512]{1,0:T(8,128)} custom-call(s32[48]{0:T(128)S(1)} %fusion.22.s, bf16[2048,512]{1,0:T(8,128)(2,1)S(1)} %shard_map.28.refs_0_.refs_2_.refs_4_, bf16[2048,512]{1,0:T(8,128)(2,1)S(1)} %shard_map.29.refs_1_.refs_3_.refs_5_, bf16[2048,512]{1,0:T(8,128)(2,1)S(1)} %shard_map.28.refs_0_.refs_2_.refs_4_, ...), custom_call_target="tpu_custom_call" | custom-call | flops 17179869184 | bytes 14680064 | tf_op jit(solution)/shard_map/pallas_call | solution.py:157
  47.7 4.1 %multiply_convert_fusion.4 = f16[2048,512]{1,0:T(8,128)(2,1)} fusion(f32[2048,512]{1,0:T(8,128)} %shard_map.30), kind=kLoop, calls=%fused_computation.4 | loop fusion | flops 2097152 | bytes 6291456 | tf_op jit(solution)/shard_map/convert_element_type | solution.py:331
  51.8 2.0 collective-permute-start.8
  53.7 27.4 %collective-permute-done.15.refs_6_.refs_4_ = bf16[2048,512]{1,0:T(8,128)(2,1)S(1)} collective-permute-done((bf16[2048,512]{1,0:T(8,128)(2,1)S(1)}, bf16[2048,512]{1,0:T(8,128)(2,1)S(1)}, u32[]{:S(2)}, u32[]{:S(2)}) %collective-permute-start.15) | collective-permute-done | bytes 2097184 | tf_op jit(solution)/shard_map/ppermute | solution.py:29
  81.1 2.0 collective-permute-start.10
  83.2 2.0 collective-permute-start.12
  87.4 2.0 collective-permute-start.19
  89.4 1.6 collective-permute-done.16.refs_3_
  91.0 1.6 copy-done.1
  92.6 9.6 %shard_map.31 = f32[2048,512]{1,0:T(8,128)} custom-call(s32[48]{0:T(128)S(1)} %fusion.22.s, bf16[2048,512]{1,0:T(8,128)(2,1)S(1)} %shard_map.28.refs_0_.refs_2_.refs_4_, bf16[2048,512]{1,0:T(8,128)(2,1)S(1)} %copy-done.1, bf16[2048,512]{1,0:T(8,128)(2,1)} %collective-permute-done.13.refs_2_, bf16[2048,512]{1,0:T(8,128)(2,1)} %collective-permute-done.16.refs_3_, ...), custom_call_target="tpu_custom_call" | custom-call | flops 17179869184 | bytes 14680064 | tf_op jit(solution)/shard_map/pallas_call | solution.py:157
  102.2 2.8 %multiply_convert_fusion.3 = f16[2048,512]{1,0:T(8,128)(2,1)S(1)} fusion(f32[2048,512]{1,0:T(8,128)} %shard_map.31), kind=kLoop, calls=%fused_computation.3 | loop fusion | flops 2097152 | bytes 6291456 | tf_op jit(solution)/shard_map/convert_element_type | solution.py:331
  105.0 2.3 collective-permute-start.22
  108.2 1.5 collective-permute-start.20
  109.6 9.6 %shard_map.32 = f32[2048,512]{1,0:T(8,128)} custom-call(s32[48]{0:T(128)S(1)} %fusion.22.s, bf16[2048,512]{1,0:T(8,128)(2,1)S(1)} %shard_map.28.refs_0_.refs_2_.refs_4_, bf16[2048,512]{1,0:T(8,128)(2,1)S(1)} %copy-done.1, bf16[2048,512]{1,0:T(8,128)(2,1)} %collective-permute-done.13.refs_2_, bf16[2048,512]{1,0:T(8,128)(2,1)} %collective-permute-done.16.refs_3_, ...), custom_call_target="tpu_custom_call" | custom-call | flops 17179869184 | bytes 14680064 | tf_op jit(solution)/shard_map/pallas_call | solution.py:157
  119.2 4.1 %multiply_convert_fusion.2 = f16[2048,512]{1,0:T(8,128)(2,1)} fusion(f32[2048,512]{1,0:T(8,128)} %shard_map.32), kind=kLoop, calls=%fused_computation.2 | loop fusion | flops 2097152 | bytes 6291456 | tf_op jit(solution)/shard_map/convert_element_type | solution.py:331
  123.3 2.6 collective-permute-start.21
  125.9 2.0 collective-permute-start.23
  129.2 24.4 %collective-permute-done.20.refs_11_.refs_6_ = bf16[2048,512]{1,0:T(8,128)(2,1)S(1)} collective-permute-done((bf16[2048,512]{1,0:T(8,128)(2,1)}, bf16[2048,512]{1,0:T(8,128)(2,1)S(1)}, u32[]{:S(2)}, u32[]{:S(2)}) %collective-permute-start.20) | collective-permute-done | bytes 2097184 | tf_op jit(solution)/shard_map/ppermute | solution.py:29
  155.0 9.3 %shard_map.33 = f32[2048,512]{1,0:T(8,128)} custom-call(s32[48]{0:T(128)S(1)} %fusion.22.s, bf16[2048,512]{1,0:T(8,128)(2,1)S(1)} %shard_map.28.refs_0_.refs_2_.refs_4_, bf16[2048,512]{1,0:T(8,128)(2,1)S(1)} %copy-done.1, bf16[2048,512]{1,0:T(8,128)(2,1)} %collective-permute-done.13.refs_2_, bf16[2048,512]{1,0:T(8,128)(2,1)} %collective-permute-done.16.refs_3_, ...), custom_call_target="tpu_custom_call" | custom-call | flops 17179869184 | bytes 14680064 | tf_op jit(solution)/shard_map/pallas_call | solution.py:157
  164.3 4.3 %multiply_convert_fusion.1 = f16[2048,512]{1,0:T(8,128)(2,1)} fusion(f32[2048,512]{1,0:T(8,128)} %shard_map.33), kind=kLoop, calls=%fused_computation.1 | loop fusion | flops 2097152 | bytes 6291456 | tf_op jit(solution)/shard_map/convert_element_type | solution.py:331
  169.9 4.3 %fusion.13 = f16[1024,512]{1,0:T(8,128)(2,1)} fusion(f32[2048,512]{1,0:T(8,128)} %shard_map.33, f32[2048,512]{1,0:T(8,128)S(1)} %copy-done.6, pred[]{:T(512)S(6)} %and.46, pred[]{:T(512)S(6)} %and.43, f16[2048,512]{1,0:T(8,128)(2,1)S(1)} %collective-permute-done.22), kind=kLoop, calls=%fused_computation.26 | loop fusion | flops 5767168 | bytes 9437186 | tf_op jit(solution)/shard_map/convert_element_type | solution.py:367
  174.2 2.0 collective-permute-done.24.refs_10_.refs_4_
  176.2 2.0 collective-permute-start.26
  178.2 9.6 %shard_map.34 = f32[2048,512]{1,0:T(8,128)} custom-call(s32[48]{0:T(128)S(1)} %fusion.22.s, bf16[2048,512]{1,0:T(8,128)(2,1)S(1)} %shard_map.28.refs_0_.refs_2_.refs_4_, bf16[2048,512]{1,0:T(8,128)(2,1)S(1)} %copy-done.1, bf16[2048,512]{1,0:T(8,128)(2,1)} %collective-permute-done.13.refs_2_, bf16[2048,512]{1,0:T(8,128)(2,1)} %collective-permute-done.16.refs_3_, ...), custom_call_target="tpu_custom_call" | custom-call | flops 17179869184 | bytes 14680064 | tf_op jit(solution)/shard_map/pallas_call | solution.py:157
  187.8 4.3 %multiply_convert_fusion = f16[2048,512]{1,0:T(8,128)(2,1)} fusion(f32[2048,512]{1,0:T(8,128)} %shard_map.34), kind=kLoop, calls=%fused_computation | loop fusion | flops 2097152 | bytes 6291456 | tf_op jit(solution)/shard_map/convert_element_type | solution.py:331
  193.4 3.8 %fusion.16 = f16[1024,512]{1,0:T(8,128)(2,1)} fusion(f32[2048,512]{1,0:T(8,128)} %shard_map.33, f32[2048,512]{1,0:T(8,128)S(1)} %copy-done.7, f32[2048,512]{1,0:T(8,128)S(1)} %copy-done.6, pred[]{:T(512)S(6)} %and.44, pred[]{:T(512)S(6)} %and.43, f16[2048,512]{1,0:T(8,128)(2,1)} %collective-permute-done.21, f16[2048,512]{1,0:T(8,128)(2,1)S(1)} %collective-permute-done.22), kind=kLoop, calls=%fused_computation.29 | loop fusion | flops 5767168 | bytes 9437186 | tf_op jit(solution)/shard_map/convert_element_type | solution.py:367
  197.9 1.7 collective-permute-start.29
  199.6 6.1 %shard_map.35 = f32[1024,512]{1,0:T(8,128)S(1)} custom-call(s32[48]{0:T(128)S(1)} %fusion.22.s, bf16[2048,512]{1,0:T(8,128)(2,1)S(1)} %shard_map.28.refs_0_.refs_2_.refs_4_, bf16[2048,512]{1,0:T(8,128)(2,1)} %copy-done, bf16[2048,512]{1,0:T(8,128)(2,1)} %collective-permute-done.13.refs_2_, bf16[2048,512]{1,0:T(8,128)(2,1)} %collective-permute-done.16.refs_3_, ...), custom_call_target="tpu_custom_call" | custom-call | flops 8589934592 | bytes 8388608 | tf_op jit(solution)/shard_map/pallas_call | solution.py:157
  205.7 5.6 %shard_map.36 = f32[1024,512]{1,0:T(8,128)S(1)} custom-call(s32[48]{0:T(128)S(1)} %fusion.22.s, bf16[2048,512]{1,0:T(8,128)(2,1)S(1)} %shard_map.28.refs_0_.refs_2_.refs_4_, bf16[2048,512]{1,0:T(8,128)(2,1)} %copy-done, bf16[2048,512]{1,0:T(8,128)(2,1)} %collective-permute-done.13.refs_2_, bf16[2048,512]{1,0:T(8,128)(2,1)} %collective-permute-done.16.refs_3_, ...), custom_call_target="tpu_custom_call" | custom-call | flops 8589934592 | bytes 8388608 | tf_op jit(solution)/shard_map/pallas_call | solution.py:157
  211.3 6.3 %add_convert_fusion.1 = (f16[1024,512]{1,0:T(8,128)(2,1)S(1)}, f32[1024,2048]{1,0:T(8,128)}) fusion(f32[2048,512]{1,0:T(8,128)S(1)} %copy-done.7, f16[2048,512]{1,0:T(8,128)(2,1)} %collective-permute-done.25, f32[1024,2048]{1,0:T(8,128)} %broadcast_in_dim.3, s32[]{:T(128)S(6)} %select_n.139, pred[]{:T(512)S(6)} %and.47, f16[2048,512]{1,0:T(8,128)(2,1)} %copy-done.8, ...), kind=kLoop, calls=%fused_computation.43 | loop fusion | flops 11534336 | bytes 18874376 | tf_op jit(solution)/shard_map/convert_element_type | solution.py:367
  217.6 3.4 %collective-permute-start.28 = (f16[1024,512]{1,0:T(8,128)(2,1)S(1)}, f16[1024,512]{1,0:T(8,128)(2,1)S(1)}, u32[]{:S(2)}, u32[]{:S(2)}) collective-permute-start(f16[1024,512]{1,0:T(8,128)(2,1)S(1)} %get-tuple-element.43), channel_id=1, source_target_pairs={{4,5},{5,4},{6,7},{7,6},{14,15},{15,14},{16,17},{17,16},{24,25},{2... | collective-permute-start | bytes 3145736 | tf_op jit(solution)/shard_map/ppermute | solution.py:29
  221.1 24.2 %collective-permute-done.28 = f16[1024,512]{1,0:T(8,128)(2,1)S(1)} collective-permute-done((f16[1024,512]{1,0:T(8,128)(2,1)S(1)}, f16[1024,512]{1,0:T(8,128)(2,1)S(1)}, u32[]{:S(2)}, u32[]{:S(2)}) %collective-permute-start.28) | collective-permute-done | bytes 1048608 | tf_op jit(solution)/shard_map/ppermute | solution.py:29
  245.3 1.7 multiply_dynamic-update-slice_fusion.1
  248.3 5.8 %add_convert_fusion = (f16[1024,512]{1,0:T(8,128)(2,1)S(1)}, f32[1024,2048]{1,0:T(8,128)}) fusion(f32[1024,512]{1,0:T(8,128)S(1)} %copy-done.3, f16[2048,512]{1,0:T(8,128)(2,1)} %collective-permute-done.30, pred[]{:T(512)S(6)} %eq.21, f16[2048,512]{1,0:T(8,128)(2,1)} %collective-permute-done.21, f32[1024,2048]{1,0:T(8,128)} %multiply_dynamic-update-slice_fusion.1, ...), kind=kLoop, calls=%fused_computation.41 | loop fusion | flops 11010048 | bytes 17825800 | tf_op jit(solution)/shard_map/convert_element_type | solution.py:367
  254.1 2.4 collective-permute-start.31
  256.6 14.4 %collective-permute-done.31 = f16[1024,512]{1,0:T(8,128)(2,1)} collective-permute-done((f16[1024,512]{1,0:T(8,128)(2,1)S(1)}, f16[1024,512]{1,0:T(8,128)(2,1)}, u32[]{:S(2)}, u32[]{:S(2)}) %collective-permute-start.31) | collective-permute-done | bytes 1048608 | tf_op jit(solution)/shard_map/ppermute | solution.py:29
  270.9 3.0 %multiply_dynamic-update-slice_fusion = f32[1024,2048]{1,0:T(8,128)} fusion(f32[1024,2048]{1,0:T(8,128)} %get-tuple-element.46, s32[]{:T(128)S(6)} %select_n.153, f16[1024,512]{1,0:T(8,128)(2,1)S(1)} %collective-permute-done.28, f16[1024,512]{1,0:T(8,128)(2,1)} %collective-permute-done.31, f16[1024,512]{1,0:T(8,128)(2,1)S(1)} %collective-permute-done.27, ...), kind=kLoop, calls=%fused_computation.40 | loop fusion | flops 2097152 | bytes 5242886 | tf_op jit(solution)/shard_map/dynamic_update_slice | solution.py:430
  (78 shorter events, 20.6 us)
Async XLA Ops:
  0.0 24.4 %collective-permute-start.7 = (s32[1024,1024]{1,0:T(8,128)}, s32[1024,1024]{1,0:T(8,128)}, u32[]{:S(2)}, u32[]{:S(2)}) collective-permute-start(s32[1024,1024]{1,0:T(8,128)} %near_ref.3), channel_id=1, source_target_pairs={{0,8},{1,9},{2,10},{3,11},{4,12},{5,13},{6,14},{7,15},{8,0},{9,1},... | collective-permute-start | bytes 12582920 | tf_op jit(solution)/shard_map/ppermute | solution.py:29
  2.6 5.4 %collective-permute-start = (s32[2048]{0:T(1024)S(1)}, s32[2048]{0:T(1024)S(1)}, u32[]{:S(2)}, u32[]{:S(2)}) collective-permute-start(s32[2048]{0:T(1024)S(1)} %pad_add_fusion.3), channel_id=1, source_target_pairs={{0,8},{1,9},{2,10},{3,11},{4,12},{5,13},{6,14},{7,15},{8,0},{9,1},... | collective-permute-start | bytes 24584 | tf_op jit(solution)/shard_map/ppermute | solution.py:29
  3.1 3.0 %collective-permute-start.2 = (s32[1024]{0:T(1024)S(1)}, s32[1024]{0:T(1024)S(1)}, u32[]{:S(2)}, u32[]{:S(2)}) collective-permute-start(s32[1024]{0:T(1024)S(1)} %get-tuple-element.41), channel_id=1, source_target_pairs={{0,24},{1,25},{2,26},{3,27},{4,28},{5,29},{6,30},{7,31},{8,16},{9,... | collective-permute-start | bytes 12296 | tf_op jit(solution)/shard_map/ppermute | solution.py:29
  4.3 3.6 %collective-permute-start.1 = (s32[1024]{0:T(1024)S(1)}, s32[1024]{0:T(1024)S(1)}, u32[]{:S(2)}, u32[]{:S(2)}) collective-permute-start(s32[1024]{0:T(1024)S(1)} %get-tuple-element.41), channel_id=1, source_target_pairs={{0,16},{1,17},{2,18},{3,19},{4,20},{5,21},{6,22},{7,23},{8,24},{9,... | collective-permute-start | bytes 12296 | tf_op jit(solution)/shard_map/ppermute | solution.py:29
  8.0 3.8 %collective-permute-start.3 = (s32[3072]{0:T(1024)S(1)}, s32[3072]{0:T(1024)S(1)}, u32[]{:S(2)}, u32[]{:S(2)}) collective-permute-start(s32[3072]{0:T(1024)S(1)} %pad_add_fusion.2), channel_id=1, source_target_pairs={{0,1},{1,0},{2,3},{3,2},{4,5},{5,4},{6,7},{7,6},{8,9},{9,8},{10,11... | collective-permute-start | bytes 36872 | tf_op jit(solution)/shard_map/ppermute | solution.py:29
  11.7 5.6 %collective-permute-start.6 = (s32[4096]{0:T(1024)S(1)}, s32[4096]{0:T(1024)S(1)}, u32[]{:S(2)}, u32[]{:S(2)}) collective-permute-start(s32[4096]{0:T(1024)S(1)} %pad_add_fusion.1), channel_id=1, source_target_pairs={{0,6},{1,7},{2,4},{3,5},{4,2},{5,3},{6,0},{7,1},{8,14},{9,15},{10,... | collective-permute-start | bytes 49160 | tf_op jit(solution)/shard_map/ppermute | solution.py:29
  12.0 5.3 %collective-permute-start.5 = (s32[4096]{0:T(1024)S(1)}, s32[4096]{0:T(1024)S(1)}, u32[]{:S(2)}, u32[]{:S(2)}) collective-permute-start(s32[4096]{0:T(1024)S(1)} %pad_add_fusion.1), channel_id=1, source_target_pairs={{0,4},{1,5},{2,6},{3,7},{4,0},{5,1},{6,2},{7,3},{8,12},{9,13},{10,... | collective-permute-start | bytes 49160 | tf_op jit(solution)/shard_map/ppermute | solution.py:29
  13.7 4.2 %collective-permute-start.4 = (s32[4096]{0:T(1024)S(1)}, s32[4096]{0:T(1024)S(1)}, u32[]{:S(2)}, u32[]{:S(2)}) collective-permute-start(s32[4096]{0:T(1024)S(1)} %pad_add_fusion.1), channel_id=1, source_target_pairs={{0,2},{1,3},{2,0},{3,1},{4,6},{5,7},{6,4},{7,5},{8,10},{9,11},{10,... | collective-permute-start | bytes 49160 | tf_op jit(solution)/shard_map/ppermute | solution.py:29
  28.7 52.4 %collective-permute-start.9 = (bf16[2048,512]{1,0:T(8,128)(2,1)S(1)}, bf16[2048,512]{1,0:T(8,128)(2,1)}, u32[]{:S(2)}, u32[]{:S(2)}) collective-permute-start(bf16[2048,512]{1,0:T(8,128)(2,1)S(1)} %shard_map.28.refs_0_.refs_2_.refs_4_), channel_id=1, source_target_pairs={{4,2},{5,3},{10,8},{11,9},{14,12},{15,13},{20,18},{21,19},{26,24},... | collective-permute-start | bytes 6291464 | tf_op jit(solution)/shard_map/ppermute | solution.py:29
  30.7 52.4 %collective-permute-start.11 = (bf16[2048,512]{1,0:T(8,128)(2,1)S(1)}, bf16[2048,512]{1,0:T(8,128)(2,1)}, u32[]{:S(2)}, u32[]{:S(2)}) collective-permute-start(bf16[2048,512]{1,0:T(8,128)(2,1)S(1)} %shard_map.28.refs_0_.refs_2_.refs_4_), channel_id=1, source_target_pairs={{0,2},{1,3},{4,6},{5,7},{10,12},{11,13},{16,18},{17,19},{20,22},{2... | collective-permute-start | bytes 6291464 | tf_op jit(solution)/shard_map/ppermute | solution.py:29
  36.3 11.3 %copy-start = (bf16[2048,512]{1,0:T(8,128)(2,1)}, bf16[2048,512]{1,0:T(8,128)(2,1)S(1)}, u32[]{:S(2)}) copy-start(bf16[2048,512]{1,0:T(8,128)(2,1)S(1)} %shard_map.29.refs_1_.refs_3_.refs_5_) | copy-start | bytes 6291460
  36.4 15.4 %collective-permute-start.14 = (bf16[2048,512]{1,0:T(8,128)(2,1)S(1)}, bf16[2048,512]{1,0:T(8,128)(2,1)S(1)}, u32[]{:S(2)}, u32[]{:S(2)}) collective-permute-start(bf16[2048,512]{1,0:T(8,128)(2,1)S(1)} %shard_map.29.refs_1_.refs_3_.refs_5_), channel_id=1, source_target_pairs={{4,2},{5,3},{14,12},{15,13},{20,18},{21,19},{26,24},{27,25},{30,28... | collective-permute-start | bytes 6291464 | tf_op jit(solution)/shard_map/ppermute | solution.py:29
  37.2 44.0 %collective-permute-start.15 = (bf16[2048,512]{1,0:T(8,128)(2,1)S(1)}, bf16[2048,512]{1,0:T(8,128)(2,1)S(1)}, u32[]{:S(2)}, u32[]{:S(2)}) collective-permute-start(bf16[2048,512]{1,0:T(8,128)(2,1)S(1)} %shard_map.29.refs_1_.refs_3_.refs_5_), channel_id=1, source_target_pairs={{0,2},{1,3},{4,6},{5,7},{10,12},{11,13},{16,18},{17,19},{26,28},{2... | collective-permute-start | bytes 6291464 | tf_op jit(solution)/shard_map/ppermute | solution.py:29
  38.5 48.0 %collective-permute-start.13 = (bf16[2048,512]{1,0:T(8,128)(2,1)S(1)}, bf16[2048,512]{1,0:T(8,128)(2,1)}, u32[]{:S(2)}, u32[]{:S(2)}) collective-permute-start(bf16[2048,512]{1,0:T(8,128)(2,1)S(1)} %shard_map.28.refs_0_.refs_2_.refs_4_), channel_id=1, source_target_pairs={{0,1},{1,0},{2,3},{3,2},{4,5},{5,4},{6,7},{7,6},{8,9},{9,8},{10,11... | collective-permute-start | bytes 6291464 | tf_op jit(solution)/shard_map/ppermute | solution.py:29
  51.8 34.8 %copy-start.9 = (bf16[2048,512]{1,0:T(8,128)(2,1)}, bf16[2048,512]{1,0:T(8,128)(2,1)S(1)}, u32[]{:S(2)}) copy-start(bf16[2048,512]{1,0:T(8,128)(2,1)S(1)} %collective-permute-done.14.refs_5_.refs_9_) | copy-start | bytes 6291460
  51.8 35.6 %collective-permute-start.8 = (f16[2048,512]{1,0:T(8,128)(2,1)}, f16[2048,512]{1,0:T(8,128)(2,1)}, u32[]{:S(2)}, u32[]{:S(2)}) collective-permute-start(f16[2048,512]{1,0:T(8,128)(2,1)} %multiply_convert_fusion.4), channel_id=1, source_target_pairs={{4,20},{5,21},{14,30},{15,31},{16,0},{17,1},{26,10},{27,11}} | collective-permute-start | bytes 6291464 | tf_op jit(solution)/shard_map/ppermute | solution.py:29
  81.1 5.4 %copy-start.10 = (bf16[2048,512]{1,0:T(8,128)(2,1)}, bf16[2048,512]{1,0:T(8,128)(2,1)S(1)}, u32[]{:S(2)}) copy-start(bf16[2048,512]{1,0:T(8,128)(2,1)S(1)} %collective-permute-done.15.refs_6_.refs_4_) | copy-start | bytes 6291460
  81.1 8.2 %collective-permute-start.10 = (bf16[2048,512]{1,0:T(8,128)(2,1)}, bf16[2048,512]{1,0:T(8,128)(2,1)}, u32[]{:S(2)}, u32[]{:S(2)}) collective-permute-start(bf16[2048,512]{1,0:T(8,128)(2,1)} %collective-permute-done.9.refs_6_.refs_9_), channel_id=1, source_target_pairs={{2,0},{3,1},{12,10},{13,11},{18,16},{19,17},{28,26},{29,27}} | collective-permute-start | bytes 6291464 | tf_op jit(solution)/shard_map/ppermute | solution.py:29
  83.2 6.2 %collective-permute-start.12 = (bf16[2048,512]{1,0:T(8,128)(2,1)}, bf16[2048,512]{1,0:T(8,128)(2,1)}, u32[]{:S(2)}, u32[]{:S(2)}) collective-permute-start(bf16[2048,512]{1,0:T(8,128)(2,1)} %collective-permute-done.11.refs_7_.refs_5_), channel_id=1, source_target_pairs={{2,4},{3,5},{12,14},{13,15},{18,20},{19,21},{28,30},{29,31}} | collective-permute-start | bytes 6291464 | tf_op jit(solution)/shard_map/ppermute | solution.py:29
  86.5 4.5 %collective-permute-start.16 = (bf16[2048,512]{1,0:T(8,128)(2,1)}, bf16[2048,512]{1,0:T(8,128)(2,1)}, u32[]{:S(2)}, u32[]{:S(2)}) collective-permute-start(bf16[2048,512]{1,0:T(8,128)(2,1)} %collective-permute-done.13.refs_2_), channel_id=1, source_target_pairs={{0,8},{1,9},{2,10},{3,11},{4,12},{5,13},{6,14},{7,15},{8,0},{9,1},... | collective-permute-start | bytes 6291464 | tf_op jit(solution)/shard_map/ppermute | solution.py:29
  86.6 36.7 %collective-permute-start.17 = (bf16[2048,512]{1,0:T(8,128)(2,1)}, bf16[2048,512]{1,0:T(8,128)(2,1)S(1)}, u32[]{:S(2)}, u32[]{:S(2)}) collective-permute-start(bf16[2048,512]{1,0:T(8,128)(2,1)} %copy-done.9), channel_id=1, source_target_pairs={{2,0},{3,1},{12,10},{13,11},{18,16},{19,17},{28,26},{29,27}} | collective-permute-start | bytes 6291464 | tf_op jit(solution)/shard_map/ppermute | solution.py:29
  87.4 38.5 %collective-permute-start.19 = (bf16[2048,512]{1,0:T(8,128)(2,1)}, bf16[2048,512]{1,0:T(8,128)(2,1)}, u32[]{:S(2)}, u32[]{:S(2)}) collective-permute-start(bf16[2048,512]{1,0:T(8,128)(2,1)} %copy-done.10), channel_id=1, source_target_pairs={{2,4},{3,5},{12,14},{13,15},{18,20},{19,21},{28,30},{29,31}} | collective-permute-start | bytes 6291464 | tf_op jit(solution)/shard_map/ppermute | solution.py:29
  91.0 1.6 copy-start.1
  105.0 64.8 %collective-permute-start.22 = (f16[2048,512]{1,0:T(8,128)(2,1)S(1)}, f16[2048,512]{1,0:T(8,128)(2,1)S(1)}, u32[]{:S(2)}, u32[]{:S(2)}) collective-permute-start(f16[2048,512]{1,0:T(8,128)(2,1)S(1)} %multiply_convert_fusion.3), channel_id=1, source_target_pairs={{2,18},{3,19},{4,20},{5,21},{6,22},{7,23},{12,28},{13,29},{14,30},... | collective-permute-start | bytes 6291464 | tf_op jit(solution)/shard_map/ppermute | solution.py:29
  107.4 20.5 %collective-permute-start.18 = (bf16[2048,512]{1,0:T(8,128)(2,1)}, bf16[2048,512]{1,0:T(8,128)(2,1)S(1)}, u32[]{:S(2)}, u32[]{:S(2)}) collective-permute-start(bf16[2048,512]{1,0:T(8,128)(2,1)} %collective-permute-done.10.refs_4_.refs_8_), channel_id=1, source_target_pairs={{10,8},{11,9},{26,24},{27,25}} | collective-permute-start | bytes 6291464 | tf_op jit(solution)/shard_map/ppermute | solution.py:29
  108.2 45.4 %collective-permute-start.20 = (bf16[2048,512]{1,0:T(8,128)(2,1)}, bf16[2048,512]{1,0:T(8,128)(2,1)S(1)}, u32[]{:S(2)}, u32[]{:S(2)}) collective-permute-start(bf16[2048,512]{1,0:T(8,128)(2,1)} %collective-permute-done.12.refs_7_.refs_6_), channel_id=1, source_target_pairs={{4,6},{5,7},{20,22},{21,23}} | collective-permute-start | bytes 6291464 | tf_op jit(solution)/shard_map/ppermute | solution.py:29
  123.3 30.3 %copy-start.11 = (bf16[2048,512]{1,0:T(8,128)(2,1)}, bf16[2048,512]{1,0:T(8,128)(2,1)S(1)}, u32[]{:S(2)}) copy-start(bf16[2048,512]{1,0:T(8,128)(2,1)S(1)} %collective-permute-done.17.refs_4_.refs_8_) | copy-start | bytes 6291460
  123.3 70.0 %collective-permute-start.21 = (f16[2048,512]{1,0:T(8,128)(2,1)}, f16[2048,512]{1,0:T(8,128)(2,1)}, u32[]{:S(2)}, u32[]{:S(2)}) collective-permute-start(f16[2048,512]{1,0:T(8,128)(2,1)} %multiply_convert_fusion.2), channel_id=1, source_target_pairs={{0,16},{1,17},{2,18},{3,19},{6,22},{7,23},{10,26},{11,27},{12,28},... | collective-permute-start | bytes 6291464 | tf_op jit(solution)/shard_map/ppermute | solution.py:29
  125.9 48.3 %collective-permute-start.23 = (bf16[2048,512]{1,0:T(8,128)(2,1)S(1)}, bf16[2048,512]{1,0:T(8,128)(2,1)}, u32[]{:S(2)}, u32[]{:S(2)}) collective-permute-start(bf16[2048,512]{1,0:T(8,128)(2,1)S(1)} %collective-permute-done.17.refs_4_.refs_8_), channel_id=1, source_target_pairs={{10,8},{11,9},{26,24},{27,25}} | collective-permute-start | bytes 6291464 | tf_op jit(solution)/shard_map/ppermute | solution.py:29
  127.9 25.7 %copy-start.12 = (bf16[2048,512]{1,0:T(8,128)(2,1)}, bf16[2048,512]{1,0:T(8,128)(2,1)S(1)}, u32[]{:S(2)}) copy-start(bf16[2048,512]{1,0:T(8,128)(2,1)S(1)} %collective-permute-done.18.refs_7_.refs_11_) | copy-start | bytes 6291460
  127.9 48.3 %collective-permute-start.24 = (bf16[2048,512]{1,0:T(8,128)(2,1)}, bf16[2048,512]{1,0:T(8,128)(2,1)}, u32[]{:S(2)}, u32[]{:S(2)}) collective-permute-start(bf16[2048,512]{1,0:T(8,128)(2,1)} %collective-permute-done.19.refs_10_.refs_5_), channel_id=1, source_target_pairs={{4,6},{5,7},{20,22},{21,23}} | collective-permute-start | bytes 6291464 | tf_op jit(solution)/shard_map/ppermute | solution.py:29
  153.6 1.4 copy-start.13
  164.3 5.6 %copy-start.6 = (f32[2048,512]{1,0:T(8,128)S(1)}, f32[2048,512]{1,0:T(8,128)}, u32[]{:S(2)}) copy-start(f32[2048,512]{1,0:T(8,128)} %shard_map.31) | copy-start | bytes 12582916
  168.5 42.8 %collective-permute-start.25 = (f16[2048,512]{1,0:T(8,128)(2,1)}, f16[2048,512]{1,0:T(8,128)(2,1)}, u32[]{:S(2)}, u32[]{:S(2)}) collective-permute-start(f16[2048,512]{1,0:T(8,128)(2,1)} %multiply_convert_fusion.1), channel_id=1, source_target_pairs={{0,16},{1,17},{8,24},{9,25},{10,26},{11,27},{20,4},{21,5},{22,6},{... | collective-permute-start | bytes 6291464 | tf_op jit(solution)/shard_map/ppermute | solution.py:29
  169.9 23.5 %copy-start.8 = (f16[2048,512]{1,0:T(8,128)(2,1)}, f16[2048,512]{1,0:T(8,128)(2,1)S(1)}, u32[]{:S(2)}) copy-start(f16[2048,512]{1,0:T(8,128)(2,1)S(1)} %collective-permute-done.22) | copy-start | bytes 6291460
  176.2 23.4 %collective-permute-start.26 = (bf16[2048,512]{1,0:T(8,128)(2,1)S(1)}, bf16[2048,512]{1,0:T(8,128)(2,1)}, u32[]{:S(2)}, u32[]{:S(2)}) collective-permute-start(bf16[2048,512]{1,0:T(8,128)(2,1)S(1)} %copy-done.1), channel_id=1, source_target_pairs={{10,8},{11,9},{20,22},{21,23}} | collective-permute-start | bytes 6291464 | tf_op jit(solution)/shard_map/ppermute | solution.py:29
  187.8 5.6 %copy-start.7 = (f32[2048,512]{1,0:T(8,128)S(1)}, f32[2048,512]{1,0:T(8,128)}, u32[]{:S(2)}) copy-start(f32[2048,512]{1,0:T(8,128)} %shard_map.34) | copy-start | bytes 12582916
  192.0 55.0 %collective-permute-start.30 = (f16[2048,512]{1,0:T(8,128)(2,1)}, f16[2048,512]{1,0:T(8,128)(2,1)}, u32[]{:S(2)}, u32[]{:S(2)}) collective-permute-start(f16[2048,512]{1,0:T(8,128)(2,1)} %multiply_convert_fusion), channel_id=1, source_target_pairs={{8,24},{9,25},{22,6},{23,7}} | collective-permute-start | bytes 6291464 | tf_op jit(solution)/shard_map/ppermute | solution.py:29
  197.2 23.9 %collective-permute-start.27 = (f16[1024,512]{1,0:T(8,128)(2,1)}, f16[1024,512]{1,0:T(8,128)(2,1)S(1)}, u32[]{:S(2)}, u32[]{:S(2)}) collective-permute-start(f16[1024,512]{1,0:T(8,128)(2,1)} %fusion.16), channel_id=1, source_target_pairs={{0,1},{1,0},{2,3},{3,2},{4,5},{5,4},{10,11},{11,10},{12,13},{13,12... | collective-permute-start | bytes 3145736 | tf_op jit(solution)/shard_map/ppermute | solution.py:29
  197.9 23.2 %collective-permute-start.29 = (f16[1024,512]{1,0:T(8,128)(2,1)}, f16[1024,512]{1,0:T(8,128)(2,1)}, u32[]{:S(2)}, u32[]{:S(2)}) collective-permute-start(f16[1024,512]{1,0:T(8,128)(2,1)} %fusion.13), channel_id=1, source_target_pairs={{0,1},{1,0},{2,3},{3,2},{8,9},{9,8},{10,11},{11,10},{12,13},{13,12... | collective-permute-start | bytes 3145736 | tf_op jit(solution)/shard_map/ppermute | solution.py:29
  205.7 5.6 %copy-start.2 = (f32[1024,512]{1,0:T(8,128)}, f32[1024,512]{1,0:T(8,128)S(1)}, u32[]{:S(2)}) copy-start(f32[1024,512]{1,0:T(8,128)S(1)} %shard_map.35) | copy-start | bytes 6291460
  211.3 6.3 %copy-start.4 = (f32[1024,512]{1,0:T(8,128)}, f32[1024,512]{1,0:T(8,128)S(1)}, u32[]{:S(2)}) copy-start(f32[1024,512]{1,0:T(8,128)S(1)} %shard_map.36) | copy-start | bytes 6291460
  217.6 27.7 %collective-permute-start.28 = (f16[1024,512]{1,0:T(8,128)(2,1)S(1)}, f16[1024,512]{1,0:T(8,128)(2,1)S(1)}, u32[]{:S(2)}, u32[]{:S(2)}) collective-permute-start(f16[1024,512]{1,0:T(8,128)(2,1)S(1)} %get-tuple-element.43), channel_id=1, source_target_pairs={{4,5},{5,4},{6,7},{7,6},{14,15},{15,14},{16,17},{17,16},{24,25},{2... | collective-permute-start | bytes 3145736 | tf_op jit(solution)/shard_map/ppermute | solution.py:29
  245.3 2.1 copy-start.3
  245.3 3.0 %copy-start.5 = (f32[1024,512]{1,0:T(8,128)S(1)}, f32[1024,512]{1,0:T(8,128)}, u32[]{:S(2)}) copy-start(f32[1024,512]{1,0:T(8,128)} %copy-done.4) | copy-start | bytes 6291460
  254.1 16.8 %collective-permute-start.31 = (f16[1024,512]{1,0:T(8,128)(2,1)S(1)}, f16[1024,512]{1,0:T(8,128)(2,1)}, u32[]{:S(2)}, u32[]{:S(2)}) collective-permute-start(f16[1024,512]{1,0:T(8,128)(2,1)S(1)} %get-tuple-element.45), channel_id=1, source_target_pairs={{6,7},{7,6},{8,9},{9,8},{22,23},{23,22},{24,25},{25,24}} | collective-permute-start | bytes 3145736 | tf_op jit(solution)/shard_map/ppermute | solution.py:29
